TPU v7x, 32 devices: a whole 2x2x4 slice. The times are simulated.
32 devices in a mesh: shard: 4 (over z), context: 2 (over x), tensor: 4 (over y, core).
Axes of the slice: x: 2, y: 2, z: 4, core: 2. Of those that a mesh axis runs over, the one named last changes fastest.
Arguments:
- prompt_tokens: bfloat16 [8, 2048, 1280], P('shard', 'context'), may hold values from -18 to 18, as said below
- later_tokens: bfloat16 [8, 8, 256, 1280], P('shard', 'context'), may hold values from -18 to 18, as said below
- prompt_upstream: bfloat16 [8, 2048, 1280], P('shard', 'context'), may hold values from -6 to 6
- later_upstream: bfloat16 [8, 8, 256, 1280], P('shard', 'context'), may hold values from -6 to 6
- prompt_lengths: int32 [8], P('shard'), may hold values from 1536 to 2048
- later_lengths: int32 [8, 8], P('shard', 'context'), may hold values from 64 to 256
- query_weight: bfloat16 [1280, 1280], P(('shard', 'context'), 'tensor'), may hold values from -0.15625 to 0.15625
- key_weight: bfloat16 [1280, 1280], P(('shard', 'context'), 'tensor'), may hold values from -0.15625 to 0.15625
- value_weight: bfloat16 [1280, 1280], P(('shard', 'context'), 'tensor'), may hold values from -0.15625 to 0.15625
- out_weight: bfloat16 [1280, 1280], P('tensor', ('shard', 'context')), may hold values from -2 to 2
- up_weight: bfloat16 [1280, 1280], P(('shard', 'context'), 'tensor'), may hold values from -1 to 1
- down_weight: bfloat16 [1280, 1280], P('tensor', ('shard', 'context')), may hold values from -0.15625 to 0.15625
- pre_gain: bfloat16 [1280], P(('shard', 'context')), may hold values from 0.099609375 to 1.8984375
- pre_shift: bfloat16 [1280], P(('shard', 'context')), may hold values from -4 to 4
- mid_gain: bfloat16 [1280], P(('shard', 'context')), may hold values from 0.099609375 to 1.8984375
- mid_shift: bfloat16 [1280], P(('shard', 'context')), may hold values from -4 to 4
- query_bias: bfloat16 [1280], P('tensor'), may hold values from -4 to 4
- value_bias: bfloat16 [1280], P('tensor'), may hold values from -0.75 to 0.75
- out_bias: bfloat16 [1280], P(('shard', 'context')), may hold values from -4 to 4
- up_bias: bfloat16 [1280], P('tensor'), may hold values from -4 to 4
- down_bias: bfloat16 [1280], P(('shard', 'context')), may hold values from -4 to 4
Outputs:
- prompt_output: bfloat16 [8, 2048, 1280], P('shard', 'context')
- later_output: bfloat16 [8, 8, 256, 1280], P('shard', 'context')
- prompt_grad: float32 [8, 2048, 1280], P('shard', 'context')
- later_grad: float32 [8, 8, 256, 1280], P('shard', 'context')
- query_weight_grad: float32 [1280, 1280], P(('shard', 'context'), 'tensor')
- key_weight_grad: float32 [1280, 1280], P(('shard', 'context'), 'tensor')
- value_weight_grad: float32 [1280, 1280], P(('shard', 'context'), 'tensor')
- out_weight_grad: float32 [1280, 1280], P('tensor', ('shard', 'context'))
- up_weight_grad: float32 [1280, 1280], P(('shard', 'context'), 'tensor')
- down_weight_grad: float32 [1280, 1280], P('tensor', ('shard', 'context'))
- pre_gain_grad: float32 [1280], P(('shard', 'context'))
- pre_shift_grad: float32 [1280], P(('shard', 'context'))
- mid_gain_grad: float32 [1280], P(('shard', 'context'))
- mid_shift_grad: float32 [1280], P(('shard', 'context'))
- query_bias_grad: float32 [1280], P('tensor')
- value_bias_grad: float32 [1280], P('tensor')
- out_bias_grad: float32 [1280], P(('shard', 'context'))
- up_bias_grad: float32 [1280], P('tensor')
- down_bias_grad: float32 [1280], P(('shard', 'context'))
- output_magnitude: float32 [8], P('shard')
Inputs may be any that keep to these rules, and one draw needn't show every extreme that they name: `prompt_tokens`: the block's input on the prompt rows. `later_tokens`: the block's input on the continuations.
All inputs are finite; a program needn't handle non-finite values.
Results may differ from a plain program's by a relative error of at most 0.019.
Values may be sent and summed in bfloat16 or wider, within the bound.
No kernel may reach another device: no remote copies, remote signals or barrier semaphores. Data moves between devices by JAX's collectives and lax.ppermute only.
A program may use at most 448 MiB of HBM per device.

v0:
```python
import functools
import math

import jax
import jax.numpy as jnp
from jax import lax
from jax.experimental import pallas as pl
from jax.experimental.pallas import tpu as pltpu
from jax.sharding import PartitionSpec as P

S, C, T = "shard", "context", "tensor"
SC = (S, C)
ALL = (S, C, T)
HEAD = 160
WIDE = 256
PAIR = 2
EPSILON = 1e-05
MASKED = -1e30
SCALE = HEAD**-0.5
LOG2E = math.log2(math.e)
VMEM = 58 * 1024 * 1024
bf16 = jnp.bfloat16
f32 = jnp.float32


def nt(a, b):
    return lax.dot_general(a, b, (((1,), (1,)), ((), ())), preferred_element_type=f32)


def nn(a, b):
    return lax.dot_general(a, b, (((1,), (0,)), ((), ())), preferred_element_type=f32)


def tn(a, b):
    return lax.dot_general(a, b, (((0,), (0,)), ((), ())), preferred_element_type=f32)


def normalise(values):
    centre = values - jnp.mean(values, axis=-1, keepdims=True)
    spread = jnp.mean(centre * centre, axis=-1, keepdims=True)
    inverse = lax.rsqrt(spread + EPSILON)
    return centre * inverse, inverse


def norm_back(grad, unit, inverse, gain):
    e = grad * gain
    inner = e - jnp.mean(e, axis=-1, keepdims=True)
    return (inner - unit * jnp.mean(e * unit, axis=-1, keepdims=True)) * inverse


def part(h):
    return slice(h * HEAD, (h + 1) * HEAD)


def wide(h):
    return slice(h * WIDE, (h + 1) * WIDE)


def tail(values, first):
    lane = lax.broadcasted_iota(jnp.int32, (values.shape[0], WIDE - HEAD), 1)
    return jnp.concatenate([values, jnp.where(lane == 0, first, 0.0)], axis=1)


def params(count=1):
    return pltpu.CompilerParams(
        vmem_limit_bytes=VMEM, dimension_semantics=("arbitrary",) * count
    )


def whole(shape):
    return pl.BlockSpec(shape, lambda j: (0,) * len(shape))


def project_kernel(fresh, later, own, info, x_ref, w_ref, g_ref, s_ref, qb_ref, vb_ref, *rest):
    q_ref, k_ref, v_ref = rest[:3]
    w_pad = rest[-1]
    j = pl.program_id(0)
    rows = x_ref.shape[0]
    prompt_all = pl.num_programs(0) * rows - later

    @pl.when(j == 0)
    def _():
        w_pad[...] = jnp.zeros_like(w_pad)
        for i in range(3 * PAIR):
            w_pad[:, i * WIDE : i * WIDE + HEAD] = w_ref[:, part(i)]

    if fresh:
        unit, _ = normalise(x_ref[...].astype(f32))
        normed = (unit * g_ref[...] + s_ref[...]).astype(bf16)
        rest[3][...] = normed
    else:
        normed = x_ref[...]

    @pl.when(j * rows < own)
    def _():
        for h in range(PAIR):
            row = tail(qb_ref[:, part(h)] * (SCALE * LOG2E), 1.0)
            product = nn(normed, w_pad[:, wide(h)])
            q_ref[:, wide(h)] = (product * (SCALE * LOG2E) + row).astype(bf16)

    place = lax.broadcasted_iota(jnp.int32, (rows, 1), 0) + (j * rows - later)
    where = place + info[1]
    where = jnp.where(where >= prompt_all, where - prompt_all, where)
    bias = jnp.where((place < 0) | (where < info[0]), 0.0, MASKED)
    lane = lax.broadcasted_iota(jnp.int32, (rows, WIDE), 1)
    mark = jnp.where(lane == HEAD, bias, 0.0)
    for h in range(PAIR):
        k_ref[:, wide(h)] = (nn(normed, w_pad[:, wide(PAIR + h)]) + mark).astype(bf16)
        row = tail(vb_ref[:, part(h)], 1.0)
        v_ref[:, wide(h)] = (nn(normed, w_pad[:, wide(2 * PAIR + h)]) + row).astype(bf16)


def project(fresh, info, x, weight, gain, shift, q_bias, v_bias, later, own):
    total, width = x.shape
    rows = min(512, later, own - later)
    last = own // rows - 1
    cols = PAIR * WIDE
    shapes = [(own, cols), (total, cols), (total, cols)] + ([(total, width)] if fresh else [])
    specs = [pl.BlockSpec((rows, cols), lambda j: (jnp.minimum(j, last), 0))]
    specs += [pl.BlockSpec((rows, s[1]), lambda j: (j, 0)) for s in shapes[1:]]
    return pl.pallas_call(
        functools.partial(project_kernel, fresh, later, own),
        grid=(total // rows,),
        in_specs=[
            pl.BlockSpec(memory_space=pltpu.SMEM),
            pl.BlockSpec((rows, width), lambda j: (j, 0)),
            whole(weight.shape),
            whole(gain.shape),
            whole(shift.shape),
            whole(q_bias.shape),
            whole(v_bias.shape),
        ],
        out_specs=specs,
        out_shape=[jax.ShapeDtypeStruct(s, bf16) for s in shapes],
        scratch_shapes=[pltpu.VMEM((width, 3 * PAIR * WIDE), bf16)],
        compiler_params=params(),
        cost_estimate=pl.CostEstimate(
            flops=6 * total * width * cols, bytes_accessed=8 * total * width, transcendentals=0
        ),
    )(info, x, weight, gain, shift, q_bias, v_bias)


def causal(count):
    row = lax.broadcasted_iota(jnp.int32, (count, count), 0)
    return row >= lax.broadcasted_iota(jnp.int32, (count, count), 1)


def attend_kernel(later, cont, q_ref, k_ref, v_ref, o_ref, log_ref):
    j = pl.program_id(0)
    rows = q_ref.shape[0]
    lanes = lax.broadcasted_iota(jnp.int32, (rows, 128), 1)

    def run(is_later):
        logs = jnp.zeros((rows, 128), f32)
        outs = []
        for h in range(PAIR):
            q = q_ref[:, wide(h)]
            scores = nt(q, k_ref[later:, wide(h)])
            top = jnp.max(scores, axis=1, keepdims=True)
            if is_later:
                near = []
                for i in range(rows // cont):
                    at = pl.ds(pl.multiple_of(j * rows + i * cont, cont), cont)
                    block = nt(q[i * cont : (i + 1) * cont], k_ref[at, wide(h)])
                    near.append(jnp.where(causal(cont), block, MASKED))
                near = jnp.concatenate(near, axis=0)
                top = jnp.maximum(top, jnp.max(near, axis=1, keepdims=True))
            out = nn(jnp.exp2(scores - top).astype(bf16), v_ref[later:, wide(h)])
            if is_later:
                near = jnp.exp2(near - top).astype(bf16)
                extra = []
                for i in range(rows // cont):
                    at = pl.ds(pl.multiple_of(j * rows + i * cont, cont), cont)
                    extra.append(nn(near[i * cont : (i + 1) * cont], v_ref[at, wide(h)]))
                out = out + jnp.concatenate(extra, axis=0)
            total = out[:, HEAD : HEAD + 1]
            outs.append(out[:, :HEAD] * (1.0 / total))
            logs = jnp.where(lanes == h, top + jnp.log2(total), logs)
        o_ref[...] = jnp.concatenate(outs, axis=1).astype(bf16)
        log_ref[...] = logs

    pl.when(j * rows < later)(lambda: run(True))
    pl.when(j * rows >= later)(lambda: run(False))


def attend(q, k, v, later, cont):
    own, cols = q.shape
    rows = min(512, later, own - later)
    block = lambda n: pl.BlockSpec((rows, n), lambda j: (j, 0))
    return pl.pallas_call(
        functools.partial(attend_kernel, later, cont),
        grid=(own // rows,),
        in_specs=[block(cols), whole(k.shape), whole(v.shape)],
        out_specs=[block(PAIR * HEAD), block(128)],
        out_shape=[
            jax.ShapeDtypeStruct((own, PAIR * HEAD), bf16),
            jax.ShapeDtypeStruct((own, 128), f32),
        ],
        compiler_params=params(),
        cost_estimate=pl.CostEstimate(
            flops=8 * own * k.shape[0] * cols // 2,
            bytes_accessed=8 * own * cols,
            transcendentals=own * k.shape[0],
        ),
    )(q, k, v)


def attend_back_kernel(
    later, cont, q_ref, k_ref, v_ref, o_ref, log_ref, g_ref, dq_ref, dk_ref, dv_ref, dk, dv
):
    j = pl.program_id(0)
    rows = q_ref.shape[0]

    @pl.when(j == 0)
    def _():
        dk[...] = jnp.zeros_like(dk)
        dv[...] = jnp.zeros_like(dv)

    def run(is_later):
        outs = []
        for h in range(PAIR):
            q = q_ref[:, wide(h)]
            log = log_ref[:, h : h + 1]
            g = g_ref[:, part(h)].astype(f32)
            inner = jnp.sum(g * o_ref[:, part(h)].astype(f32), axis=1, keepdims=True)
            g = tail(g, 0.0).astype(bf16)
            k = k_ref[later:, wide(h)]
            probs = jnp.exp2(nt(q, k) - log)
            drift = (probs * (nt(g, v_ref[later:, wide(h)]) - inner)).astype(bf16)
            dv[later:, wide(h)] += tn(probs.astype(bf16), g)
            dk[later:, wide(h)] += tn(drift, q)
            dq = nn(drift, k)
            if is_later:
                extra = []
                for i in range(rows // cont):
                    at = pl.ds(pl.multiple_of(j * rows + i * cont, cont), cont)
                    mine = slice(i * cont, (i + 1) * cont)
                    k = k_ref[at, wide(h)]
                    probs = jnp.where(causal(cont), jnp.exp2(nt(q[mine], k) - log[mine]), 0.0)
                    drift = nt(g[mine], v_ref[at, wide(h)]) - inner[mine]
                    drift = (probs * drift).astype(bf16)
                    dv[at, wide(h)] += tn(probs.astype(bf16), g[mine])
                    dk[at, wide(h)] += tn(drift, q[mine])
                    extra.append(nn(drift, k))
                dq = dq + jnp.concatenate(extra, axis=0)
            outs.append(dq[:, :HEAD] * SCALE)
        dq_ref[...] = jnp.concatenate(outs, axis=1).astype(bf16)

    pl.when(j * rows < later)(lambda: run(True))
    pl.when(j * rows >= later)(lambda: run(False))

    @pl.when(j == pl.num_programs(0) - 1)
    def _():
        outs = [dk[:, h * WIDE : h * WIDE + HEAD] * (1.0 / LOG2E) for h in range(PAIR)]
        dk_ref[...] = jnp.concatenate(outs, axis=1).astype(bf16)
        outs = [dv[:, h * WIDE : h * WIDE + HEAD] for h in range(PAIR)]
        dv_ref[...] = jnp.concatenate(outs, axis=1).astype(bf16)


def attend_back(q, k, v, out, logs, grad, later, cont):
    own, cols = q.shape
    total = k.shape[0]
    dense = PAIR * HEAD
    rows = min(512, later, own - later)
    block = lambda n: pl.BlockSpec((rows, n), lambda j: (j, 0))
    return pl.pallas_call(
        functools.partial(attend_back_kernel, later, cont),
        grid=(own // rows,),
        in_specs=[block(cols), whole(k.shape), whole(v.shape), block(dense), block(128), block(dense)],
        out_specs=[block(dense), whole((total, dense)), whole((total, dense))],
        out_shape=[
            jax.ShapeDtypeStruct((own, dense), bf16),
            jax.ShapeDtypeStruct((total, dense), bf16),
            jax.ShapeDtypeStruct((total, dense), bf16),
        ],
        scratch_shapes=[pltpu.VMEM((total, cols), f32)] * 2,
        compiler_params=params(),
        cost_estimate=pl.CostEstimate(
            flops=10 * own * total * cols,
            bytes_accessed=16 * own * cols,
            transcendentals=own * total * PAIR,
        ),
    )(q, k, v, out, logs, grad)


def swap(value, axis, bit):
    count = lax.axis_size(axis)
    return lax.ppermute(value, axis, [(i, i ^ bit) for i in range(count)])


def in_order(index, mine, theirs, axis=0):
    first = index == 0
    return jnp.stack(
        [jnp.where(first, mine, theirs), jnp.where(first, theirs, mine)], axis=axis
    )


def gather_rows(piece):
    if lax.axis_size(C) != 2:
        return lax.all_gather(piece, SC, axis=0, tiled=True)
    stacked = lax.all_gather(piece, S, axis=0, tiled=False)
    other = swap(stacked, C, 1)
    return in_order(lax.axis_index(C), stacked, other, 1).reshape(-1, piece.shape[1])


def scatter_rows(whole_sum):
    n = lax.axis_size(S) * lax.axis_size(C)
    low = whole_sum.astype(bf16)
    if lax.axis_size(C) != 2:
        return lax.psum_scatter(low, SC, scatter_dimension=0, tiled=True).astype(f32)
    split = whole_sum.reshape(lax.axis_size(S), 2, -1, whole_sum.shape[1])
    x = lax.axis_index(C)
    away = lax.dynamic_index_in_dim(split, 1 - x, 1, keepdims=False)
    keep = lax.dynamic_index_in_dim(split, x, 1, keepdims=False)
    summed = keep.astype(f32) + swap(away.astype(bf16), C, 1).astype(f32)
    summed = summed.reshape(-1, whole_sum.shape[1]).astype(bf16)
    return lax.psum_scatter(summed, S, scatter_dimension=0, tiled=True).astype(f32)


def pick(array, index, axis=0):
    return lax.dynamic_index_in_dim(array, index, axis, keepdims=False)


def body(
    prompt_tokens,
    later_tokens,
    prompt_upstream,
    later_upstream,
    prompt_lengths,
    later_lengths,
    query_weight,
    key_weight,
    value_weight,
    out_weight,
    up_weight,
    down_weight,
    pre_gain,
    pre_shift,
    mid_gain,
    mid_shift,
    query_bias,
    value_bias,
    out_bias,
    up_bias,
    down_bias,
):
    groups, prompt_rows, width = prompt_tokens.shape
    count, cont = later_tokens.shape[1:3]
    later = count * cont
    own = later + prompt_rows
    contexts = lax.axis_size(C)
    prompt_all = prompt_rows * contexts
    cols = query_weight.shape[1]
    x = lax.axis_index(C)
    t = lax.axis_index(T)
    y, c = t // 2, t % 2
    turn = (t, t ^ 2, t ^ 1, t ^ 3)

    def mine(array):
        return pick(array.reshape(2, 2, -1, *array.shape[1:]), c, 1).reshape(
            -1, *array.shape[1:]
        )

    def theirs(array):
        return pick(array.reshape(2, 2, -1, *array.shape[1:]), 1 - c, 1).reshape(
            -1, *array.shape[1:]
        )

    def join(own_half, other_half):
        a = own_half.reshape(2, -1, own_half.shape[-1])
        b = other_half.reshape(2, -1, own_half.shape[-1])
        return in_order(c, a, b, 1).reshape(-1, own_half.shape[-1])

    qkv_own = gather_rows(jnp.concatenate([query_weight, key_weight, value_weight], axis=1))
    oud_own = gather_rows(jnp.concatenate([out_weight.T, up_weight, down_weight.T], axis=1))
    vectors = jnp.stack([pre_gain, pre_shift, mid_gain, mid_shift, out_bias, down_bias])
    vectors = lax.all_gather(vectors, SC, axis=1, tiled=True).astype(f32)
    pre_gain, pre_shift, mid_gain, mid_shift, out_bias, down_bias = [
        vectors[i : i + 1] for i in range(6)
    ]
    biases = lax.all_gather(jnp.stack([query_bias, value_bias, up_bias]), T).astype(f32)
    biases = jnp.stack([pick(biases, i) for i in turn])
    up_bias = biases[:, 2].reshape(1, -1)

    prompt = pick(prompt_tokens, y)
    follow = pick(later_tokens, y).reshape(later, width)
    tokens = jnp.concatenate([follow, prompt], axis=0)
    if contexts == 2:
        half = pick(prompt.reshape(2, -1, width), c)
        half = swap(half, C, 1)
        beyond = in_order(c, half, swap(half, T, 1)).reshape(-1, width)
    else:
        beyond = lax.all_gather(prompt, C)
        beyond = jnp.roll(beyond, -x, axis=0)[1:].reshape(-1, width)
    length = pick(prompt_lengths, y)
    lengths = pick(later_lengths, y)
    info = jnp.stack([length, x * prompt_rows]).astype(jnp.int32)

    qkv_far = swap(qkv_own, T, 2)
    oud_far = swap(oud_own, T, 2)
    oud_pair = jnp.stack([oud_own, oud_far])
    oud_core = swap(oud_pair, T, 1)

    q0, k0, v0, normed_in = project(
        True,
        info,
        jnp.concatenate([tokens, beyond], axis=0),
        qkv_own,
        pre_gain,
        pre_shift,
        biases[0, 0:1],
        biases[0, 1:2],
        later,
        own,
    )
    a0, log0 = attend(q0, k0, v0, later, cont)
    q1, k1, v1 = project(
        False, info, normed_in, qkv_far, pre_gain, pre_shift,
        biases[1, 0:1], biases[1, 1:2], later, own,
    )
    a1, log1 = attend(q1, k1, v1, later, cont)

    attended = jnp.concatenate([a0, a1], axis=1)
    attended = jnp.concatenate([mine(attended), swap(theirs(attended), T, 1)], axis=1)
    out_t, up, down_t = [
        jnp.concatenate(
            [w[:, i * cols : (i + 1) * cols] for w in (oud_own, oud_far, oud_core[0], oud_core[1])],
            axis=1,
        )
        for i in range(3)
    ]
    row_tokens = mine(tokens).astype(f32)
    mixed = row_tokens + nt(attended, out_t) + out_bias
    unit, inverse = normalise(mixed)
    normed_mid = (unit * mid_gain + mid_shift).astype(bf16)
    upper = nn(normed_mid, up) + up_bias
    cumulative = 0.5 * (1.0 + lax.erf(upper * (0.5**0.5)))
    active = (upper * cumulative).astype(bf16)
    output = mixed + nt(active, down_t) + down_bias

    later_valid = jnp.arange(cont, dtype=jnp.int32)[None, :] < lengths[:, None]
    prompt_valid = x * prompt_rows + jnp.arange(prompt_rows, dtype=jnp.int32) < length
    valid = jnp.concatenate([later_valid.reshape(later), prompt_valid]).astype(f32)
    valid = mine(valid[:, None])
    squares = jnp.sum(output * output * valid)
    here = (jnp.arange(groups, dtype=jnp.int32) == y).astype(f32)[:, None]
    sums = here * jnp.stack([squares, jnp.sum(valid)])[None, :]
    sums = lax.psum(sums, (C, T))
    magnitude = jnp.sqrt(sums[:, 0] / (sums[:, 1] * width))

    output_low = output.astype(bf16)

    def spread(rows_mine):
        other = swap(rows_mine, T, 2)
        both = jnp.stack([rows_mine, other])
        core = swap(both, T, 1)
        near, far = join(both[0], core[0]), join(both[1], core[1])
        full = in_order(y, near, far)
        follow = full[:, :later].reshape(groups, count, cont, width)
        return full[:, later:], follow

    prompt_output, later_output = spread(output_low)

    upstream = jnp.concatenate(
        [pick(later_upstream, y).reshape(later, width), pick(prompt_upstream, y)], axis=0
    )
    grad_low = (mine(upstream).astype(f32) * valid).astype(bf16)
    grad_out = grad_low.astype(f32)
    down_grad = tn(grad_low, active)
    down_bias_grad = jnp.sum(grad_out, axis=0)
    density = jnp.exp(-0.5 * upper * upper) * (1.0 / math.sqrt(2.0 * math.pi))
    grad_upper = nn(grad_low, down_t) * (cumulative + upper * density)
    grad_upper_low = grad_upper.astype(bf16)
    up_grad = tn(normed_mid, grad_upper_low)
    up_bias_grad = jnp.sum(grad_upper, axis=0)
    grad_mid = nt(grad_upper_low, up)
    mid_gain_grad = jnp.sum(grad_mid * unit, axis=0)
    mid_shift_grad = jnp.sum(grad_mid, axis=0)
    grad_mixed = grad_out + norm_back(grad_mid, unit, inverse, mid_gain)
    grad_mixed_low = grad_mixed.astype(bf16)
    out_grad = tn(grad_mixed_low, attended)
    out_bias_grad = jnp.sum(grad_mixed, axis=0)
    grad_attended = nn(grad_mixed_low, out_t).astype(bf16)

    def over_cores(grad):
        grad = grad.astype(bf16).reshape(width, 4, cols)
        return grad[:, :2].reshape(width, -1), grad[:, 2:].reshape(width, -1)

    pairs = [over_cores(g) for g in (out_grad, up_grad, down_grad)]
    summed = [a.astype(f32) + swap(b, T, 1).astype(f32) for a, b in pairs]
    near = jnp.concatenate([g[:, :cols] for g in summed], axis=1)
    far = jnp.concatenate([g[:, cols:] for g in summed], axis=1)
    oud_grad = scatter_rows(near + swap(far.astype(bf16), T, 2).astype(f32))
    out_weight_grad = oud_grad[:, :cols].T
    up_weight_grad = oud_grad[:, cols : 2 * cols]
    down_weight_grad = oud_grad[:, 2 * cols :].T

    half = 2 * cols
    grad_heads = join(grad_attended[:, :half], swap(grad_attended[:, half:], T, 1))
    dq0, dk0, dv0 = attend_back(q0, k0, v0, a0, log0, grad_heads[:, :cols], later, cont)
    dq1, dk1, dv1 = attend_back(q1, k1, v1, a1, log1, grad_heads[:, cols:], later, cont)

    def weight_sums(dq, dk, dv):
        return jnp.concatenate(
            [tn(normed_in[:own], dq), tn(normed_in, dk), tn(normed_in, dv)], axis=1
        )

    near = weight_sums(dq0, dk0, dv0)
    far = weight_sums(dq1, dk1, dv1)
    qkv_grad = scatter_rows(near + swap(far.astype(bf16), T, 2).astype(f32))

    own_share = nt(
        jnp.concatenate([dq0, dk0[:own], dv0[:own]], axis=1), qkv_own
    ) + nt(jnp.concatenate([dq1, dk1[:own], dv1[:own]], axis=1), qkv_far)
    beyond_share = nt(jnp.concatenate([dk0[own:], dv0[own:]], axis=1), qkv_own[:, cols:]) + nt(
        jnp.concatenate([dk1[own:], dv1[own:]], axis=1), qkv_far[:, cols:]
    )
    grad_in = mine(own_share) + swap(theirs(own_share).astype(bf16), T, 1).astype(f32)
    if contexts == 2:
        split = beyond_share.reshape(2, -1, width)
        back = pick(split, c) + swap(pick(split, 1 - c).astype(bf16), T, 1).astype(f32)
        back = swap(back.astype(bf16), C, 1).astype(f32)
    else:
        back = beyond_share + swap(beyond_share.astype(bf16), T, 1).astype(f32)
        back = back.reshape(contexts - 1, prompt_rows, width)
        back = jnp.concatenate([jnp.zeros_like(back[:1]), back], axis=0)
        back = jnp.roll(back, x, axis=0).astype(bf16)
        back = lax.psum_scatter(back, C, scatter_dimension=0, tiled=True).astype(f32)
        back = pick(back.reshape(2, -1, width), c)
    grad_in = grad_in + jnp.concatenate([jnp.zeros((later // 2, width), f32), back], axis=0)
    unit, inverse = normalise(row_tokens)
    pre_gain_grad = jnp.sum(grad_in * unit, axis=0)
    pre_shift_grad = jnp.sum(grad_in, axis=0)
    grad_tokens = grad_mixed + norm_back(grad_in, unit, inverse, pre_gain)
    prompt_grad, later_grad = spread(grad_tokens.astype(bf16))

    def placed(pieces, places):
        rows = jnp.zeros((lax.axis_size(T), cols), f32)
        for piece, place in zip(pieces, places):
            rows = lax.dynamic_update_slice(rows, piece.reshape(1, cols), (place, 0))
        return rows.reshape(-1)

    def total(values):
        return jnp.sum(values.astype(f32), axis=0)

    sums = jnp.stack(
        [
            pre_gain_grad,
            pre_shift_grad,
            mid_gain_grad,
            mid_shift_grad,
            out_bias_grad,
            down_bias_grad,
            placed([total(dq0), total(dq1)], [t, t ^ 2]),
            placed([total(dv0), total(dv1)], [t, t ^ 2]),
            placed(list(up_bias_grad.reshape(4, cols)), turn),
        ]
    )
    sums = lax.psum(sums, ALL)
    n = lax.axis_size(S) * contexts
    z = lax.axis_index(S) * contexts + x
    full = lax.dynamic_slice(sums, (0, z * (width // n)), (6, width // n))
    heads = lax.dynamic_slice(sums, (6, t * cols), (3, cols))

    return (
        prompt_output,
        later_output,
        prompt_grad.astype(f32),
        later_grad.astype(f32),
        qkv_grad[:, :cols],
        qkv_grad[:, cols : 2 * cols],
        qkv_grad[:, 2 * cols :],
        out_weight_grad,
        up_weight_grad,
        down_weight_grad,
        full[0],
        full[1],
        full[2],
        full[3],
        heads[0],
        heads[1],
        full[4],
        heads[2],
        full[5],
        magnitude,
    )


def solution(mesh):
    rows, later, vector = P(S, C, None), P(S, C, None, None), P(SC)
    weight, turned, column = P(SC, T), P(T, SC), P(T)
    return jax.shard_map(
        body,
        mesh=mesh,
        in_specs=(rows, later, rows, later, P(S), P(S, C))
        + (weight, weight, weight, turned, weight, turned)
        + (vector,) * 4
        + (column, column, vector, column, vector),
        out_specs=(rows, later, rows, later)
        + (weight, weight, weight, turned, weight, turned)
        + (vector,) * 4
        + (column, column, vector, column, vector, P(S)),
        check_vma=False,
    )
```

profile of v0, /device:TPU:0, one launch (start us, length us, event | category | flops | bytes accessed | tf_op | source)
XLA Modules:
  0.0 794.8 jit_solution(14545832424747933413)
XLA Ops:
  24.7 44.3 %all-gather.3 = bf16[8,160,6]{1,2,0:T(8,128)(2,1)S(1)} all-gather(bf16[1,160,6]{1,2,0:T(8,128)(2,1)S(1)} %bitcast.288), channel_id=1, replica_groups=mesh['shard'=4,'context'=2,'tensor'=4] {'shard','context'}, dimensions={0}, use_global_device_ids=true | all-gather | bytes 17280 | tf_op jit(solution)/shard_map/all_gather | solution.py:377
  97.1 22.8 %collective-permute-done.5 = bf16[4,160,960]{2,1,0:T(8,128)(2,1)S(1)} collective-permute-done((bf16[4,160,960]{2,1,0:T(8,128)(2,1)}, bf16[4,160,960]{2,1,0:T(8,128)(2,1)S(1)}, u32[]{:S(2)}, u32[]{:S(2)}) %collective-permute-start.5) | collective-permute-done | bytes 1228832 | tf_op jit(solution)/shard_map/ppermute | solution.py:288
  124.9 8.1 %pad_maximum_fusion.x_ref = bf16[3072,1280]{1,0:T(8,128)(2,1)} fusion(bf16[1024,1280]{1,0:T(8,128)(2,1)} %bitcast.260, bf16[1024,1280]{1,0:T(8,128)(2,1)} %copy-done.4, bf16[1024,1280]{1,0:T(8,128)(2,1)} %bitcast.229), kind=kLoop, calls=%fused_computation.5 | loop fusion | flops 23592960 | bytes 15728640 | tf_op jit(solution)/shard_map/concatenate | solution.py:407
  133.0 12.4 %collective-permute-done.2 = bf16[4,160,960]{2,1,0:T(8,128)(2,1)} collective-permute-done((bf16[4,160,960]{2,1,0:T(8,128)(2,1)}, bf16[4,160,960]{2,1,0:T(8,128)(2,1)}, u32[]{:S(2)}, u32[]{:S(2)}) %collective-permute-start.2) | collective-permute-done | bytes 1228832 | tf_op jit(solution)/shard_map/ppermute | solution.py:288
  154.9 23.3 %shard_map.356 = (bf16[2048,512]{1,0:T(8,128)(2,1)}, bf16[3072,512]{1,0:T(8,128)(2,1)}, bf16[3072,512]{1,0:T(8,128)(2,1)}, bf16[3072,1280]{1,0:T(8,128)(2,1)}) custom-call(s32[2]{0:T(128)} %pad_add_fusion.info, bf16[3072,1280]{1,0:T(8,128)(2,1)} %pad_maximum_fusion.x_ref, bf16[1280,960]{1,0:T(8,128)(2,1)} %bitcast.251, f32[1,1280]{1,0:T(1,128)} %get-tuple-element.141.g_ref, ...), custom_call_target="tpu_custom_call" | custom-call | flops 12079595520 | bytes 31457280 | tf_op jit(solution)/shard_map/pallas_call | solution.py:121
  189.0 7.9 copy.113
  199.2 20.6 %shard_map.357 = (bf16[2048,320]{1,0:T(8,128)(2,1)}, f32[2048,128]{1,0:T(8,128)}) custom-call(bf16[2048,512]{1,0:T(8,128)(2,1)} %get-tuple-element.37.q_ref, bf16[3072,512]{1,0:T(8,128)(2,1)} %get-tuple-element.38.k_ref, bf16[3072,512]{1,0:T(8,128)(2,1)} %get-tuple-element.39.v_ref), custom_call_target="tpu_custom_call" | custom-call | flops 12884901888 | bytes 8388608 | tf_op jit(solution)/shard_map/pallas_call | solution.py:190
  230.7 17.5 %shard_map.358 = (bf16[2048,512]{1,0:T(8,128)(2,1)}, bf16[3072,512]{1,0:T(8,128)(2,1)}, bf16[3072,512]{1,0:T(8,128)(2,1)}) custom-call(s32[2]{0:T(128)} %pad_add_fusion.info, bf16[3072,1280]{1,0:T(8,128)(2,1)} %get-tuple-element.41.x_ref, bf16[1280,960]{1,0:T(8,128)(2,1)} %copy.108.w_ref, f32[1,1280]{1,0:T(1,128)} %get-tuple-element.141.g_ref, ...), custom_call_target="tpu_custom_call" | custom-call | flops 12079595520 | bytes 31457280 | tf_op jit(solution)/shard_map/pallas_call | solution.py:121
  248.2 20.3 %shard_map.359 = (bf16[2048,320]{1,0:T(8,128)(2,1)}, f32[2048,128]{1,0:T(8,128)}) custom-call(bf16[2048,512]{1,0:T(8,128)(2,1)} %get-tuple-element.42.q_ref, bf16[3072,512]{1,0:T(8,128)(2,1)} %get-tuple-element.43.k_ref, bf16[3072,512]{1,0:T(8,128)(2,1)} %get-tuple-element.44.v_ref), custom_call_target="tpu_custom_call" | custom-call | flops 12884901888 | bytes 8388608 | tf_op jit(solution)/shard_map/pallas_call | solution.py:190
  310.9 6.8 concatenate.84
  324.4 7.2 multiply_convert_fusion.1
  331.6 7.7 multiply_reduce_fusion
  383.7 38.7 %shard_map.361 = (bf16[2048,320]{1,0:T(8,128)(2,1)}, bf16[3072,320]{1,0:T(8,128)(2,1)}, bf16[3072,320]{1,0:T(8,128)(2,1)}) custom-call(bf16[2048,512]{1,0:T(8,128)(2,1)} %get-tuple-element.42.q_ref, bf16[3072,512]{1,0:T(8,128)(2,1)} %get-tuple-element.43.k_ref, bf16[3072,512]{1,0:T(8,128)(2,1)} %get-tuple-element.44.v_ref, ...), custom_call_target="tpu_custom_call" | custom-call | flops 32212254720 | bytes 16777216 | tf_op jit(solution)/shard_map/pallas_call | solution.py:266
  441.9 38.7 %shard_map.360 = (bf16[2048,320]{1,0:T(8,128)(2,1)}, bf16[3072,320]{1,0:T(8,128)(2,1)}, bf16[3072,320]{1,0:T(8,128)(2,1)}) custom-call(bf16[2048,512]{1,0:T(8,128)(2,1)} %get-tuple-element.37.q_ref, bf16[3072,512]{1,0:T(8,128)(2,1)} %get-tuple-element.38.k_ref, bf16[3072,512]{1,0:T(8,128)(2,1)} %get-tuple-element.39.v_ref, ...), custom_call_target="tpu_custom_call" | custom-call | flops 32212254720 | bytes 16777216 | tf_op jit(solution)/shard_map/pallas_call | solution.py:266
  483.5 7.4 fusion.96
  491.3 7.3 fusion.97
  504.8 8.5 %fusion.27 = f32[2048,1280]{1,0:T(8,128)} fusion(bf16[1280,960]{1,0:T(8,128)(2,1)S(1)} %bitcast.253, bf16[2048,320]{1,0:T(8,128)(2,1)S(1)} %slice.276, bf16[2048,320]{1,0:T(8,128)(2,1)S(1)} %slice.275, bf16[2048,320]{1,0:T(8,128)(2,1)S(1)} %copy-done.31), kind=kOutput, calls=%fused_computation.78 | convolution fusion | flops 5044961280 | bytes 16875520 | tf_op jit(solution)/shard_map/dot_general | solution.py:27
  517.0 10.1 %convolution_add_fusion = f32[2048,1280]{1,0:T(8,128)S(1)} fusion(f32[2048,1280]{1,0:T(8,128)} %fusion.27, bf16[1280,960]{0,1:T(8,128)(2,1)} %collective-permute-done.3, bf16[2048,320]{1,0:T(8,128)(2,1)} %slice.279, bf16[2048,320]{1,0:T(8,128)(2,1)} %slice.278, bf16[2048,320]{1,0:T(8,128)(2,1)} %get-tuple-element.51), kind=kOutput, calls=%fused_computation.4 | convolution fusion | flops 5047582720 | bytes 27361280 | tf_op jit(solution)/shard_map/dot_general | solution.py:27
  575.0 8.6 %collective-permute-done.13 = bf16[512,1280]{1,0:T(8,128)(2,1)} collective-permute-done((bf16[512,1280]{1,0:T(8,128)(2,1)}, bf16[512,1280]{1,0:T(8,128)(2,1)}, u32[]{:S(2)}, u32[]{:S(2)}) %collective-permute-start.13) | collective-permute-done | bytes 1310752 | tf_op jit(solution)/shard_map/ppermute | solution.py:288
  583.6 7.6 fusion.22
  591.3 19.1 %collective-permute-done.17 = bf16[4,160,960]{2,1,0:T(8,128)(2,1)S(1)} collective-permute-done((bf16[4,160,960]{2,1,0:T(8,128)(2,1)S(1)}, bf16[4,160,960]{2,1,0:T(8,128)(2,1)S(1)}, u32[]{:S(2)}, u32[]{:S(2)}) %collective-permute-start.17) | collective-permute-done | bytes 1228832 | tf_op jit(solution)/shard_map/ppermute | solution.py:288
  636.7 18.2 %collective-permute-done.22 = bf16[4,160,960]{2,1,0:T(8,128)(2,1)S(1)} collective-permute-done((bf16[4,160,960]{2,1,0:T(8,128)(2,1)S(1)}, bf16[4,160,960]{2,1,0:T(8,128)(2,1)S(1)}, u32[]{:S(2)}, u32[]{:S(2)}) %collective-permute-start.22) | collective-permute-done | bytes 1228832 | tf_op jit(solution)/shard_map/ppermute | solution.py:288
  657.9 38.6 %psum.15 = f32[2,2]{0,1:T(2,128)S(1)} all-reduce(f32[2,2]{0,1:T(2,128)S(1)} %broadcast_multiply_fusion.6), channel_id=1, replica_groups=mesh['shard'=4,'context'=2,'tensor'=4] {'context','tensor'}, use_global_device_ids=true, to_apply=%region_24.25 | all-reduce | flops 4 | bytes 32 | tf_op jit(solution)/shard_map/psum | solution.py:448
  707.5 41.9 %psum.14 = f32[9,1280]{1,0:T(8,128)S(1)} all-reduce(f32[9,1280]{1,0:T(8,128)S(1)} %stack.207), channel_id=1, replica_groups=mesh['shard'=4,'context'=2,'tensor'=4] {'shard','context','tensor'}, use_global_device_ids=true, to_apply=%region_21.22 | all-reduce | flops 11520 | bytes 92160 | tf_op jit(solution)/shard_map/psum | solution.py:559
  (399 shorter events, 335.5 us)
Async XLA Ops:
  7.2 80.8 %all-gather.10.cloned.1.call-start = ((), (), s32[]{:S(2)}) async-start(), calls=%async_computation.5 | async-start | bytes 1638400 | tf_op jit(solution)/shard_map/all_gather | solution.py:301
  9.1 84.2 %all-gather.8.cloned.1.call-start = ((), (), s32[]{:S(2)}) async-start(), calls=%async_computation.4 | async-start | bytes 1638400 | tf_op jit(solution)/shard_map/all_gather | solution.py:301
  12.5 69.4 %collective-permute-start = (bf16[512,1280]{1,0:T(8,128)(2,1)}, bf16[512,1280]{1,0:T(8,128)(2,1)}, u32[]{:S(2)}, u32[]{:S(2)}) collective-permute-start(bf16[512,1280]{1,0:T(8,128)(2,1)} %dynamic-slice_bitcast_fusion.1), channel_id=1, source_target_pairs={{0,4},{4,0},{1,5},{5,1},{2,6},{6,2},{3,7},{7,3},{8,12},{12,8},{9,1... | collective-permute-start | bytes 3932168 | tf_op jit(solution)/shard_map/ppermute | solution.py:288
  16.3 734.4 %reduce-scatter.3.cloned.1.call-start = ((), (), s32[]{:S(2)}) async-start(), calls=%async_computation.2 | async-start | bytes 1638400 | tf_op jit(solution)/shard_map/reduce_scatter | solution.py:317
  88.0 31.9 %collective-permute-start.5 = (bf16[4,160,960]{2,1,0:T(8,128)(2,1)}, bf16[4,160,960]{2,1,0:T(8,128)(2,1)S(1)}, u32[]{:S(2)}, u32[]{:S(2)}) collective-permute-start(bf16[4,160,960]{2,1,0:T(8,128)(2,1)} %bitcast.274), channel_id=1, source_target_pairs={{0,4},{4,0},{1,5},{5,1},{2,6},{6,2},{3,7},{7,3},{8,12},{12,8},{9,1... | collective-permute-start | bytes 3686408 | tf_op jit(solution)/shard_map/ppermute | solution.py:288
  93.4 52.1 %collective-permute-start.2 = (bf16[4,160,960]{2,1,0:T(8,128)(2,1)}, bf16[4,160,960]{2,1,0:T(8,128)(2,1)}, u32[]{:S(2)}, u32[]{:S(2)}) collective-permute-start(bf16[4,160,960]{2,1,0:T(8,128)(2,1)} %bitcast.276), channel_id=1, source_target_pairs={{0,4},{4,0},{1,5},{5,1},{2,6},{6,2},{3,7},{7,3},{8,12},{12,8},{9,1... | collective-permute-start | bytes 3686408 | tf_op jit(solution)/shard_map/ppermute | solution.py:288
  123.4 56.6 %collective-permute-start.6 = (bf16[1280,960]{0,1:T(8,128)(2,1)}, bf16[1280,960]{0,1:T(8,128)(2,1)}, u32[]{:S(2)}, u32[]{:S(2)}) collective-permute-start(bf16[1280,960]{0,1:T(8,128)(2,1)} %copy.110), channel_id=1, source_target_pairs={{0,2},{1,3},{2,0},{3,1},{4,6},{5,7},{6,4},{7,5},{8,10},{9,11},{10,... | collective-permute-start | bytes 7372808 | tf_op jit(solution)/shard_map/ppermute | solution.py:288
  153.4 72.9 %collective-permute-start.3 = (bf16[1280,960]{0,1:T(8,128)(2,1)}, bf16[1280,960]{0,1:T(8,128)(2,1)}, u32[]{:S(2)}, u32[]{:S(2)}) collective-permute-start(bf16[1280,960]{0,1:T(8,128)(2,1)} %copy.107), channel_id=1, source_target_pairs={{0,2},{1,3},{2,0},{3,1},{4,6},{5,7},{6,4},{7,5},{8,10},{9,11},{10,... | collective-permute-start | bytes 7372808 | tf_op jit(solution)/shard_map/ppermute | solution.py:288
  196.9 78.9 %collective-permute-start.7 = (bf16[2,1280,960]{1,2,0:T(8,128)(2,1)}, bf16[2,1280,960]{1,2,0:T(8,128)(2,1)}, u32[]{:S(2)}, u32[]{:S(2)}) collective-permute-start(bf16[2,1280,960]{1,2,0:T(8,128)(2,1)} %copy.113), channel_id=1, source_target_pairs={{0,1},{1,0},{2,3},{3,2},{4,5},{5,4},{6,7},{7,6},{8,9},{9,8},{10,11... | collective-permute-start | bytes 14745608 | tf_op jit(solution)/shard_map/ppermute | solution.py:288
  272.6 27.2 %collective-permute-start.4 = (bf16[1024,640]{1,0:T(8,128)(2,1)}, bf16[1024,640]{1,0:T(8,128)(2,1)}, u32[]{:S(2)}, u32[]{:S(2)}) collective-permute-start(bf16[1024,640]{1,0:T(8,128)(2,1)} %bitcast.24), channel_id=1, source_target_pairs={{0,1},{1,0},{2,3},{3,2},{4,5},{5,4},{6,7},{7,6},{8,9},{9,8},{10,11... | collective-permute-start | bytes 3932168 | tf_op jit(solution)/shard_map/ppermute | solution.py:288
  351.4 184.9 %collective-permute-start.20 = (bf16[1280,640]{0,1:T(8,128)(2,1)}, bf16[1280,640]{0,1:T(8,128)(2,1)}, u32[]{:S(2)}, u32[]{:S(2)}) collective-permute-start(bf16[1280,640]{0,1:T(8,128)(2,1)} %bitcast.85), channel_id=1, source_target_pairs={{0,1},{1,0},{2,3},{3,2},{4,5},{5,4},{6,7},{7,6},{8,9},{9,8},{10,11... | collective-permute-start | bytes 4915208 | tf_op jit(solution)/shard_map/ppermute | solution.py:288
  371.8 167.7 %collective-permute-start.18 = (bf16[1280,640]{0,1:T(8,128)(2,1)}, bf16[1280,640]{0,1:T(8,128)(2,1)}, u32[]{:S(2)}, u32[]{:S(2)}) collective-permute-start(bf16[1280,640]{0,1:T(8,128)(2,1)} %bitcast.79), channel_id=1, source_target_pairs={{0,1},{1,0},{2,3},{3,2},{4,5},{5,4},{6,7},{7,6},{8,9},{9,8},{10,11... | collective-permute-start | bytes 4915208 | tf_op jit(solution)/shard_map/ppermute | solution.py:288
  379.1 165.0 %collective-permute-start.19 = (bf16[1280,640]{0,1:T(8,128)(2,1)}, bf16[1280,640]{0,1:T(8,128)(2,1)}, u32[]{:S(2)}, u32[]{:S(2)}) collective-permute-start(bf16[1280,640]{0,1:T(8,128)(2,1)} %bitcast.82), channel_id=1, source_target_pairs={{0,1},{1,0},{2,3},{3,2},{4,5},{5,4},{6,7},{7,6},{8,9},{9,8},{10,11... | collective-permute-start | bytes 4915208 | tf_op jit(solution)/shard_map/ppermute | solution.py:288
  379.1 190.3 %collective-permute-start.8 = (bf16[1024,1280]{1,0:T(8,128)(2,1)}, bf16[1024,1280]{1,0:T(8,128)(2,1)}, u32[]{:S(2)}, u32[]{:S(2)}) collective-permute-start(bf16[1024,1280]{1,0:T(8,128)(2,1)} %get-tuple-element.84), channel_id=1, source_target_pairs={{0,2},{1,3},{2,0},{3,1},{4,6},{5,7},{6,4},{7,5},{8,10},{9,11},{10,... | collective-permute-start | bytes 7864328 | tf_op jit(solution)/shard_map/ppermute | solution.py:288
  500.8 56.3 %collective-permute-start.16 = (bf16[1280,960]{0,1:T(8,128)(2,1)S(1)}, bf16[1280,960]{0,1:T(8,128)(2,1)S(1)}, u32[]{:S(2)}, u32[]{:S(2)}) collective-permute-start(bf16[1280,960]{0,1:T(8,128)(2,1)S(1)} %pad_maximum_fusion.18), channel_id=1, source_target_pairs={{0,2},{1,3},{2,0},{3,1},{4,6},{5,7},{6,4},{7,5},{8,10},{9,11},{10,... | collective-permute-start | bytes 7372808 | tf_op jit(solution)/shard_map/ppermute | solution.py:288
  539.4 44.2 %collective-permute-start.11 = (bf16[1024,1280]{1,0:T(8,128)(2,1)}, bf16[1024,1280]{1,0:T(8,128)(2,1)}, u32[]{:S(2)}, u32[]{:S(2)}) collective-permute-start(bf16[1024,1280]{1,0:T(8,128)(2,1)} %bitcast.60), channel_id=1, source_target_pairs={{0,1},{1,0},{2,3},{3,2},{4,5},{5,4},{6,7},{7,6},{8,9},{9,8},{10,11... | collective-permute-start | bytes 7864328 | tf_op jit(solution)/shard_map/ppermute | solution.py:288
  549.7 62.4 %collective-permute-start.21 = (bf16[1280,960]{0,1:T(8,128)(2,1)}, bf16[1280,960]{0,1:T(8,128)(2,1)}, u32[]{:S(2)}, u32[]{:S(2)}) collective-permute-start(bf16[1280,960]{0,1:T(8,128)(2,1)} %pad_maximum_fusion.19), channel_id=1, source_target_pairs={{0,2},{1,3},{2,0},{3,1},{4,6},{5,7},{6,4},{7,5},{8,10},{9,11},{10,... | collective-permute-start | bytes 7372808 | tf_op jit(solution)/shard_map/ppermute | solution.py:288
  551.6 32.0 %collective-permute-start.13 = (bf16[512,1280]{1,0:T(8,128)(2,1)}, bf16[512,1280]{1,0:T(8,128)(2,1)}, u32[]{:S(2)}, u32[]{:S(2)}) collective-permute-start(bf16[512,1280]{1,0:T(8,128)(2,1)} %fusion.43), channel_id=1, source_target_pairs={{0,4},{4,0},{1,5},{5,1},{2,6},{6,2},{3,7},{7,3},{8,12},{12,8},{9,1... | collective-permute-start | bytes 3932168 | tf_op jit(solution)/shard_map/ppermute | solution.py:288
  567.9 42.5 %collective-permute-start.17 = (bf16[4,160,960]{2,1,0:T(8,128)(2,1)S(1)}, bf16[4,160,960]{2,1,0:T(8,128)(2,1)S(1)}, u32[]{:S(2)}, u32[]{:S(2)}) collective-permute-start(bf16[4,160,960]{2,1,0:T(8,128)(2,1)S(1)} %fusion.48), channel_id=1, source_target_pairs={{0,4},{4,0},{1,5},{5,1},{2,6},{6,2},{3,7},{7,3},{8,12},{12,8},{9,1... | collective-permute-start | bytes 3686408 | tf_op jit(solution)/shard_map/ppermute | solution.py:288
  574.9 181.3 %collective-permute-start.9 = (bf16[2,1024,1280]{2,1,0:T(8,128)(2,1)}, bf16[2,1024,1280]{2,1,0:T(8,128)(2,1)}, u32[]{:S(2)}, u32[]{:S(2)}) collective-permute-start(bf16[2,1024,1280]{2,1,0:T(8,128)(2,1)} %pad_maximum_fusion.5), channel_id=1, source_target_pairs={{0,1},{1,0},{2,3},{3,2},{4,5},{5,4},{6,7},{7,6},{8,9},{9,8},{10,11... | collective-permute-start | bytes 15728648 | tf_op jit(solution)/shard_map/ppermute | solution.py:288
  612.0 140.7 %reduce-scatter.5.cloned.1.call-start = ((), (), s32[]{:S(2)}) async-start(), calls=%async_computation.3 | async-start | bytes 1638400 | tf_op jit(solution)/shard_map/reduce_scatter | solution.py:317
  625.2 29.7 %collective-permute-start.22 = (bf16[4,160,960]{2,1,0:T(8,128)(2,1)S(1)}, bf16[4,160,960]{2,1,0:T(8,128)(2,1)S(1)}, u32[]{:S(2)}, u32[]{:S(2)}) collective-permute-start(bf16[4,160,960]{2,1,0:T(8,128)(2,1)S(1)} %fusion.49), channel_id=1, source_target_pairs={{0,4},{4,0},{1,5},{5,1},{2,6},{6,2},{3,7},{7,3},{8,12},{12,8},{9,1... | collective-permute-start | bytes 3686408 | tf_op jit(solution)/shard_map/ppermute | solution.py:288
  632.8 69.2 %collective-permute-start.14 = (bf16[1024,1280]{1,0:T(8,128)(2,1)S(1)}, bf16[1024,1280]{1,0:T(8,128)(2,1)}, u32[]{:S(2)}, u32[]{:S(2)}) collective-permute-start(bf16[1024,1280]{1,0:T(8,128)(2,1)S(1)} %fusion.21), channel_id=1, source_target_pairs={{0,2},{1,3},{2,0},{3,1},{4,6},{5,7},{6,4},{7,5},{8,10},{9,11},{10,... | collective-permute-start | bytes 7864328 | tf_op jit(solution)/shard_map/ppermute | solution.py:288
  706.7 64.2 %collective-permute-start.15 = (bf16[2,1024,1280]{2,1,0:T(8,128)(2,1)}, bf16[2,1024,1280]{2,1,0:T(8,128)(2,1)}, u32[]{:S(2)}, u32[]{:S(2)}) collective-permute-start(bf16[2,1024,1280]{2,1,0:T(8,128)(2,1)} %pad_maximum_fusion.9), channel_id=1, source_target_pairs={{0,1},{1,0},{2,3},{3,2},{4,5},{5,4},{6,7},{7,6},{8,9},{9,8},{10,11... | collective-permute-start | bytes 15728648 | tf_op jit(solution)/shard_map/ppermute | solution.py:288
  (78 other events, 1197.1 us)
Sparse Core Ops, SparseCore 0:
  10.2 35.3 all-gather.9
  47.7 31.8 all-gather.7
  612.1 32.1 reduce-scatter.2
  656.6 32.1 reduce-scatter.4
where the time goes:
time: 802 us; the launch traced here: 795 us
  Pallas kernels  159 us (20%)
  local copies, waits for them, and re-layouts  155 us (19%)
  blocking collectives  130 us (16%)
  other arithmetic  114 us (14%)
  matrix products  109 us (14%)
  waiting for transfers between devices  93.7 us (12%)
  starting transfers between devices  18.2 us (2%)
  between operations  15.4 us (2%)
    ppermute x23, waiting for transfers between devices, swap(): return lax.ppermute(value, axis, [(i, i ^ bit) for i in range(count)])  93.7 us
    pallas_call x2, Pallas kernels, attend_back(): pl.pallas_call(functools.partial(attend_back_kernel, later, cont), grid=(...  77.4 us
    dot_general x9, matrix products, tn(): lax.dot_general(a, b, (((0,), (0,)), ((), ())), preferred_element_type=f32)  47.8 us
    all_gather x1, blocking collectives, body(): vectors = lax.all_gather(vectors, SC, axis=1, tiled=True).astype(f32)  44.3 us
    dot_general x7, matrix products, nt(): lax.dot_general(a, b, (((1,), (1,)), ((), ())), preferred_element_type=f32)  43.7 us
    psum x1, blocking collectives, body(): sums = lax.psum(sums, ALL)  41.9 us
    pallas_call x2, Pallas kernels, attend(): pl.pallas_call(functools.partial(attend_kernel, later, cont), grid=(own /...  40.9 us
    pallas_call x2, Pallas kernels, project(): pl.pallas_call(functools.partial(project_kernel, fresh, later, own), grid...  40.8 us
  transfers between devices with their start and end apart: 27, of which 8 were waited for; matrix products, arithmetic and copies ran while one was open for 37% of the time, Pallas kernels for 20%

commit v1 on v0

v1 whole, which is shorter than its diff:
```python
import functools
import math

import jax
import jax.numpy as jnp
from jax import lax
from jax.experimental import pallas as pl
from jax.experimental.pallas import tpu as pltpu
from jax.sharding import PartitionSpec as P

S, C, T = "shard", "context", "tensor"
SC = (S, C)
ALL = (S, C, T)
HEAD = 160
WIDE = 256
PAIR = 2
EPSILON = 1e-05
MASKED = -1e30
SCALE = HEAD**-0.5
LOG2E = math.log2(math.e)
VMEM = 58 * 1024 * 1024
bf16 = jnp.bfloat16
f32 = jnp.float32


def nt(a, b):
    return lax.dot_general(a, b, (((1,), (1,)), ((), ())), preferred_element_type=f32)


def nn(a, b):
    return lax.dot_general(a, b, (((1,), (0,)), ((), ())), preferred_element_type=f32)


def tn(a, b):
    return lax.dot_general(a, b, (((0,), (0,)), ((), ())), preferred_element_type=f32)


def normalise(values):
    centre = values - jnp.mean(values, axis=-1, keepdims=True)
    spread = jnp.mean(centre * centre, axis=-1, keepdims=True)
    inverse = lax.rsqrt(spread + EPSILON)
    return centre * inverse, inverse


def norm_back(grad, unit, inverse, gain):
    e = grad * gain
    inner = e - jnp.mean(e, axis=-1, keepdims=True)
    return (inner - unit * jnp.mean(e * unit, axis=-1, keepdims=True)) * inverse


def part(h):
    return slice(h * HEAD, (h + 1) * HEAD)


def wide(h):
    return slice(h * WIDE, (h + 1) * WIDE)


def tail(values, first):
    lane = lax.broadcasted_iota(jnp.int32, (values.shape[0], WIDE - HEAD), 1)
    return jnp.concatenate([values, jnp.where(lane == 0, first, 0.0)], axis=1)


def params(count=1):
    return pltpu.CompilerParams(
        vmem_limit_bytes=VMEM, dimension_semantics=("arbitrary",) * count
    )


def whole(shape):
    return pl.BlockSpec(shape, lambda j, *_: (0,) * len(shape))


def once(shape):
    return pl.BlockSpec(
        shape, lambda j, *_: (0,) * len(shape), pipeline_mode=pl.Buffered(1)
    )


def cost(flops, moved, exps=0):
    return pl.CostEstimate(flops=int(flops), bytes_accessed=int(moved), transcendentals=0)


def project_kernel(fresh, own, spans, weights, info, *refs):
    x_refs, refs = refs[: len(spans)], refs[len(spans) :]
    w_refs, refs = refs[: len(weights)], refs[len(weights) :]
    qb_ref, vb_ref, q_ref, k_ref, v_ref = refs[:5]
    w_pad, columns = refs[-2:]
    vectors = refs[6] if fresh else None
    dense = 3 * PAIR * HEAD
    j = pl.program_id(0)
    rows = k_ref.shape[0]

    @pl.when(j == 0)
    def _():
        w_pad[...] = jnp.zeros_like(w_pad)
        spot = 2
        for w_ref in w_refs:
            count, deep = w_ref.shape[:2]
            for b in range(count):
                at = pl.ds(pl.multiple_of(info[spot], 16), deep)
                spot += 1
                for i in range(3 * PAIR):
                    w_pad[at, i * WIDE : i * WIDE + HEAD] = w_ref[b, :, part(i)]
                if fresh:
                    columns[at, 0:2] = w_ref[b, :, dense : dense + 2].astype(f32)
        if fresh:
            vectors[...] = columns[...].T[:8]

    if fresh:
        n_ref = refs[5]
        for x_ref, (low, high) in zip(x_refs, spans):

            @pl.when((j >= low) & (j < high))
            def _():
                unit, _ = normalise(x_ref[...].reshape(rows, -1).astype(f32))
                n_ref[...] = (unit * vectors[0:1, :] + vectors[1:2, :]).astype(bf16)

        normed = n_ref[...]
    else:
        normed = x_refs[0][...]

    @pl.when(j * rows < own)
    def _():
        for h in range(PAIR):
            row = tail(qb_ref[:, part(h)] * (SCALE * LOG2E), 1.0)
            product = nn(normed, w_pad[:, wide(h)])
            q_ref[:, wide(h)] = (product * (SCALE * LOG2E) + row).astype(bf16)

    start = info[2 + sum(weights) + j]
    where = lax.broadcasted_iota(jnp.int32, (rows, 1), 0) + start
    bias = jnp.where((start < 0) | (where < info[1]), 0.0, MASKED)
    lane = lax.broadcasted_iota(jnp.int32, (rows, WIDE), 1)
    mark = jnp.where(lane == HEAD, bias, 0.0)
    for h in range(PAIR):
        k_ref[:, wide(h)] = (nn(normed, w_pad[:, wide(PAIR + h)]) + mark).astype(bf16)
        row = tail(vb_ref[:, part(h)], 1.0)
        v_ref[:, wide(h)] = (nn(normed, w_pad[:, wide(2 * PAIR + h)]) + row).astype(bf16)


def span_spec(shape, rows, low, count, grouped):
    inside = lambda j: jnp.clip(j - low, 0, count - 1)
    if grouped:
        return pl.BlockSpec((1, rows, shape[-1]), lambda j, info: (info[0], inside(j), 0))
    return pl.BlockSpec((rows, shape[-1]), lambda j, info: (inside(j), 0))


def project(fresh, info, sources, weights, q_bias, v_bias, rows, own, total):
    width = sources[0].shape[-1]
    last = own // rows - 1
    cols = PAIR * WIDE
    spans, specs = [], []
    for x in sources:
        low = spans[-1][1] if spans else 0
        count = x.shape[-2] // rows
        spans.append((low, low + count))
        specs.append(span_spec(x.shape, rows, low, count, x.ndim == 3))
    shapes = [(own, cols), (total, cols), (total, cols)] + ([(total, width)] if fresh else [])
    outs = [pl.BlockSpec((rows, cols), lambda j, info: (jnp.minimum(j, last), 0))]
    outs += [pl.BlockSpec((rows, s[1]), lambda j, info: (j, 0)) for s in shapes[1:]]
    outs += [whole((8, width))] if fresh else []
    flat = [q_bias, v_bias]
    return pl.pallas_call(
        functools.partial(project_kernel, fresh, own, spans, [w.shape[0] for w in weights]),
        grid_spec=pltpu.PrefetchScalarGridSpec(
            num_scalar_prefetch=1,
            grid=(total // rows,),
            in_specs=specs + [once(w.shape) for w in weights] + [whole(a.shape) for a in flat],
            out_specs=outs,
            scratch_shapes=[
                pltpu.VMEM((width, 3 * PAIR * WIDE), bf16),
                pltpu.VMEM((width, 128), f32),
            ],
        ),
        out_shape=[jax.ShapeDtypeStruct(s, bf16) for s in shapes]
        + ([jax.ShapeDtypeStruct((8, width), f32)] if fresh else []),
        compiler_params=params(),
        cost_estimate=cost(14 * total * width * cols, 8 * total * width),
    )(info, *sources, *weights, *flat)


def causal(count):
    row = lax.broadcasted_iota(jnp.int32, (count, count), 0)
    return row >= lax.broadcasted_iota(jnp.int32, (count, count), 1)


def attend_kernel(later, cont, q_ref, k_ref, v_ref, o_ref, log_ref):
    j = pl.program_id(0)
    rows = q_ref.shape[0]
    lanes = lax.broadcasted_iota(jnp.int32, (rows, 128), 1)

    def run(is_later):
        logs = jnp.zeros((rows, 128), f32)
        outs = []
        for h in range(PAIR):
            q = q_ref[:, wide(h)]
            scores = nt(q, k_ref[later:, wide(h)])
            top = jnp.max(scores, axis=1, keepdims=True)
            if is_later:
                near = []
                for i in range(rows // cont):
                    at = pl.ds(pl.multiple_of(j * rows + i * cont, cont), cont)
                    block = nt(q[i * cont : (i + 1) * cont], k_ref[at, wide(h)])
                    near.append(jnp.where(causal(cont), block, MASKED))
                near = jnp.concatenate(near, axis=0)
                top = jnp.maximum(top, jnp.max(near, axis=1, keepdims=True))
            out = nn(jnp.exp2(scores - top).astype(bf16), v_ref[later:, wide(h)])
            if is_later:
                near = jnp.exp2(near - top).astype(bf16)
                extra = []
                for i in range(rows // cont):
                    at = pl.ds(pl.multiple_of(j * rows + i * cont, cont), cont)
                    extra.append(nn(near[i * cont : (i + 1) * cont], v_ref[at, wide(h)]))
                out = out + jnp.concatenate(extra, axis=0)
            total = out[:, HEAD : HEAD + 1]
            outs.append(out[:, :HEAD] * (1.0 / total))
            logs = jnp.where(lanes == h, top + jnp.log2(total), logs)
        o_ref[...] = jnp.concatenate(outs, axis=1).astype(bf16)
        log_ref[...] = logs

    pl.when(j * rows < later)(lambda: run(True))
    pl.when(j * rows >= later)(lambda: run(False))


def attend(q, k, v, later, cont):
    own, cols = q.shape
    rows = min(512, later, own - later)
    block = lambda n: pl.BlockSpec((rows, n), lambda j: (j, 0))
    return pl.pallas_call(
        functools.partial(attend_kernel, later, cont),
        grid=(own // rows,),
        in_specs=[block(cols), whole(k.shape), whole(v.shape)],
        out_specs=[block(PAIR * HEAD), block(128)],
        out_shape=[
            jax.ShapeDtypeStruct((own, PAIR * HEAD), bf16),
            jax.ShapeDtypeStruct((own, 128), f32),
        ],
        compiler_params=params(),
        cost_estimate=cost(8 * own * k.shape[0] * cols // 2, 8 * own * cols),
    )(q, k, v)


def attend_back_kernel(
    later, cont, first, q_ref, k_ref, v_ref, o_ref, log_ref, g_ref, dq_ref, dk_ref, dv_ref, dk, dv
):
    j = pl.program_id(0)
    rows = q_ref.shape[0]

    @pl.when(j == 0)
    def _():
        dk[...] = jnp.zeros_like(dk)
        dv[...] = jnp.zeros_like(dv)

    def run(is_later):
        outs = []
        for h in range(PAIR):
            q = q_ref[:, wide(h)]
            log = log_ref[:, h : h + 1]
            g = g_ref[:, part(first + h)].astype(f32)
            inner = jnp.sum(g * o_ref[:, part(h)].astype(f32), axis=1, keepdims=True)
            g = tail(g, 0.0).astype(bf16)
            k = k_ref[later:, wide(h)]
            probs = jnp.exp2(nt(q, k) - log)
            drift = (probs * (nt(g, v_ref[later:, wide(h)]) - inner)).astype(bf16)
            dv[later:, wide(h)] += tn(probs.astype(bf16), g)
            dk[later:, wide(h)] += tn(drift, q)
            dq = nn(drift, k)
            if is_later:
                extra = []
                for i in range(rows // cont):
                    at = pl.ds(pl.multiple_of(j * rows + i * cont, cont), cont)
                    mine = slice(i * cont, (i + 1) * cont)
                    k = k_ref[at, wide(h)]
                    probs = jnp.where(causal(cont), jnp.exp2(nt(q[mine], k) - log[mine]), 0.0)
                    drift = nt(g[mine], v_ref[at, wide(h)]) - inner[mine]
                    drift = (probs * drift).astype(bf16)
                    dv[at, wide(h)] += tn(probs.astype(bf16), g[mine])
                    dk[at, wide(h)] += tn(drift, q[mine])
                    extra.append(nn(drift, k))
                dq = dq + jnp.concatenate(extra, axis=0)
            outs.append(dq[:, :HEAD] * SCALE)
        dq_ref[...] = jnp.concatenate(outs, axis=1).astype(bf16)

    pl.when(j * rows < later)(lambda: run(True))
    pl.when(j * rows >= later)(lambda: run(False))

    @pl.when(j == pl.num_programs(0) - 1)
    def _():
        outs = [dk[:, h * WIDE : h * WIDE + HEAD] * (1.0 / LOG2E) for h in range(PAIR)]
        dk_ref[...] = jnp.concatenate(outs, axis=1).astype(bf16)
        outs = [dv[:, h * WIDE : h * WIDE + HEAD] for h in range(PAIR)]
        dv_ref[...] = jnp.concatenate(outs, axis=1).astype(bf16)


def attend_back(q, k, v, out, logs, grad, first, later, cont):
    own, cols = q.shape
    total = k.shape[0]
    dense = PAIR * HEAD
    rows = min(512, later, own - later)
    block = lambda n: pl.BlockSpec((rows, n), lambda j: (j, 0))
    return pl.pallas_call(
        functools.partial(attend_back_kernel, later, cont, first),
        grid=(own // rows,),
        in_specs=[block(cols), whole(k.shape), whole(v.shape), block(dense), block(128), block(grad.shape[1])],
        out_specs=[block(dense), whole((total, dense)), whole((total, dense))],
        out_shape=[
            jax.ShapeDtypeStruct((own, dense), bf16),
            jax.ShapeDtypeStruct((total, dense), bf16),
            jax.ShapeDtypeStruct((total, dense), bf16),
        ],
        scratch_shapes=[pltpu.VMEM((total, cols), f32)] * 2,
        compiler_params=params(),
        cost_estimate=cost(1000, 1000),
    )(q, k, v, out, logs, grad)


WEIGHTS = 3


def middle_kernel(counts, info, tok_ref, go_ref, valid_ref, *refs):
    a_refs, refs = refs[:4], refs[4:]
    w_refs, refs = refs[: 4 * len(counts)], refs[4 * len(counts) :]
    ub_ref, y_ref, gm_ref, near_ref, far_ref, sum_ref, keep_ref, send_ref = refs[:8]
    w, acc, att, columns, vectors, sem = refs[8:]
    j = pl.program_id(0)
    cols = a_refs[0].shape[1]
    half = 2 * cols

    @pl.when(j == 0)
    def _():
        acc[...] = jnp.zeros_like(acc)
        sum_ref[...] = jnp.zeros_like(sum_ref)
        for r in range(4):
            spot = 1
            for w_ref in w_refs[r * len(counts) : (r + 1) * len(counts)]:
                count, deep = w_ref.shape[:2]
                for b in range(count):
                    at = pl.ds(pl.multiple_of(info[spot], 16), deep)
                    spot += 1
                    for m in range(WEIGHTS):
                        w[m, at, r * cols : (r + 1) * cols] = w_ref[
                            b, :, m * cols : (m + 1) * cols
                        ]
                    if r == 0:
                        columns[at, 0:4] = w_ref[b, :, 3 * cols : 3 * cols + 4].astype(f32)
        vectors[...] = columns[...].T[:8]

    for r in range(4):
        att[:, r * cols : (r + 1) * cols] = a_refs[r][...]
    attended = att[...]
    mixed = tok_ref[...].astype(f32) + nt(attended, w[0]) + vectors[2:3, :]
    unit, inverse = normalise(mixed)
    gain = vectors[0:1, :]
    normed = (unit * gain + vectors[1:2, :]).astype(bf16)
    upper = nn(normed, w[1]) + ub_ref[...]
    cumulative = 0.5 + 0.5 * lax.erf(upper * (0.5**0.5))
    active = (upper * cumulative).astype(bf16)
    output = mixed + nt(active, w[2]) + vectors[3:4, :]
    y_ref[...] = output.astype(bf16)
    sum_ref[0:1, :] += jnp.sum(output * output * valid_ref[...], axis=0, keepdims=True)

    go = go_ref[...]
    acc[2] += tn(go, active)
    density = jnp.exp(-0.5 * upper * upper) * (1.0 / math.sqrt(2.0 * math.pi))
    grad_upper = nn(go, w[2]) * (cumulative + upper * density)
    sum_ref[5:6, :] += jnp.sum(grad_upper, axis=0, keepdims=True)
    low = grad_upper.astype(bf16)
    acc[1] += tn(normed, low)
    grad_mid = nt(low, w[1])
    sum_ref[2:3, :] += jnp.sum(grad_mid * unit, axis=0, keepdims=True)
    sum_ref[3:4, :] += jnp.sum(grad_mid, axis=0, keepdims=True)
    grad_out = go.astype(f32)
    sum_ref[1:2, :] += jnp.sum(grad_out, axis=0, keepdims=True)
    grad_mixed = grad_out + norm_back(grad_mid, unit, inverse, gain)
    sum_ref[4:5, :] += jnp.sum(grad_mixed, axis=0, keepdims=True)
    gm_ref[...] = grad_mixed
    low = grad_mixed.astype(bf16)
    acc[0] += tn(low, attended)
    grad_attended = nn(low, w[0]).astype(bf16)
    near_ref[...] = grad_attended[:, :half]
    far_ref[...] = grad_attended[:, half:]

    @pl.when(j == pl.num_programs(0) - 1)
    def _():
        copies = []
        for m in range(WEIGHTS):
            w[m] = acc[m].astype(bf16)
            for i, out_ref in enumerate((keep_ref, send_ref)):
                source = w.at[m, :, pl.ds(i * half, half)]
                target = out_ref.at[:, pl.ds(m * half, half)]
                copies.append(pltpu.make_async_copy(source, target, sem.at[2 * m + i]))
                copies[-1].start()
        for copy in copies:
            copy.wait()


def middle(info, tokens, grad, valid, mine, theirs, weights, up_bias, rows, half):
    count, width = tokens.shape
    cols = mine[0].shape[1]
    per = half // rows
    block = lambda n: pl.BlockSpec((rows, n), lambda j, info: (j, 0))
    own = pl.BlockSpec(
        (rows, cols), lambda j, info: ((2 * (j // per) + info[0]) * per + j % per, 0)
    )
    flat = [w for group in weights for w in group]
    hbm = pl.BlockSpec(memory_space=pl.ANY)
    shape = jax.ShapeDtypeStruct
    return pl.pallas_call(
        functools.partial(middle_kernel, [w.shape[0] for w in weights[0]]),
        grid_spec=pltpu.PrefetchScalarGridSpec(
            num_scalar_prefetch=1,
            grid=(count // rows,),
            in_specs=[block(width), block(width), block(1), own, own, block(cols), block(cols)]
            + [once(w.shape) for w in flat]
            + [whole(up_bias.shape)],
            out_specs=[block(width), block(width), block(2 * cols), block(2 * cols)]
            + [whole((8, width)), hbm, hbm],
            scratch_shapes=[
                pltpu.VMEM((WEIGHTS, width, 4 * cols), bf16),
                pltpu.VMEM((WEIGHTS, width, 4 * cols), f32),
                pltpu.VMEM((rows, 4 * cols), bf16),
                pltpu.VMEM((width, 128), f32),
                pltpu.VMEM((8, width), f32),
                pltpu.SemaphoreType.DMA((2 * WEIGHTS,)),
            ],
        ),
        out_shape=[
            shape((count, width), bf16),
            shape((count, width), f32),
            shape((count, 2 * cols), bf16),
            shape((count, 2 * cols), bf16),
            shape((8, width), f32),
            shape((width, 2 * WEIGHTS * cols), bf16),
            shape((width, 2 * WEIGHTS * cols), bf16),
        ],
        compiler_params=params(),
        cost_estimate=cost(148 * count * width * cols, 30 * count * width),
    )(info, tokens, grad, valid, *mine, *theirs, *flat, up_bias)


BEYOND, THEIRS, MINE = 0, 1, 2


def project_back_kernel(sums, spans, more, adding, counts, info, *refs):
    x_ref, dq_ref, dk_ref, dv_ref = refs[:4]
    refs = refs[4:]
    w_refs, refs = refs[: len(counts)], refs[len(counts) :]
    prev_refs, refs = refs[:more], refs[more:]
    other, refs = refs[:adding], refs[adding:]
    outs, refs = refs[: len(spans)], refs[len(spans) :]
    d = refs[-1]
    j = pl.program_id(0)
    cols = dq_ref.shape[1]
    if spans:
        w = refs[-2]

        @pl.when(j == 0)
        def _():
            spot = 1
            for w_ref in w_refs:
                count, deep = w_ref.shape[:2]
                for b in range(count):
                    at = pl.ds(pl.multiple_of(info[spot], 16), deep)
                    w[at, : 3 * cols] = w_ref[b, :, : 3 * cols]
                    spot += 1
            w[:, 3 * cols :] = jnp.zeros_like(w[:, 3 * cols :])

    @pl.when(j == 0)
    def _():
        d[:, 3 * cols :] = jnp.zeros_like(d[:, 3 * cols :])

    asked = info[1 + sum(counts)]

    @pl.when(j < asked)
    def _():
        d[:, :cols] = jnp.zeros_like(dq_ref)

    @pl.when(j >= asked)
    def _():
        d[:, :cols] = dq_ref[...]

    d[:, cols : 2 * cols] = dk_ref[...]
    d[:, 2 * cols : 3 * cols] = dv_ref[...]
    all_d = d[...]
    if sums:
        dw_refs, (sum_ref, acc) = refs[:sums], refs[sums : sums + 2]

        @pl.when(j == 0)
        def _():
            acc[...] = jnp.zeros_like(acc)
            sum_ref[...] = jnp.zeros_like(sum_ref)

        acc[...] += tn(x_ref[...], all_d)
        sum_ref[0:1, :] += jnp.sum(all_d.astype(f32), axis=0, keepdims=True)

        @pl.when(j == pl.num_programs(0) - 1)
        def _():
            at = 0
            for piece in other:
                acc[:, at : at + piece.shape[1]] += piece[...].astype(f32)
                at += piece.shape[1]
            at = 0
            for dw_ref in dw_refs:
                dw_ref[...] = acc[:, at : at + dw_ref.shape[1]].astype(bf16)
                at += dw_ref.shape[1]

    if spans:
        grad = nt(all_d, w[...])
        for i, (low, high) in enumerate(spans):

            @pl.when((j >= low) & (j < high))
            def _():
                if more:
                    outs[i][...] = (grad + prev_refs[i][...].astype(f32)).astype(bf16)
                else:
                    outs[i][...] = grad.astype(bf16)


def tiled(count):
    return -(-count // 256) * 256


def project_back(
    sums, wanted, c, starts, x, dq, dk, dv, weights, previous, rows, half, own, other=()
):
    total, width = x.shape
    cols = dq.shape[1]
    sizes = ((total - own) // rows, own // 2 // rows, own // 2 // rows)
    n_beyond = sizes[0] if BEYOND in wanted else 0
    n_half = sizes[1]
    per = half // rows
    steps = sum(sizes[i] for i in wanted)
    info = jnp.stack([jnp.asarray(v, jnp.int32) for v in (c, *starts, n_beyond)])

    def row(j, info):
        i = j - n_beyond
        share = (i >= n_half).astype(jnp.int32)
        i = i - share * n_half
        side = jnp.where(share == 1, info[0], 1 - info[0])
        inner = (2 * (i // per) + side) * per + i % per
        return jnp.where(j < n_beyond, own // rows + j, inner)

    def dq_row(j, info):
        return jnp.minimum(row(jnp.maximum(j, n_beyond), info), own // rows - 1)

    x_spec = pl.BlockSpec((rows, width), lambda j, info: (row(j, info), 0))
    d_spec = pl.BlockSpec((rows, cols), lambda j, info: (row(j, info), 0))
    q_spec = pl.BlockSpec((rows, cols), lambda j, info: (dq_row(j, info), 0))
    parts, spans, low = [], [], 0
    if previous is not None:
        for i in wanted:
            n = sizes[i]
            spans.append((low, low + n))
            parts.append(
                pl.BlockSpec(
                    (rows, width),
                    functools.partial(lambda a, b, j, info: (jnp.clip(j - a, 0, b - 1), 0), low, n),
                )
            )
            low += n
    shape = jax.ShapeDtypeStruct
    out_specs = list(parts)
    out_shape = [shape((sizes[i] * rows, width), bf16) for i in wanted[: len(parts)]]
    scratch = []
    lanes = tiled(3 * cols)
    if sums:
        out_specs += [whole((width, n)) for n in sums] + [whole((8, lanes))]
        out_shape += [shape((width, n), bf16) for n in sums] + [shape((8, lanes), f32)]
        scratch.append(pltpu.VMEM((width, lanes), f32))
    if parts:
        scratch.append(pltpu.VMEM((width, lanes), bf16))
    scratch.append(pltpu.VMEM((rows, lanes), bf16))
    return pl.pallas_call(
        functools.partial(
            project_back_kernel,
            len(sums),
            spans,
            len(previous or []),
            len(other),
            [w.shape[0] for w in weights],
        ),
        grid_spec=pltpu.PrefetchScalarGridSpec(
            num_scalar_prefetch=1,
            grid=(steps,),
            in_specs=[x_spec, q_spec, d_spec, d_spec]
            + [once(w.shape) for w in weights]
            + (parts if previous else [])
            + [once(o.shape) for o in other],
            out_specs=out_specs,
            scratch_shapes=scratch,
        ),
        out_shape=out_shape,
        compiler_params=params(),
        cost_estimate=cost(1000, 1000),
    )(info, x, dq, dk, dv, *weights, *(previous or []), *other)


def finish_kernel(n, gain_ref, tok_ref, mix_ref, *refs):
    shares, (low_ref, sum_ref) = refs[:n], refs[n:]

    @pl.when(pl.program_id(0) == 0)
    def _():
        sum_ref[...] = jnp.zeros_like(sum_ref)

    grad = shares[0][...].astype(f32)
    for share in shares[1:]:
        grad = grad + share[...].astype(f32)
    unit, inverse = normalise(tok_ref[...].astype(f32))
    back = norm_back(grad, unit, inverse, gain_ref[0:1, :])
    low_ref[...] = (mix_ref[...] + back).astype(bf16)
    sum_ref[0:1, :] += jnp.sum(grad * unit, axis=0, keepdims=True)
    sum_ref[1:2, :] += jnp.sum(grad, axis=0, keepdims=True)


def finish(kind, gain, tokens, mixed, shares, back, half):
    width = tokens.shape[1]
    rows = min(128, half)
    n = half // rows
    block = pl.BlockSpec((rows, width), lambda j: (kind * n + j, 0))
    plain = pl.BlockSpec((rows, width), lambda j: (j, 0))
    return pl.pallas_call(
        functools.partial(finish_kernel, len(shares) + len(back)),
        grid=(n,),
        in_specs=[whole(gain.shape), block, block] + [block] * len(shares) + [plain] * len(back),
        out_specs=[plain, whole((8, width))],
        out_shape=[
            jax.ShapeDtypeStruct((half, width), bf16),
            jax.ShapeDtypeStruct((8, width), f32),
        ],
        compiler_params=params(),
        cost_estimate=cost(1000, 1000),
    )(gain, tokens, mixed, *shares, *back)


def assemble_kernel(info, *refs):
    i = pl.program_id(0)
    for m in range(4):

        @pl.when(i == m)
        def _():
            refs[4][...] = refs[m][...].astype(refs[4].dtype)[None]


def assemble(info, pieces, kind, half, dtype):
    width = pieces[0].shape[1]
    rows = half
    n = half // rows

    def source(m, i, s):
        return kind * n + jnp.where(i < m, 0, jnp.where(i > m, n - 1, s))

    def target(i, s, info):
        return info[0] ^ (i // 2), (info[1] ^ (i % 2)) * n + s, 0

    return pl.pallas_call(
        assemble_kernel,
        grid_spec=pltpu.PrefetchScalarGridSpec(
            num_scalar_prefetch=1,
            grid=(4, n),
            in_specs=[
                pl.BlockSpec(
                    (rows, width), functools.partial(lambda m, i, s, info: (source(m, i, s), 0), m)
                )
                for m in range(4)
            ],
            out_specs=pl.BlockSpec((1, rows, width), target),
        ),
        out_shape=jax.ShapeDtypeStruct((2, 2 * half, width), dtype),
        compiler_params=params(2),
        cost_estimate=cost(1000, 1000),
    )(info, *pieces)


def swap(value, axis, bit):
    count = lax.axis_size(axis)
    return lax.ppermute(value, axis, [(i, i ^ bit) for i in range(count)])


def pick(array, index, axis=0):
    return lax.dynamic_index_in_dim(array, index, axis, keepdims=False)


def in_order(index, mine, theirs, axis=0):
    first = index == 0
    return jnp.stack(
        [jnp.where(first, mine, theirs), jnp.where(first, theirs, mine)], axis=axis
    )


def direct():
    return lax.axis_size(C) == 2 and lax.axis_size(S) == 4


def phase(*values):
    return lax.optimization_barrier(values)


def over_z(piece):
    return [swap(piece, S, i) for i in (1, 2, 3)]


def z_parts(rows, axis):
    z = lax.axis_index(S)
    low = rows.astype(bf16)
    return [pick(low, z ^ i, axis) for i in (1, 2, 3)], pick(rows, z, axis)


def z_sum(mine, parts):
    for piece in parts:
        mine = mine + piece.astype(f32)
    return mine


def z_moves(parts):
    return [swap(piece, S, i + 1) for i, piece in enumerate(parts)]


def x_parts(rows, axis):
    x = lax.axis_index(C)
    shape = rows.shape
    split = rows.reshape(*shape[:axis], 4, 2, shape[axis] // 8, *shape[axis + 1 :])
    return pick(split, 1 - x, axis + 1).astype(bf16), pick(split, x, axis + 1)


def sum_over(values, axis):
    count, bit = lax.axis_size(axis), 1
    while bit < count:
        values = values + swap(values, axis, bit)
        bit *= 2
    return values


def body(
    prompt_tokens,
    later_tokens,
    prompt_upstream,
    later_upstream,
    prompt_lengths,
    later_lengths,
    query_weight,
    key_weight,
    value_weight,
    out_weight,
    up_weight,
    down_weight,
    pre_gain,
    pre_shift,
    mid_gain,
    mid_shift,
    query_bias,
    value_bias,
    out_bias,
    up_bias,
    down_bias,
):
    groups, prompt_rows, width = prompt_tokens.shape
    count, cont = later_tokens.shape[1:3]
    later = count * cont
    own = later + prompt_rows
    contexts = lax.axis_size(C)
    total = later + prompt_rows * contexts
    cols = query_weight.shape[1]
    half = later // 2
    big = min(512, later)
    x = lax.axis_index(C)
    t = lax.axis_index(T)
    y, c = t // 2, t % 2
    turn = (t, t ^ 2, t ^ 1, t ^ 3)

    def share(array, side):
        rows = array.reshape(2, 2, half, array.shape[-1])
        return pick(rows, side, 1).reshape(2 * half, array.shape[-1])

    prompt = pick(prompt_tokens, y)
    qkv_piece = jnp.concatenate(
        [query_weight, key_weight, value_weight, pre_gain[:, None], pre_shift[:, None]], axis=1
    )
    oud_piece = jnp.concatenate(
        [out_weight.T, up_weight, down_weight.T]
        + [v[:, None] for v in (mid_gain, mid_shift, out_bias, down_bias)],
        axis=1,
    )
    length = pick(prompt_lengths, y)
    lengths = pick(later_lengths, y)
    follow = pick(later_tokens, y).reshape(later, width)
    row_tokens = share(jnp.concatenate([follow, prompt], axis=0), c)
    later_valid = jnp.arange(cont, dtype=jnp.int32)[None, :] < lengths[:, None]
    prompt_valid = x * prompt_rows + jnp.arange(prompt_rows, dtype=jnp.int32) < length
    valid = jnp.concatenate([later_valid.reshape(later), prompt_valid]).astype(f32)
    valid = share(valid[:, None], c)
    upstream = jnp.concatenate(
        [pick(later_upstream, y).reshape(later, width), pick(prompt_upstream, y)], axis=0
    )
    grad_low = (share(upstream, c).astype(f32) * valid).astype(bf16)

    biases = jnp.concatenate([query_bias, value_bias, up_bias])[None]
    if direct():
        z = lax.axis_index(S)
        deep = query_weight.shape[0]
        starts = [((z ^ i) * 2 + (x ^ k)) * deep for k in (0, 1) for i in range(4)]
        places = [(1 - x) * prompt_rows + side * half for side in (c, 1 - c)]
        tokens_piece = pick(prompt.reshape(2, half, width), c)
        tokens_piece, qkv_piece = phase(tokens_piece, qkv_piece)
        tokens_piece = swap(tokens_piece, C, 1)
        parts = over_z(qkv_piece)
        rows = jnp.pad(biases, ((0, 15), (0, qkv_piece.shape[1] - biases.shape[1])))
        far_piece = swap(jnp.concatenate([qkv_piece, rows]), T, 2)
        far_piece, tokens_piece, oud_piece, row_tokens, grad_low, valid, *parts = phase(
            far_piece, tokens_piece, oud_piece, row_tokens, grad_low, valid, *parts
        )
        far_biases = far_piece[deep : deep + 1, : biases.shape[1]]
        far_piece = far_piece[:deep]
        near = jnp.stack([qkv_piece, *parts])
        qkv_own = [near, swap(near, C, 1)]
        beyond = [tokens_piece, swap(tokens_piece, T, 1)]
        parts = [far_piece, *over_z(far_piece)]
        parts = phase(*qkv_own, *beyond, *parts, oud_piece)
        qkv_own, beyond, oud_piece = list(parts[:2]), list(parts[2:4]), parts[8]
        near = jnp.stack(parts[4:8])
        qkv_far = [near, swap(near, C, 1)]
        oud_parts = over_z(oud_piece)
    else:
        starts = [0]
        rolled = jnp.roll(lax.all_gather(prompt, C), -x, axis=0)[1:]
        beyond = [rolled.reshape(-1, width)]
        places = [((x + i) % contexts) * prompt_rows for i in range(1, contexts)]
        qkv_own = [lax.all_gather(qkv_piece, SC, axis=0, tiled=True)[None]]
        qkv_far = [swap(w, T, 2) for w in qkv_own]
        far_biases = swap(biases, T, 2)
    biases = jnp.concatenate([biases, far_biases]).astype(f32)

    def ints(*values):
        return jnp.stack([jnp.asarray(v, jnp.int32) for v in values])

    blocks = [-1] * (later // big)
    blocks += [x * prompt_rows + i * big for i in range(prompt_rows // big)]
    blocks += [p + i * big for p in places for i in range(max(half if direct() else prompt_rows, big) // big)]
    info = ints(y, length, *starts, *blocks)

    q0, k0, v0, normed_in, pre_vectors = project(
        True,
        info,
        [later_tokens.reshape(groups, later, width), prompt_tokens] + beyond,
        qkv_own,
        biases[0:1, :cols],
        biases[0:1, cols : 2 * cols],
        big,
        own,
        total,
    )
    if direct():
        q0, k0, v0, normed_in, *parts = phase(q0, k0, v0, normed_in, *qkv_far, *oud_parts)
        qkv_far = parts[:2]
        near = jnp.stack([oud_piece, *parts[2:]])
        oud_own = [near, swap(near, C, 1)]
        near = swap(near, T, 2)
    a0, log0 = attend(q0, k0, v0, later, cont)
    if direct():
        a0, near, *oud_own = phase(a0, near, *oud_own)
        oud_far = [near, swap(near, C, 1)]
    else:
        oud_own = [lax.all_gather(oud_piece, SC, axis=0, tiled=True)[None]]
        oud_far = [swap(w, T, 2) for w in oud_own]
    oud = [oud_own, oud_far] + [[swap(w, T, 1) for w in ws] for ws in (oud_own, oud_far)]
    r0 = swap(share(a0, 1 - c), T, 1)
    up_bias = biases[:, 2 * cols :]
    up_bias = jnp.concatenate([up_bias, swap(up_bias, T, 1)]).reshape(1, -1)
    q1, k1, v1 = project(
        False,
        info,
        [normed_in],
        qkv_far,
        biases[1:2, :cols],
        biases[1:2, cols : 2 * cols],
        big,
        own,
        total,
    )
    if direct():
        q1, k1, v1, oud[2][0], oud[2][1], oud[3][0], r0, up_bias = phase(
            q1, k1, v1, oud[2][0], oud[2][1], oud[3][0], r0, up_bias
        )
    a1, log1 = attend(q1, k1, v1, later, cont)
    if direct():
        a1, oud_far[1] = phase(a1, oud_far[1])
        oud[3][1] = swap(oud_far[1], T, 1)
    r1 = swap(share(a1, 1 - c), T, 1)

    output, grad_mixed, grad_near, grad_away, sums, oud_keep, oud_send = middle(
        ints(c, *starts),
        row_tokens,
        grad_low,
        valid,
        [a0, a1],
        [r0, r1],
        oud,
        up_bias,
        min(256, half),
        half,
    )

    where = ints(y, c)

    outputs = [output, swap(output, T, 1), swap(output, T, 2), None]

    received = swap(grad_away, T, 1)
    grad_heads = in_order(
        c, grad_near.reshape(2, half, -1), received.reshape(2, half, -1), 1
    ).reshape(own, -1)
    oud_send = swap(oud_send, T, 1)
    wide_part = min(1024, oud_send.shape[1])
    oud_pieces = [slice(0, wide_part), slice(wide_part, None)]
    oud_pieces = [oud_keep[:, p].astype(f32) + oud_send[:, p].astype(f32) for p in oud_pieces]
    if direct():
        away, kept = zip(*[x_parts(p, 0) for p in oud_pieces])
        grad_heads, *parts = phase(grad_heads, *away, *[k.astype(bf16) for k in kept])
        away, kept = parts[:2], parts[2:]
        away[0] = swap(away[0], C, 1)
    dq, dk, dv = attend_back(q1, k1, v1, a1, log1, grad_heads, PAIR, later, cont)
    if direct():
        dq, away[0], away[1] = phase(dq, away[0], away[1])
        away[1] = swap(away[1], C, 1)
        parts, first_sum = z_parts(kept[0].astype(f32) + away[0].astype(f32), 0)
        dq, first_sum, *parts = phase(dq, first_sum, *parts)
        first_parts = z_moves(parts)
    back_rows = min(512, half)
    everything = (BEYOND, THEIRS, MINE)
    lanes = tiled(3 * cols)
    far_widths = (3 * lanes // 4, lanes // 4)
    *shares, far, far_rest, sums1 = project_back(
        far_widths, everything, c, starts, normed_in, dq, dk, dv, qkv_far, [], back_rows, half, own
    )
    if direct():
        far, far_rest, grad_heads, outputs[1], outputs[2], away[1], first_sum, *parts = phase(
            far, far_rest, grad_heads, outputs[1], outputs[2], away[1], first_sum, *first_parts
        )
        first_sum = z_sum(first_sum, parts)
        parts, last_sum = z_parts(kept[1].astype(f32) + away[1].astype(f32), 0)
        first_sum, last_sum, grad_heads, far, *parts = phase(
            first_sum, last_sum, grad_heads, far, *parts
        )
        last_parts = z_moves(parts)
    far = swap(far, T, 2)
    outputs[3] = swap(outputs[2], T, 1)
    dq, dk, dv = attend_back(q0, k0, v0, a0, log0, grad_heads, 0, later, cont)
    def near_back(sums, wanted, dq, *rest):
        previous, other = rest[0], rest[1:]
        return project_back(
            sums,
            wanted,
            c,
            starts,
            normed_in,
            dq,
            dk,
            dv,
            qkv_own,
            previous,
            back_rows,
            half,
            own,
            other,
        )

    if direct():
        dq, dk, dv, outputs[3], far, far_rest, last_sum, *parts = phase(
            dq, dk, dv, outputs[3], far, far_rest, last_sum, *last_parts
        )
        oud_grad = jnp.concatenate([first_sum, z_sum(last_sum, parts)], axis=1).astype(bf16)
        far_rest = swap(far_rest, T, 2)
        their_share, my_share = near_back((), (THEIRS, MINE), dq, shares[1:])
        their_share, my_share, dq, far_rest = phase(their_share, my_share, dq, far_rest)
        their_share = swap(their_share, T, 1)
        (beyond_share,) = near_back((), (BEYOND,), dq, shares[:1])
        shares = [my_share, their_share]
        back = [beyond_share[:half], swap(beyond_share[half:], T, 1)]
        low, sums_later = finish(0, pre_vectors, row_tokens, grad_mixed, shares, [], half)
        low, dq, sums_later, *parts = phase(low, dq, sums_later, *shares, *back)
        shares = parts[:2]
        back = swap((parts[2].astype(f32) + parts[3].astype(f32)).astype(bf16), C, 1)
        pieces = [low, None, swap(low, T, 2), None]
        *near, sums0 = near_back((lanes // 2,) * 2, everything, dq, None, far, far_rest)
        near = [n.reshape(4, 2 * deep, lanes // 2) for n in near]
        parts = [pick(n, z ^ i) for n in near for i in (1, 2, 3)]
        near = [pick(n, z) for n in near]
        near[0], near[1], sums0, *parts = phase(*near, sums0, *parts)
        early, parts = z_moves(parts[:3]), parts[3:]
        back, pieces[2] = phase(back, pieces[2])
        pieces[3] = swap(pieces[2], T, 1)
        low, sums_prompt = finish(1, pre_vectors, row_tokens, grad_mixed, shares, [back], half)
    else:
        beyond_share, their_share, my_share, near, sums0 = near_back(
            (lanes,), everything, dq, shares, far, swap(far_rest, T, 2)
        )
        shares = [my_share, swap(their_share, T, 1)]
        back = beyond_share.astype(f32) + swap(beyond_share, T, 1).astype(f32)
        back = back.reshape(contexts - 1, prompt_rows, width)
        back = jnp.concatenate([jnp.zeros_like(back[:1]), back], axis=0)
        back = jnp.roll(back, x, axis=0).astype(bf16)
        back = lax.psum_scatter(back, C, scatter_dimension=0, tiled=True)
        back = pick(back.reshape(2, half, width), c)
        low, sums_later = finish(0, pre_vectors, row_tokens, grad_mixed, shares, [], half)
        pieces = [low, swap(low, T, 1), swap(low, T, 2), None]
        low, sums_prompt = finish(1, pre_vectors, row_tokens, grad_mixed, shares, [back], half)
        oud_grad = jnp.concatenate([p.astype(bf16) for p in oud_pieces], axis=1)
        qkv_grad, oud_grad = [
            lax.psum_scatter(g, SC, scatter_dimension=0, tiled=True) for g in (near, oud_grad)
        ]
        qkv_grad = qkv_grad.astype(f32)

    def placed(*pieces):
        block = lax.broadcasted_iota(jnp.int32, (lax.axis_size(T), cols), 0)
        return sum(jnp.where(block == i, v[None], 0.0) for i, v in zip(turn, pieces)).reshape(-1)

    row = lax.broadcasted_iota(jnp.int32, (8, width), 0)
    lane = lax.broadcasted_iota(jnp.int32, (8, width), 1)
    group = lax.axis_index(S) * groups + y
    every = lax.axis_size(S) * groups
    scalars = jnp.where(lane == group, jnp.sum(sums[0]), 0.0)
    scalars = jnp.where(lane == every + group, jnp.sum(valid), scalars)
    up_sums = placed(*sums[5].reshape(4, cols))
    sums = jnp.where(row == 6, scalars, jnp.where(row == 7, up_sums[None], sums))
    q_sums = placed(sums0[0, :cols], sums1[0, :cols])
    v_sums = placed(sums0[0, 2 * cols : 3 * cols], sums1[0, 2 * cols : 3 * cols])
    more = jnp.where(row == 2, q_sums[None], jnp.where(row == 3, v_sums[None], sums_later))
    if direct():
        low, sums_prompt, sums, more, pieces[3], *rest = phase(
            low, sums_prompt, sums, more, pieces[3], *early, *parts
        )
        near[0], parts = z_sum(near[0].astype(f32), rest[:3]), z_moves(rest[3:])
    sums = jnp.concatenate([sums, more + sums_prompt])
    last = [low, None, swap(low, T, 2), None]
    pieces[1] = swap(pieces[0], T, 1)
    if not direct():
        pieces[3] = swap(pieces[2], T, 1)
    later_grad = assemble(where, pieces, 0, half, f32)
    later_output = assemble(where, outputs, 0, half, bf16)
    prompt_output = assemble(where, outputs, 1, half, bf16)
    if direct():
        later_grad, later_output, prompt_output, near[0], near[1], sums, last[2], *parts = phase(
            later_grad, later_output, prompt_output, *near, sums, last[2], *parts
        )
        near[1] = z_sum(near[1].astype(f32), parts)
        split = jnp.concatenate(near, axis=1).reshape(2, deep, lanes)
        away = swap(pick(split, 1 - x).astype(bf16), C, 1)
        qkv_grad = pick(split, x) + away.astype(f32)
    last[1] = swap(last[0], T, 1)
    last[3] = swap(last[2], T, 1)
    sums = sum_over(sum_over(sum_over(sums, C), S), T)
    squares = lax.dynamic_slice(sums[6], (lax.axis_index(S) * groups,), (groups,))
    counted = lax.dynamic_slice(sums[6], (every + lax.axis_index(S) * groups,), (groups,))
    magnitude = jnp.sqrt(squares / (counted * width))
    oud_grad = oud_grad.reshape(-1, WEIGHTS, 2, cols)
    oud_grad = oud_grad[:, :, 0].astype(f32) + swap(oud_grad[:, :, 1], T, 2).astype(f32)
    prompt_grad = assemble(where, last, 0, half, f32)
    n = width // (lax.axis_size(S) * contexts)
    place = lax.axis_index(S) * contexts + x

    def own_vector(row):
        return lax.dynamic_slice(row, (place * n,), (n,))

    def own_heads(row):
        return lax.dynamic_slice(row, (t * cols,), (cols,))

    shaped = (groups, count, cont, width)
    return (
        prompt_output,
        later_output.reshape(shaped),
        prompt_grad,
        later_grad.reshape(shaped),
        qkv_grad[:, :cols],
        qkv_grad[:, cols : 2 * cols],
        qkv_grad[:, 2 * cols : 3 * cols],
        oud_grad[:, 0].T,
        oud_grad[:, 1],
        oud_grad[:, 2].T,
        own_vector(sums[8]),
        own_vector(sums[9]),
        own_vector(sums[2]),
        own_vector(sums[3]),
        own_heads(sums[10]),
        own_heads(sums[11]),
        own_vector(sums[4]),
        own_heads(sums[7]),
        own_vector(sums[1]),
        magnitude,
    )


def solution(mesh):
    rows, later, vector = P(S, C, None), P(S, C, None, None), P(SC)
    weight, turned, column = P(SC, T), P(T, SC), P(T)
    return jax.shard_map(
        body,
        mesh=mesh,
        in_specs=(rows, later, rows, later, P(S), P(S, C))
        + (weight, weight, weight, turned, weight, turned)
        + (vector,) * 4
        + (column, column, vector, column, vector),
        out_specs=(rows, later, rows, later)
        + (weight, weight, weight, turned, weight, turned)
        + (vector,) * 4
        + (column, column, vector, column, vector, P(S)),
        check_vma=False,
    )
```

time: 802 us -> 594 us (0.74)
  Pallas kernels: 159 us -> 330 us
  blocking collectives: 130 us -> 0 us
  matrix products: 109 us -> 0 us
  local copies, waits for them, and re-layouts: 155 us -> 58.7 us
  other arithmetic: 114 us -> 37 us
  starting transfers between devices: 18.2 us -> 70.8 us
  between operations: 15.4 us -> 1.91 us
    pallas_call x4 -> x15, Pallas kernels: 118 us -> 289 us  [the longest x2 77.6 us: attend_back(): pl.pallas_call(functools.partial(attend_back_kernel, later, cont, first),...]
    dot_general x19 -> x0, matrix products: 109 us -> none  [the longest x9 47.8 us: tn(): lax.dot_general(a, b, (((0,), (0,)), ((), ())), preferred_element_type=f32)]
    psum x2 -> x0, blocking collectives: 80.6 us -> none  [the longest x1 41.9 us: body(): sums = lax.psum(sums, ALL)]
    ppermute x23 -> x61, starting transfers between devices: 18 us -> 70.8 us  [swap(): return lax.ppermute(value, axis, [(i, i ^ bit) for i in range(count)])]
    all_gather x2 -> x0, blocking collectives: 49.5 us -> none  [the longest x1 44.3 us: body(): vectors = lax.all_gather(vectors, SC, axis=1, tiled=True).astype(f32)]
    slice x32 -> x9, local copies, waits for them, and re-layouts: 45.9 us -> 8.17 us  [the longest x1 2.93 us: body(): back = [beyond_share[:half], swap(beyond_share[half:], T, 1)]]
    reduce_sum x11 -> x2, other arithmetic: 20.2 us -> 1.22 us  [the longest x1 0.61 us: body(): scalars = jnp.where(lane == every + group, jnp.sum(valid), scalars)]
    unnamed x151 -> x102, local copies, waits for them, and re-layouts: 25.6 us -> 7.4 us
  transfers between devices with their start and end apart: 27 -> 61, of which waited for: 8 -> 18; matrix products, arithmetic and copies ran while one was open for 37% -> 14% of each run, Pallas kernels for 20% -> 46%
where the time goes in v1:
time: 594 us; the launch traced here: 589 us
  Pallas kernels  330 us (56%)
  waiting for transfers between devices  90.3 us (15%)
  starting transfers between devices  70.8 us (12%)
  local copies, waits for them, and re-layouts  58.7 us (10%)
  other arithmetic  37 us (6%)
    ppermute x61, waiting for transfers between devices, swap(): return lax.ppermute(value, axis, [(i, i ^ bit) for i in range(count)])  90.3 us
    pallas_call x2, Pallas kernels, attend_back(): pl.pallas_call(functools.partial(attend_back_kernel, later, cont, first),...  77.6 us
    pallas_call x4, Pallas kernels, project_back(): pl.pallas_call(functools.partial(project_back_kernel, len(sums), spans, l...  75 us
    ppermute x61, starting transfers between devices, swap(): return lax.ppermute(value, axis, [(i, i ^ bit) for i in range(count)])  70.8 us
    pallas_call x1, Pallas kernels, middle(): pl.pallas_call(functools.partial(middle_kernel, [w.shape[0] for w in weig...  53.2 us
    pallas_call x2, Pallas kernels, project(): pl.pallas_call(functools.partial(project_kernel, fresh, own, spans, [w.sh...  44 us
    pallas_call x2, Pallas kernels, attend(): pl.pallas_call(functools.partial(attend_kernel, later, cont), grid=(own /...  41.2 us
    pallas_call x4, Pallas kernels, assemble(): pl.pallas_call(assemble_kernel, grid_spec=pltpu.PrefetchScalarGridSpec(nu...  26.8 us
  transfers between devices with their start and end apart: 61, of which 18 were waited for; matrix products, arithmetic and copies ran while one was open for 14% of the time, Pallas kernels for 46%

profile of v1, /device:TPU:0, one launch (start us, length us, event | category | flops | bytes accessed | tf_op | source)
XLA Modules:
  0.0 588.5 jit_solution(2031860198606530437)
XLA Ops:
  52.5 9.5 %collective-permute-done.7 = bf16[160,962]{1,0:T(8,128)(2,1)} collective-permute-done((bf16[160,962]{1,0:T(8,128)(2,1)S(1)}, bf16[160,962]{1,0:T(8,128)(2,1)}, u32[]{:S(2)}, u32[]{:S(2)}) %collective-permute-start.7) | collective-permute-done | bytes 307872 | tf_op jit(solution)/shard_map/ppermute | solution.py:676
  62.0 10.3 %collective-permute-done.8 = bf16[160,962]{1,0:T(8,128)(2,1)} collective-permute-done((bf16[160,962]{1,0:T(8,128)(2,1)S(1)}, bf16[160,962]{1,0:T(8,128)(2,1)}, u32[]{:S(2)}, u32[]{:S(2)}) %collective-permute-start.8) | collective-permute-done | bytes 307872 | tf_op jit(solution)/shard_map/ppermute | solution.py:676
  83.8 25.9 %shard_map.356 = (bf16[2048,512]{1,0:T(8,128)(2,1)}, bf16[3072,512]{1,0:T(8,128)(2,1)}, bf16[3072,512]{1,0:T(8,128)(2,1)}, bf16[3072,1280]{1,0:T(8,128)(2,1)}, f32[8,1280]{1,0:T(8,128)}) custom-call(s32[16]{0:T(128)} %stack.85.info, bf16[2,1024,1280]{2,1,0:T(8,128)(2,1)} %bitcast.174, bf16[2,1024,1280]{2,1,0:T(8,128)(2,1)} %refs_1_.1, ...), custom_call_target="tpu_custom_call" | custom-call | flops 28185722880 | bytes 31457280 | tf_op jit(solution)/shard_map/pallas_call | solution.py:163
  118.3 20.3 %shard_map.357 = (bf16[2048,320]{1,0:T(8,128)(2,1)}, f32[2048,128]{1,0:T(8,128)}) custom-call(bf16[2048,512]{1,0:T(8,128)(2,1)} %get-tuple-element.211.q_ref, bf16[3072,512]{1,0:T(8,128)(2,1)} %get-tuple-element.212.k_ref, bf16[3072,512]{1,0:T(8,128)(2,1)} %get-tuple-element.213.v_ref), custom_call_target="tpu_custom_call" | custom-call | flops 12884901888 | bytes 8388608 | tf_op jit(solution)/shard_map/pallas_call | solution.py:229
  148.4 18.1 %shard_map.358 = (bf16[2048,512]{1,0:T(8,128)(2,1)}, bf16[3072,512]{1,0:T(8,128)(2,1)}, bf16[3072,512]{1,0:T(8,128)(2,1)}) custom-call(s32[16]{0:T(128)} %stack.85.info, bf16[3072,1280]{1,0:T(8,128)(2,1)} %get-tuple-element.219.refs_0_, bf16[4,160,962]{2,1,0:T(8,128)(2,1)} %copy-done.6, bf16[4,160,962]{2,1,0:T(8,128)(2,1)} %copy-done.9, ...), custom_call_target="tpu_custom_call" | custom-call | flops 28185722880 | bytes 31457280 | tf_op jit(solution)/shard_map/pallas_call | solution.py:163
  166.5 20.9 %shard_map.359 = (bf16[2048,320]{1,0:T(8,128)(2,1)}, f32[2048,128]{1,0:T(8,128)}) custom-call(bf16[2048,512]{1,0:T(8,128)(2,1)} %get-tuple-element.228.q_ref, bf16[3072,512]{1,0:T(8,128)(2,1)} %get-tuple-element.229.k_ref, bf16[3072,512]{1,0:T(8,128)(2,1)} %get-tuple-element.230.v_ref), custom_call_target="tpu_custom_call" | custom-call | flops 12884901888 | bytes 8388608 | tf_op jit(solution)/shard_map/pallas_call | solution.py:229
  193.6 53.2 %shard_map.360 = (bf16[1024,1280]{1,0:T(8,128)(2,1)}, f32[1024,1280]{1,0:T(8,128)}, bf16[1024,640]{1,0:T(8,128)(2,1)}, bf16[1024,640]{1,0:T(8,128)(2,1)}, f32[8,...) custom-call(s32[9]{0:T(128)} %stack.177.info, bf16[1024,1280]{1,0:T(8,128)(2,1)} %bitcast.149, ...), custom_call_target="tpu_custom_call" | custom-call | flops 62075699200 | bytes 39321600 | tf_op jit(solution)/shard_map/pallas_call | solution.py:408
  248.1 12.9 %collective-permute-done.24 = bf16[1024,640]{1,0:T(8,128)(2,1)} collective-permute-done((bf16[1024,640]{1,0:T(8,128)(2,1)}, bf16[1024,640]{1,0:T(8,128)(2,1)}, u32[]{:S(2)}, u32[]{:S(2)}) %collective-permute-start.24) | collective-permute-done | bytes 1310752 | tf_op jit(solution)/shard_map/ppermute | solution.py:676
  275.0 38.8 %shard_map.361 = (bf16[2048,320]{1,0:T(8,128)(2,1)}, bf16[3072,320]{1,0:T(8,128)(2,1)}, bf16[3072,320]{1,0:T(8,128)(2,1)}) custom-call(bf16[2048,512]{1,0:T(8,128)(2,1)} %get-tuple-element.228.q_ref, bf16[3072,512]{1,0:T(8,128)(2,1)} %get-tuple-element.229.k_ref, bf16[3072,512]{1,0:T(8,128)(2,1)} %get-tuple-element.230.v_ref, ...), custom_call_target="tpu_custom_call" | custom-call | flops 1000 | bytes 1000 | tf_op jit(solution)/shard_map/pallas_call | solution.py:301
  323.2 32.9 %shard_map.362 = (bf16[1024,1280]{1,0:T(8,128)(2,1)}, bf16[1024,1280]{1,0:T(8,128)(2,1)}, bf16[1024,1280]{1,0:T(8,128)(2,1)}, bf16[1280,768]{1,0:T(8,128)(2,1)},...) custom-call(s32[10]{0:T(128)} %stack.189.info, bf16[3072,1280]{1,0:T(8,128)(2,1)} %get-tuple-element.219.refs_0_, ...), custom_call_target="tpu_custom_call" | custom-call | flops 1000 | bytes 1000 | tf_op jit(solution)/shard_map/pallas_call | solution.py:573
  365.1 38.8 %shard_map.363 = (bf16[2048,320]{1,0:T(8,128)(2,1)}, bf16[3072,320]{1,0:T(8,128)(2,1)}, bf16[3072,320]{1,0:T(8,128)(2,1)}) custom-call(bf16[2048,512]{1,0:T(8,128)(2,1)} %get-tuple-element.211.q_ref, bf16[3072,512]{1,0:T(8,128)(2,1)} %get-tuple-element.212.k_ref, bf16[3072,512]{1,0:T(8,128)(2,1)} %get-tuple-element.213.v_ref, ...), custom_call_target="tpu_custom_call" | custom-call | flops 1000 | bytes 1000 | tf_op jit(solution)/shard_map/pallas_call | solution.py:301
  407.1 13.8 %shard_map.364 = (bf16[1024,1280]{1,0:T(8,128)(2,1)}, bf16[1024,1280]{1,0:T(8,128)(2,1)}) custom-call(s32[10]{0:T(128)} %stack.188.info, bf16[3072,1280]{1,0:T(8,128)(2,1)} %get-tuple-element.219.refs_0_, bf16[2048,320]{1,0:T(8,128)(2,1)} %get-tuple-element.307.refs_1_, bf16[3072,320]{1,0:T(8,128)(2,1)} %get-tuple-element.284.refs_2_, ...), custom_call_target="tpu_custom_call" | custom-call | flops 1000 | bytes 1000 | tf_op jit(solution)/shard_map/pallas_call | solution.py:573
  422.8 9.0 %shard_map.366 = bf16[1024,1280]{1,0:T(8,128)(2,1)} custom-call(s32[10]{0:T(128)} %stack.189.info, bf16[3072,1280]{1,0:T(8,128)(2,1)} %get-tuple-element.219.refs_0_, bf16[2048,320]{1,0:T(8,128)(2,1)} %get-tuple-element.307.refs_1_, bf16[3072,320]{1,0:T(8,128)(2,1)} %get-tuple-element.284.refs_2_, bf16[3072,320]{1,0:T(8,128)(2,1)} %get-tuple-element.285.refs_3_, ...), custom_call_target="tpu_custom_call" | custom-call | flops 1000 | bytes 1000 | tf_op jit(solution)/shard_map/pallas_call | solution.py:573
  436.8 5.7 shard_map.365
  450.2 5.9 %shard_map.371 = bf16[2,1024,1280]{2,1,0:T(8,128)(2,1)} custom-call(s32[2]{0:T(128)} %pad_add_fusion.info, bf16[1024,1280]{1,0:T(8,128)(2,1)} %get-tuple-element.258.refs_0_, bf16[1024,1280]{1,0:T(8,128)(2,1)} %copy-done.4, bf16[1024,1280]{1,0:T(8,128)(2,1)} %collective-permute-done.28.refs_2_, bf16[1024,1280]{1,0:T(8,128)(2,1)} %collective-permute-done.33.refs_3_), custom_call_target="tpu_custom_call" | custom-call | flops 1000 | bytes 1000 | tf_op jit(solution)/shard_map/pallas_call | solution.py:655
  456.2 5.9 %shard_map.370 = bf16[2,1024,1280]{2,1,0:T(8,128)(2,1)} custom-call(s32[2]{0:T(128)} %pad_add_fusion.info, bf16[1024,1280]{1,0:T(8,128)(2,1)} %get-tuple-element.258.refs_0_, bf16[1024,1280]{1,0:T(8,128)(2,1)} %copy-done.4, bf16[1024,1280]{1,0:T(8,128)(2,1)} %collective-permute-done.28.refs_2_, bf16[1024,1280]{1,0:T(8,128)(2,1)} %collective-permute-done.33.refs_3_), custom_call_target="tpu_custom_call" | custom-call | flops 1000 | bytes 1000 | tf_op jit(solution)/shard_map/pallas_call | solution.py:655
  462.1 19.3 %shard_map.368 = (bf16[1280,512]{1,0:T(8,128)(2,1)}, bf16[1280,512]{1,0:T(8,128)(2,1)}, f32[8,1024]{1,0:T(8,128)}) custom-call(s32[10]{0:T(128)} %stack.189.info, bf16[3072,1280]{1,0:T(8,128)(2,1)} %get-tuple-element.219.refs_0_, bf16[2048,320]{1,0:T(8,128)(2,1)} %get-tuple-element.307.refs_1_, bf16[3072,320]{1,0:T(8,128)(2,1)} %get-tuple-element.284.refs_2_, ...), custom_call_target="tpu_custom_call" | custom-call | flops 1000 | bytes 1000 | tf_op jit(solution)/shard_map/pallas_call | solution.py:573
  492.1 6.4 %shard_map.367 = (bf16[512,1280]{1,0:T(8,128)(2,1)}, f32[8,1280]{1,0:T(8,128)}) custom-call(f32[8,1280]{1,0:T(8,128)} %get-tuple-element.198.gain_ref, bf16[1024,1280]{1,0:T(8,128)(2,1)} %bitcast.151, f32[1024,1280]{1,0:T(8,128)} %get-tuple-element.239.mix_ref, bf16[1024,1280]{1,0:T(8,128)(2,1)} %get-tuple-element.301.refs_0_, bf16[1024,1280]{1,0:T(8,128)(2,1)} %copy-done.5, ...), custom_call_target="tpu_custom_call" | custom-call | flops 1000 | bytes 1000 | tf_op jit(solution)/shard_map/pallas_call | solution.py:621
  501.4 9.6 %collective-permute-done.46 = bf16[320,512]{1,0:T(8,128)(2,1)} collective-permute-done((bf16[320,512]{1,0:T(8,128)(2,1)S(1)}, bf16[320,512]{1,0:T(8,128)(2,1)}, u32[]{:S(2)}, u32[]{:S(2)}) %collective-permute-start.46) | collective-permute-done | bytes 327712 | tf_op jit(solution)/shard_map/ppermute | solution.py:676
  514.6 6.7 %collective-permute-start.49 = (bf16[320,512]{1,0:T(8,128)(2,1)S(1)}, bf16[320,512]{1,0:T(8,128)(2,1)S(1)}, u32[]{:S(2)}, u32[]{:S(2)}) collective-permute-start(bf16[320,512]{1,0:T(8,128)(2,1)S(1)} %copy-done.22), channel_id=1, source_target_pairs={{0,8},{8,0},{16,24},{24,16},{1,9},{9,1},{17,25},{25,17},{2,10},{10... | collective-permute-start | bytes 983048 | tf_op jit(solution)/shard_map/ppermute | solution.py:676
  524.4 7.4 %shard_map.369 = f32[2,1024,1280]{2,1,0:T(8,128)} custom-call(s32[2]{0:T(128)} %pad_add_fusion.info, bf16[512,1280]{1,0:T(8,128)(2,1)} %get-tuple-element.297.refs_0_, bf16[512,1280]{1,0:T(8,128)(2,1)} %collective-permute-done.41.refs_1_, bf16[512,1280]{1,0:T(8,128)(2,1)} %collective-permute-done.43.refs_2_, bf16[512,1280]{1,0:T(8,128)(2,1)} %collective-permute-done.44.refs_3_), custom_call_target="tpu_custom_call" | custom-call | flops 1000 | bytes 1000 | tf_op jit(solution)/shard_map/pallas_call | solution.py:655
  533.8 13.1 %collective-permute-done.50 = bf16[320,512]{1,0:T(8,128)(2,1)S(1)} collective-permute-done((bf16[320,512]{1,0:T(8,128)(2,1)S(1)}, bf16[320,512]{1,0:T(8,128)(2,1)S(1)}, u32[]{:S(2)}, u32[]{:S(2)}) %collective-permute-start.50) | collective-permute-done | bytes 327712 | tf_op jit(solution)/shard_map/ppermute | solution.py:676
  551.4 5.6 collective-permute-start.57
  580.8 7.5 %shard_map.372 = f32[2,1024,1280]{2,1,0:T(8,128)} custom-call(s32[2]{0:T(128)} %pad_add_fusion.info, bf16[512,1280]{1,0:T(8,128)(2,1)} %get-tuple-element.333.refs_0_, bf16[512,1280]{1,0:T(8,128)(2,1)} %copy-done.12, bf16[512,1280]{1,0:T(8,128)(2,1)} %collective-permute-done.48.refs_2_, bf16[512,1280]{1,0:T(8,128)(2,1)} %copy-done.13), custom_call_target="tpu_custom_call" | custom-call | flops 1000 | bytes 1000 | tf_op jit(solution)/shard_map/pallas_call | solution.py:655
  (334 shorter events, 189.2 us)
Async XLA Ops:
  5.6 30.7 %collective-permute-start.2 = (bf16[160,962]{1,0:T(8,128)(2,1)S(1)}, bf16[160,962]{1,0:T(8,128)(2,1)}, u32[]{:S(2)}, u32[]{:S(2)}) collective-permute-start(bf16[160,962]{1,0:T(8,128)(2,1)S(1)} %concatenate.48), channel_id=1, source_target_pairs={{0,8},{8,0},{16,24},{24,16},{1,9},{9,1},{17,25},{25,17},{2,10},{10... | collective-permute-start | bytes 923528 | tf_op jit(solution)/shard_map/ppermute | solution.py:676
  41.5 32.6 %collective-permute-start.6 = (bf16[512,1280]{1,0:T(8,128)(2,1)}, bf16[512,1280]{1,0:T(8,128)(2,1)}, u32[]{:S(2)}, u32[]{:S(2)}) collective-permute-start(bf16[512,1280]{1,0:T(8,128)(2,1)} %collective-permute-done.1.refs_2_), channel_id=1, source_target_pairs={{0,1},{1,0},{2,3},{3,2},{4,5},{5,4},{6,7},{7,6},{8,9},{9,8},{10,11... | collective-permute-start | bytes 3932168 | tf_op jit(solution)/shard_map/ppermute | solution.py:676
  42.9 31.3 %collective-permute-start.5 = (bf16[4,160,962]{2,1,0:T(8,128)(2,1)S(1)}, bf16[4,160,962]{2,1,0:T(8,128)(2,1)S(1)}, u32[]{:S(2)}, u32[]{:S(2)}) collective-permute-start(bf16[4,160,962]{2,1,0:T(8,128)(2,1)S(1)} %pad_maximum_fusion.3.refs_4_), channel_id=1, source_target_pairs={{0,4},{4,0},{1,5},{5,1},{2,6},{6,2},{3,7},{7,3},{8,12},{12,8},{9,1... | collective-permute-start | bytes 3694088 | tf_op jit(solution)/shard_map/ppermute | solution.py:676
  62.0 55.6 %collective-permute-start.20 = (f32[2,320]{1,0:T(2,128)S(1)}, f32[2,320]{1,0:T(2,128)S(1)}, u32[]{:S(2)}, u32[]{:S(2)}) collective-permute-start(f32[2,320]{1,0:T(2,128)S(1)} %fusion.13), channel_id=1, source_target_pairs={{0,1},{1,0},{2,3},{3,2},{4,5},{5,4},{6,7},{7,6},{8,9},{9,8},{10,11... | collective-permute-start | bytes 7688 | tf_op jit(solution)/shard_map/ppermute | solution.py:676
  74.1 35.6 %collective-permute-start.11 = (bf16[160,964]{1,0:T(8,128)(2,1)S(1)}, bf16[160,964]{1,0:T(8,128)(2,1)}, u32[]{:S(2)}, u32[]{:S(2)}) collective-permute-start(bf16[160,964]{1,0:T(8,128)(2,1)S(1)} %concatenate.51), channel_id=1, source_target_pairs={{0,8},{8,0},{16,24},{24,16},{1,9},{9,1},{17,25},{25,17},{2,10},{10... | collective-permute-start | bytes 925448 | tf_op jit(solution)/shard_map/ppermute | solution.py:676
  79.3 30.4 %collective-permute-start.12 = (bf16[160,964]{1,0:T(8,128)(2,1)S(1)}, bf16[160,964]{1,0:T(8,128)(2,1)}, u32[]{:S(2)}, u32[]{:S(2)}) collective-permute-start(bf16[160,964]{1,0:T(8,128)(2,1)S(1)} %concatenate.51), channel_id=1, source_target_pairs={{0,16},{8,24},{16,0},{24,8},{1,17},{9,25},{17,1},{25,9},{2,18},{10... | collective-permute-start | bytes 925448 | tf_op jit(solution)/shard_map/ppermute | solution.py:676
  145.1 42.3 %collective-permute-start.21 = (bf16[4,160,964]{2,1,0:T(8,128)(2,1)}, bf16[4,160,964]{2,1,0:T(8,128)(2,1)}, u32[]{:S(2)}, u32[]{:S(2)}) collective-permute-start(bf16[4,160,964]{2,1,0:T(8,128)(2,1)} %collective-permute-done.14.refs_6_), channel_id=1, source_target_pairs={{0,4},{4,0},{1,5},{5,1},{2,6},{6,2},{3,7},{7,3},{8,12},{12,8},{9,1... | collective-permute-start | bytes 3701768 | tf_op jit(solution)/shard_map/ppermute | solution.py:676
  247.3 73.9 %collective-permute-start.27 = (bf16[1024,1280]{1,0:T(8,128)(2,1)}, bf16[1024,1280]{1,0:T(8,128)(2,1)S(1)}, u32[]{:S(2)}, u32[]{:S(2)}) collective-permute-start(bf16[1024,1280]{1,0:T(8,128)(2,1)} %get-tuple-element.258.refs_0_), channel_id=1, source_target_pairs={{0,1},{1,0},{2,3},{3,2},{4,5},{5,4},{6,7},{7,6},{8,9},{9,8},{10,11... | collective-permute-start | bytes 7864328 | tf_op jit(solution)/shard_map/ppermute | solution.py:676
  247.6 108.5 %collective-permute-start.28 = (bf16[1024,1280]{1,0:T(8,128)(2,1)}, bf16[1024,1280]{1,0:T(8,128)(2,1)}, u32[]{:S(2)}, u32[]{:S(2)}) collective-permute-start(bf16[1024,1280]{1,0:T(8,128)(2,1)} %get-tuple-element.258.refs_0_), channel_id=1, source_target_pairs={{0,2},{1,3},{2,0},{3,1},{4,6},{5,7},{6,4},{7,5},{8,10},{9,11},{10,... | collective-permute-start | bytes 7864328 | tf_op jit(solution)/shard_map/ppermute | solution.py:676
  273.9 39.9 %collective-permute-start.26 = (bf16[4,160,1024]{2,1,0:T(8,128)(2,1)S(1)}, bf16[4,160,1024]{2,1,0:T(8,128)(2,1)}, u32[]{:S(2)}, u32[]{:S(2)}) collective-permute-start(bf16[4,160,1024]{2,1,0:T(8,128)(2,1)S(1)} %get-tuple-element.248), channel_id=1, source_target_pairs={{0,4},{4,0},{1,5},{5,1},{2,6},{6,2},{3,7},{7,3},{8,12},{12,8},{9,1... | collective-permute-start | bytes 3932168 | tf_op jit(solution)/shard_map/ppermute | solution.py:676
  313.8 42.3 %collective-permute-start.29 = (bf16[4,160,896]{2,1,0:T(8,128)(2,1)}, bf16[4,160,896]{2,1,0:T(8,128)(2,1)}, u32[]{:S(2)}, u32[]{:S(2)}) collective-permute-start(bf16[4,160,896]{2,1,0:T(8,128)(2,1)} %get-tuple-element.259), channel_id=1, source_target_pairs={{0,4},{4,0},{1,5},{5,1},{2,6},{6,2},{3,7},{7,3},{8,12},{12,8},{9,1... | collective-permute-start | bytes 3440648 | tf_op jit(solution)/shard_map/ppermute | solution.py:676
  318.2 37.9 %collective-permute-start.30 = (bf16[160,1024]{1,0:T(8,128)(2,1)}, bf16[160,1024]{1,0:T(8,128)(2,1)}, u32[]{:S(2)}, u32[]{:S(2)}) collective-permute-start(bf16[160,1024]{1,0:T(8,128)(2,1)} %get-tuple-element.261), channel_id=1, source_target_pairs={{0,8},{8,0},{16,24},{24,16},{1,9},{9,1},{17,25},{25,17},{2,10},{10... | collective-permute-start | bytes 983048 | tf_op jit(solution)/shard_map/ppermute | solution.py:676
  318.7 37.4 %collective-permute-start.31 = (bf16[160,1024]{1,0:T(8,128)(2,1)}, bf16[160,1024]{1,0:T(8,128)(2,1)}, u32[]{:S(2)}, u32[]{:S(2)}) collective-permute-start(bf16[160,1024]{1,0:T(8,128)(2,1)} %get-tuple-element.262), channel_id=1, source_target_pairs={{0,16},{8,24},{16,0},{24,8},{1,17},{9,25},{17,1},{25,9},{2,18},{10... | collective-permute-start | bytes 983048 | tf_op jit(solution)/shard_map/ppermute | solution.py:676
  321.2 34.9 %collective-permute-start.32 = (bf16[160,1024]{1,0:T(8,128)(2,1)}, bf16[160,1024]{1,0:T(8,128)(2,1)}, u32[]{:S(2)}, u32[]{:S(2)}) collective-permute-start(bf16[160,1024]{1,0:T(8,128)(2,1)} %get-tuple-element.263), channel_id=1, source_target_pairs={{0,24},{8,16},{16,8},{24,0},{1,25},{9,17},{17,9},{25,1},{2,26},{10... | collective-permute-start | bytes 983048 | tf_op jit(solution)/shard_map/ppermute | solution.py:676
  356.1 49.4 %collective-permute-start.33 = (bf16[1024,1280]{1,0:T(8,128)(2,1)}, bf16[1024,1280]{1,0:T(8,128)(2,1)}, u32[]{:S(2)}, u32[]{:S(2)}) collective-permute-start(bf16[1024,1280]{1,0:T(8,128)(2,1)} %collective-permute-done.28.refs_2_), channel_id=1, source_target_pairs={{0,1},{1,0},{2,3},{3,2},{4,5},{5,4},{6,7},{7,6},{8,9},{9,8},{10,11... | collective-permute-start | bytes 7864328 | tf_op jit(solution)/shard_map/ppermute | solution.py:676
  360.2 45.3 %collective-permute-start.34 = (bf16[1280,768]{1,0:T(8,128)(2,1)S(1)}, bf16[1280,768]{1,0:T(8,128)(2,1)}, u32[]{:S(2)}, u32[]{:S(2)}) collective-permute-start(bf16[1280,768]{1,0:T(8,128)(2,1)S(1)} %copy-done.45), channel_id=1, source_target_pairs={{0,2},{1,3},{2,0},{3,1},{4,6},{5,7},{6,4},{7,5},{8,10},{9,11},{10,... | collective-permute-start | bytes 5898248 | tf_op jit(solution)/shard_map/ppermute | solution.py:676
  360.7 43.3 %collective-permute-start.35 = (bf16[160,896]{1,0:T(8,128)(2,1)S(1)}, bf16[160,896]{1,0:T(8,128)(2,1)S(1)}, u32[]{:S(2)}, u32[]{:S(2)}) collective-permute-start(bf16[160,896]{1,0:T(8,128)(2,1)S(1)} %get-tuple-element.280), channel_id=1, source_target_pairs={{0,8},{8,0},{16,24},{24,16},{1,9},{9,1},{17,25},{25,17},{2,10},{10... | collective-permute-start | bytes 860168 | tf_op jit(solution)/shard_map/ppermute | solution.py:676
  360.7 43.3 %collective-permute-start.36 = (bf16[160,896]{1,0:T(8,128)(2,1)S(1)}, bf16[160,896]{1,0:T(8,128)(2,1)S(1)}, u32[]{:S(2)}, u32[]{:S(2)}) collective-permute-start(bf16[160,896]{1,0:T(8,128)(2,1)S(1)} %get-tuple-element.281), channel_id=1, source_target_pairs={{0,16},{8,24},{16,0},{24,8},{1,17},{9,25},{17,1},{25,9},{2,18},{10... | collective-permute-start | bytes 860168 | tf_op jit(solution)/shard_map/ppermute | solution.py:676
  363.7 40.3 %collective-permute-start.37 = (bf16[160,896]{1,0:T(8,128)(2,1)S(1)}, bf16[160,896]{1,0:T(8,128)(2,1)S(1)}, u32[]{:S(2)}, u32[]{:S(2)}) collective-permute-start(bf16[160,896]{1,0:T(8,128)(2,1)S(1)} %get-tuple-element.282), channel_id=1, source_target_pairs={{0,24},{8,16},{16,8},{24,0},{1,25},{9,17},{17,9},{25,1},{2,26},{10... | collective-permute-start | bytes 860168 | tf_op jit(solution)/shard_map/ppermute | solution.py:676
  445.3 38.5 %collective-permute-start.42 = (bf16[512,1280]{1,0:T(8,128)(2,1)}, bf16[512,1280]{1,0:T(8,128)(2,1)}, u32[]{:S(2)}, u32[]{:S(2)}) collective-permute-start(bf16[512,1280]{1,0:T(8,128)(2,1)} %add_convert_fusion), channel_id=1, source_target_pairs={{0,4},{4,0},{1,5},{5,1},{2,6},{6,2},{3,7},{7,3},{8,12},{12,8},{9,1... | collective-permute-start | bytes 3932168 | tf_op jit(solution)/shard_map/ppermute | solution.py:676
  446.4 37.4 %collective-permute-start.43 = (bf16[512,1280]{1,0:T(8,128)(2,1)S(1)}, bf16[512,1280]{1,0:T(8,128)(2,1)}, u32[]{:S(2)}, u32[]{:S(2)}) collective-permute-start(bf16[512,1280]{1,0:T(8,128)(2,1)S(1)} %copy-done.10), channel_id=1, source_target_pairs={{0,2},{1,3},{2,0},{3,1},{4,6},{5,7},{6,4},{7,5},{8,10},{9,11},{10,... | collective-permute-start | bytes 3932168 | tf_op jit(solution)/shard_map/ppermute | solution.py:676
  462.1 61.7 %collective-permute-start.41 = (bf16[512,1280]{1,0:T(8,128)(2,1)S(1)}, bf16[512,1280]{1,0:T(8,128)(2,1)}, u32[]{:S(2)}, u32[]{:S(2)}) collective-permute-start(bf16[512,1280]{1,0:T(8,128)(2,1)S(1)} %copy-done.10), channel_id=1, source_target_pairs={{0,1},{1,0},{2,3},{3,2},{4,5},{5,4},{6,7},{7,6},{8,9},{9,8},{10,11... | collective-permute-start | bytes 3932168 | tf_op jit(solution)/shard_map/ppermute | solution.py:676
  511.0 35.9 %collective-permute-start.48 = (bf16[512,1280]{1,0:T(8,128)(2,1)}, bf16[512,1280]{1,0:T(8,128)(2,1)}, u32[]{:S(2)}, u32[]{:S(2)}) collective-permute-start(bf16[512,1280]{1,0:T(8,128)(2,1)} %get-tuple-element.333.refs_0_), channel_id=1, source_target_pairs={{0,2},{1,3},{2,0},{3,1},{4,6},{5,7},{6,4},{7,5},{8,10},{9,11},{10,... | collective-permute-start | bytes 3932168 | tf_op jit(solution)/shard_map/ppermute | solution.py:676
  523.8 38.6 %collective-permute-start.55 = (bf16[160,3,320]{2,0,1:T(8,128)(2,1)S(1)}, bf16[160,3,320]{2,0,1:T(8,128)(2,1)S(1)}, u32[]{:S(2)}, u32[]{:S(2)}) collective-permute-start(bf16[160,3,320]{2,0,1:T(8,128)(2,1)S(1)} %bitcast.175), channel_id=1, source_target_pairs={{0,2},{1,3},{2,0},{3,1},{4,6},{5,7},{6,4},{7,5},{8,10},{9,11},{10,... | collective-permute-start | bytes 921608 | tf_op jit(solution)/shard_map/ppermute | solution.py:676
  (88 other events, 1188.3 us)

commit v2 on v1

--- a/solution.py
+++ b/solution.py
@@ -438,17 +438,18 @@
     )(info, tokens, grad, valid, *mine, *theirs, *flat, up_bias)
 
 
-BEYOND, THEIRS, MINE = 0, 1, 2
-
-
-def project_back_kernel(sums, spans, more, adding, counts, info, *refs):
+BEYOND, BEYOND_TOO, THEIRS, MINE = 0, 1, 2, 3
+
+
+def project_back_kernel(sums, spans, more, adding, placing, counts, info, *refs):
     x_ref, dq_ref, dk_ref, dv_ref = refs[:4]
     refs = refs[4:]
     w_refs, refs = refs[: len(counts)], refs[len(counts) :]
     prev_refs, refs = refs[:more], refs[more:]
     other, refs = refs[:adding], refs[adding:]
+    shares, refs = refs[:placing], refs[placing:]
     outs, refs = refs[: len(spans)], refs[len(spans) :]
-    d = refs[-1]
+    d = refs[-3] if placing else refs[-1]
     j = pl.program_id(0)
     cols = dq_ref.shape[1]
     if spans:
@@ -483,7 +484,39 @@
     d[:, 2 * cols : 3 * cols] = dv_ref[...]
     all_d = d[...]
     if sums:
-        dw_refs, (sum_ref, acc) = refs[:sums], refs[sums : sums + 2]
+        dw_refs, refs = refs[:sums], refs[sums:]
+        if placing:
+            targets, (stage, sem) = refs[1:3], refs[-2:]
+            refs = (refs[0], *refs[3:-2])
+            half = stage.shape[1]
+            c, y = info[0], info[2 + sum(counts)]
+            loads, stores = [], []
+            for i, share in enumerate(shares):
+                spot = pl.ds(pl.multiple_of((c ^ (i % 2)) * half, 16), half)
+                for kind, target in enumerate(targets):
+                    n = 2 * i + kind
+                    source, place = share.at[pl.ds(kind * half, half)], stage.at[n]
+                    loads.append(pltpu.make_async_copy(source, place, sem.at[0, n]))
+                    place = target.at[y ^ (i // 2), spot]
+                    stores.append(pltpu.make_async_copy(stage.at[n], place, sem.at[1, n]))
+
+            @pl.when(j == 0)
+            def _():
+                for copy in loads:
+                    copy.start()
+
+            @pl.when(j == 2)
+            def _():
+                for load, store in zip(loads, stores):
+                    load.wait()
+                    store.start()
+
+            @pl.when(j == pl.num_programs(0) - 1)
+            def _():
+                for copy in stores:
+                    copy.wait()
+
+        sum_ref, acc = refs[:2]
 
         @pl.when(j == 0)
         def _():
@@ -521,16 +554,16 @@
 
 
 def project_back(
-    sums, wanted, c, starts, x, dq, dk, dv, weights, previous, rows, half, own, other=()
+    sums, wanted, c, y, starts, x, dq, dk, dv, weights, previous, rows, half, own, other, shares
 ):
     total, width = x.shape
     cols = dq.shape[1]
-    sizes = ((total - own) // rows, own // 2 // rows, own // 2 // rows)
-    n_beyond = sizes[0] if BEYOND in wanted else 0
-    n_half = sizes[1]
+    sizes = ((total - own) // 2 // rows,) * 2 + (own // 2 // rows,) * 2
+    n_beyond = 2 * sizes[0] if BEYOND in wanted else 0
+    n_half = sizes[2]
     per = half // rows
     steps = sum(sizes[i] for i in wanted)
-    info = jnp.stack([jnp.asarray(v, jnp.int32) for v in (c, *starts, n_beyond)])
+    info = jnp.stack([jnp.asarray(v, jnp.int32) for v in (c, *starts, n_beyond, y)])
 
     def row(j, info):
         i = j - n_beyond
@@ -567,9 +600,16 @@
         out_specs += [whole((width, n)) for n in sums] + [whole((8, lanes))]
         out_shape += [shape((width, n), bf16) for n in sums] + [shape((8, lanes), f32)]
         scratch.append(pltpu.VMEM((width, lanes), f32))
+    hbm = pl.BlockSpec(memory_space=pl.ANY)
+    if shares:
+        out_specs += [hbm, hbm]
+        out_shape += [shape((2, own // 2, width), bf16)] * 2
     if parts:
         scratch.append(pltpu.VMEM((width, lanes), bf16))
     scratch.append(pltpu.VMEM((rows, lanes), bf16))
+    if shares:
+        scratch.append(pltpu.VMEM((2 * len(shares), half, width), bf16))
+        scratch.append(pltpu.SemaphoreType.DMA((2, 2 * len(shares))))
     return pl.pallas_call(
         functools.partial(
             project_back_kernel,
@@ -577,6 +617,7 @@
             spans,
             len(previous or []),
             len(other),
+            len(shares),
             [w.shape[0] for w in weights],
         ),
         grid_spec=pltpu.PrefetchScalarGridSpec(
@@ -585,14 +626,15 @@
             in_specs=[x_spec, q_spec, d_spec, d_spec]
             + [once(w.shape) for w in weights]
             + (parts if previous else [])
-            + [once(o.shape) for o in other],
+            + [once(o.shape) for o in other]
+            + [hbm] * len(shares),
             out_specs=out_specs,
             scratch_shapes=scratch,
         ),
         out_shape=out_shape,
         compiler_params=params(),
         cost_estimate=cost(1000, 1000),
-    )(info, x, dq, dk, dv, *weights, *(previous or []), *other)
+    )(info, x, dq, dk, dv, *weights, *(previous or []), *other, *shares)
 
 
 def finish_kernel(n, gain_ref, tok_ref, mix_ref, *refs):
@@ -632,43 +674,35 @@
     )(gain, tokens, mixed, *shares, *back)
 
 
-def assemble_kernel(info, *refs):
+def assemble_kernel(count, info, *refs):
     i = pl.program_id(0)
-    for m in range(4):
+    for m in range(count):
 
         @pl.when(i == m)
         def _():
-            refs[4][...] = refs[m][...].astype(refs[4].dtype)[None]
-
-
-def assemble(info, pieces, kind, half, dtype):
+            refs[-1][...] = refs[m][...].astype(refs[-1].dtype)[None]
+
+
+def assemble(info, pieces, kind, half, dtype, first=0, into=()):
     width = pieces[0].shape[1]
-    rows = half
-    n = half // rows
-
-    def source(m, i, s):
-        return kind * n + jnp.where(i < m, 0, jnp.where(i > m, n - 1, s))
-
-    def target(i, s, info):
-        return info[0] ^ (i // 2), (info[1] ^ (i % 2)) * n + s, 0
-
+    count = len(pieces)
     return pl.pallas_call(
-        assemble_kernel,
+        functools.partial(assemble_kernel, count),
         grid_spec=pltpu.PrefetchScalarGridSpec(
             num_scalar_prefetch=1,
-            grid=(4, n),
-            in_specs=[
-                pl.BlockSpec(
-                    (rows, width), functools.partial(lambda m, i, s, info: (source(m, i, s), 0), m)
-                )
-                for m in range(4)
-            ],
-            out_specs=pl.BlockSpec((1, rows, width), target),
+            grid=(count,),
+            in_specs=[pl.BlockSpec((half, width), lambda i, info: (kind, 0))] * count
+            + [pl.BlockSpec(memory_space=pl.ANY)] * len(into),
+            out_specs=pl.BlockSpec(
+                (1, half, width),
+                lambda i, info: (info[0] ^ ((first + i) // 2), info[1] ^ ((first + i) % 2), 0),
+            ),
         ),
         out_shape=jax.ShapeDtypeStruct((2, 2 * half, width), dtype),
-        compiler_params=params(2),
+        input_output_aliases={count + 1: 0} if into else {},
+        compiler_params=params(),
         cost_estimate=cost(1000, 1000),
-    )(info, *pieces)
+    )(info, *pieces, *into)
 
 
 def swap(value, axis, bit):
@@ -799,7 +833,7 @@
         deep = query_weight.shape[0]
         starts = [((z ^ i) * 2 + (x ^ k)) * deep for k in (0, 1) for i in range(4)]
         places = [(1 - x) * prompt_rows + side * half for side in (c, 1 - c)]
-        tokens_piece = pick(prompt.reshape(2, half, width), c)
+        tokens_piece = pick(prompt_tokens.reshape(groups * 2, half, width), 2 * y + c)
         tokens_piece, qkv_piece = phase(tokens_piece, qkv_piece)
         tokens_piece = swap(tokens_piece, C, 1)
         parts = over_z(qkv_piece)
@@ -900,109 +934,146 @@
     )
 
     where = ints(y, c)
-
-    outputs = [output, swap(output, T, 1), swap(output, T, 2), None]
-
+    back_rows = min(512, half)
+    everything = (BEYOND, BEYOND_TOO, THEIRS, MINE)
+    lanes = tiled(3 * cols)
+    far_widths = (3 * lanes // 4, lanes // 4)
     received = swap(grad_away, T, 1)
     grad_heads = in_order(
         c, grad_near.reshape(2, half, -1), received.reshape(2, half, -1), 1
     ).reshape(own, -1)
+    if direct():
+        grad_heads, oud_send, output = phase(grad_heads, oud_send, output)
     oud_send = swap(oud_send, T, 1)
-    wide_part = min(1024, oud_send.shape[1])
-    oud_pieces = [slice(0, wide_part), slice(wide_part, None)]
-    oud_pieces = [oud_keep[:, p].astype(f32) + oud_send[:, p].astype(f32) for p in oud_pieces]
-    if direct():
-        away, kept = zip(*[x_parts(p, 0) for p in oud_pieces])
-        grad_heads, *parts = phase(grad_heads, *away, *[k.astype(bf16) for k in kept])
-        away, kept = parts[:2], parts[2:]
-        away[0] = swap(away[0], C, 1)
-    dq, dk, dv = attend_back(q1, k1, v1, a1, log1, grad_heads, PAIR, later, cont)
-    if direct():
-        dq, away[0], away[1] = phase(dq, away[0], away[1])
-        away[1] = swap(away[1], C, 1)
-        parts, first_sum = z_parts(kept[0].astype(f32) + away[0].astype(f32), 0)
-        dq, first_sum, *parts = phase(dq, first_sum, *parts)
+    outputs = [output, swap(output, T, 1), swap(output, T, 2), None]
+
+    def back_from(q, k, v, out, logs, weights, first):
+        def run(grads):
+            return attend_back(q, k, v, out, logs, grads, first, later, cont)
+
+        def inputs(grads, wanted, widths, previous, other=(), shares=()):
+            return project_back(
+                widths,
+                wanted,
+                c,
+                y,
+                starts,
+                normed_in,
+                *grads,
+                weights,
+                previous,
+                back_rows,
+                half,
+                own,
+                other,
+                shares,
+            )
+
+        return run, inputs
+
+    far_attend, far_back = back_from(q1, k1, v1, a1, log1, qkv_far, PAIR)
+    near_attend, near_back = back_from(q0, k0, v0, a0, log0, qkv_own, 0)
+
+    grads = far_attend(grad_heads)
+    if direct():
+        *grads, oud_keep, oud_send = phase(*grads, oud_keep, oud_send)
+    oud_parts = [slice(0, min(1024, oud_send.shape[1])), slice(min(1024, oud_send.shape[1]), None)]
+    oud_parts = [oud_keep[:, p].astype(f32) + oud_send[:, p].astype(f32) for p in oud_parts]
+    if direct():
+        away, kept = zip(*[x_parts(p, 0) for p in oud_parts])
+        kept = [k.astype(bf16) for k in kept]
+        *grads, kept[0], kept[1], away0, away1 = phase(*grads, *kept, *away)
+        away0 = swap(away0, C, 1)
+    *shares, far, far_rest, sums1 = far_back(grads, everything, far_widths, [])
+    if direct():
+        far, far_rest, grad_heads, away0, away1, outputs[1], outputs[2] = phase(
+            far, far_rest, grad_heads, away0, away1, outputs[1], outputs[2]
+        )
+        parts, first_sum = z_parts(kept[0].astype(f32) + away0.astype(f32), 0)
+        grad_heads, far, away1, first_sum, *parts = phase(grad_heads, far, away1, first_sum, *parts)
+        away1 = swap(away1, C, 1)
         first_parts = z_moves(parts)
-    back_rows = min(512, half)
-    everything = (BEYOND, THEIRS, MINE)
-    lanes = tiled(3 * cols)
-    far_widths = (3 * lanes // 4, lanes // 4)
-    *shares, far, far_rest, sums1 = project_back(
-        far_widths, everything, c, starts, normed_in, dq, dk, dv, qkv_far, [], back_rows, half, own
-    )
-    if direct():
-        far, far_rest, grad_heads, outputs[1], outputs[2], away[1], first_sum, *parts = phase(
-            far, far_rest, grad_heads, outputs[1], outputs[2], away[1], first_sum, *first_parts
-        )
-        first_sum = z_sum(first_sum, parts)
-        parts, last_sum = z_parts(kept[1].astype(f32) + away[1].astype(f32), 0)
-        first_sum, last_sum, grad_heads, far, *parts = phase(
-            first_sum, last_sum, grad_heads, far, *parts
-        )
+    far = swap(far, T, 2)
+    grads = near_attend(grad_heads)
+    if direct():
+        *grads, far, far_rest, away1, first_sum, outputs[2], p1, p2, p3 = phase(
+            *grads, far, far_rest, away1, first_sum, outputs[2], *first_parts
+        )
+        first_done = [p1, p2, p3]
+        parts, last_sum = z_parts(kept[1].astype(f32) + away1.astype(f32), 0)
+        g0, far_rest, first_sum, last_sum, *parts = phase(
+            grads[0], far_rest, first_sum, last_sum, *parts
+        )
+        grads[0] = g0
         last_parts = z_moves(parts)
-    far = swap(far, T, 2)
+    far_rest = swap(far_rest, T, 2)
     outputs[3] = swap(outputs[2], T, 1)
-    dq, dk, dv = attend_back(q0, k0, v0, a0, log0, grad_heads, 0, later, cont)
-    def near_back(sums, wanted, dq, *rest):
-        previous, other = rest[0], rest[1:]
-        return project_back(
-            sums,
-            wanted,
-            c,
-            starts,
-            normed_in,
-            dq,
-            dk,
-            dv,
-            qkv_own,
-            previous,
-            back_rows,
-            half,
-            own,
-            other,
-        )
-
-    if direct():
-        dq, dk, dv, outputs[3], far, far_rest, last_sum, *parts = phase(
-            dq, dk, dv, outputs[3], far, far_rest, last_sum, *last_parts
-        )
-        oud_grad = jnp.concatenate([first_sum, z_sum(last_sum, parts)], axis=1).astype(bf16)
-        far_rest = swap(far_rest, T, 2)
-        their_share, my_share = near_back((), (THEIRS, MINE), dq, shares[1:])
-        their_share, my_share, dq, far_rest = phase(their_share, my_share, dq, far_rest)
-        their_share = swap(their_share, T, 1)
-        (beyond_share,) = near_back((), (BEYOND,), dq, shares[:1])
+    if direct():
+        b0, b1, their_share, my_share = near_back(grads, everything, (), shares)
+        b0, b1, their_share, my_share, first_sum, last_sum, far, far_rest, *parts = phase(
+            b0,
+            b1,
+            their_share,
+            my_share,
+            first_sum,
+            last_sum,
+            far,
+            far_rest,
+            grads[0],
+            outputs[3],
+            *first_done,
+            *last_parts,
+        )
+        grads[0], outputs[3] = parts[:2]
+        their_share, b1 = swap(their_share, T, 1), swap(b1, T, 1)
+        first_sum, last_sum = z_sum(first_sum, parts[2:5]), z_sum(last_sum, parts[5:])
+        oud_grad = jnp.concatenate([first_sum, last_sum], axis=1).astype(bf16)
+        oud_far = oud_grad.reshape(-1, WEIGHTS, 2, cols)[:, :, 1]
+        my_share, their_share, b0, b1, oud_grad, oud_far = phase(
+            my_share, their_share, b0, b1, oud_grad, oud_far
+        )
+        oud_far = swap(oud_far, T, 2)
+        back = swap((b0.astype(f32) + b1.astype(f32)).astype(bf16), C, 1)
         shares = [my_share, their_share]
-        back = [beyond_share[:half], swap(beyond_share[half:], T, 1)]
         low, sums_later = finish(0, pre_vectors, row_tokens, grad_mixed, shares, [], half)
-        low, dq, sums_later, *parts = phase(low, dq, sums_later, *shares, *back)
-        shares = parts[:2]
-        back = swap((parts[2].astype(f32) + parts[3].astype(f32)).astype(bf16), C, 1)
-        pieces = [low, None, swap(low, T, 2), None]
-        *near, sums0 = near_back((lanes // 2,) * 2, everything, dq, None, far, far_rest)
-        near = [n.reshape(4, 2 * deep, lanes // 2) for n in near]
-        parts = [pick(n, z ^ i) for n in near for i in (1, 2, 3)]
-        near = [pick(n, z) for n in near]
-        near[0], near[1], sums0, *parts = phase(*near, sums0, *parts)
-        early, parts = z_moves(parts[:3]), parts[3:]
+        low, sums_later, shares[0], shares[1], oud_far, far, far_rest, g0, *outputs = phase(
+            low, sums_later, *shares, oud_far, far, far_rest, grads[0], *outputs
+        )
+        grads[0] = g0
+        pieces = [low, swap(low, T, 1), swap(low, T, 2), None]
+        widths = (5 * lanes // 8, 3 * lanes // 8)
+        *near, sums0, later_output, prompt_output = near_back(
+            grads, everything, widths, None, (far, far_rest), outputs
+        )
+        x_away, x_kept = x_parts(near[0], 0)
+        z_split = near[1].reshape(4, 2 * deep, widths[1])
+        parts, z_kept = [pick(z_split, z ^ i) for i in (1, 2, 3)], pick(z_split, z)
+        x_away, x_kept, z_kept, sums0, pieces[1], *parts = phase(
+            x_away, x_kept, z_kept, sums0, pieces[1], *parts
+        )
+        x_away = swap(x_away, C, 1)
+        z_away = z_moves(parts)
         back, pieces[2] = phase(back, pieces[2])
         pieces[3] = swap(pieces[2], T, 1)
         low, sums_prompt = finish(1, pre_vectors, row_tokens, grad_mixed, shares, [back], half)
     else:
-        beyond_share, their_share, my_share, near, sums0 = near_back(
-            (lanes,), everything, dq, shares, far, swap(far_rest, T, 2)
+        oud_grad = jnp.concatenate([p.astype(bf16) for p in oud_parts], axis=1)
+        b0, b1, their_share, my_share, near, sums0 = near_back(
+            grads, everything, (lanes,), shares, (far, far_rest)
         )
         shares = [my_share, swap(their_share, T, 1)]
-        back = beyond_share.astype(f32) + swap(beyond_share, T, 1).astype(f32)
+        back = jnp.concatenate([b0, b1])
+        back = back.astype(f32) + swap(back, T, 1).astype(f32)
         back = back.reshape(contexts - 1, prompt_rows, width)
         back = jnp.concatenate([jnp.zeros_like(back[:1]), back], axis=0)
         back = jnp.roll(back, x, axis=0).astype(bf16)
         back = lax.psum_scatter(back, C, scatter_dimension=0, tiled=True)
         back = pick(back.reshape(2, half, width), c)
         low, sums_later = finish(0, pre_vectors, row_tokens, grad_mixed, shares, [], half)
-        pieces = [low, swap(low, T, 1), swap(low, T, 2), None]
+        pieces = [low, None, swap(low, T, 2), None]
         low, sums_prompt = finish(1, pre_vectors, row_tokens, grad_mixed, shares, [back], half)
-        oud_grad = jnp.concatenate([p.astype(bf16) for p in oud_pieces], axis=1)
+        later_output = assemble(where, outputs, 0, half, bf16)
+        prompt_output = assemble(where, outputs, 1, half, bf16)
         qkv_grad, oud_grad = [
             lax.psum_scatter(g, SC, scatter_dimension=0, tiled=True) for g in (near, oud_grad)
         ]
@@ -1024,35 +1095,62 @@
     v_sums = placed(sums0[0, 2 * cols : 3 * cols], sums1[0, 2 * cols : 3 * cols])
     more = jnp.where(row == 2, q_sums[None], jnp.where(row == 3, v_sums[None], sums_later))
     if direct():
-        low, sums_prompt, sums, more, pieces[3], *rest = phase(
-            low, sums_prompt, sums, more, pieces[3], *early, *parts
-        )
-        near[0], parts = z_sum(near[0].astype(f32), rest[:3]), z_moves(rest[3:])
+        low, sums_prompt, sums, more, oud_grad, oud_far, x_away, x_kept, z_kept, *rest = phase(
+            low,
+            sums_prompt,
+            sums,
+            more,
+            oud_grad,
+            oud_far,
+            x_away,
+            x_kept,
+            z_kept,
+            *pieces,
+            *z_away,
+        )
+        pieces, z_away = rest[:4], rest[4:]
     sums = jnp.concatenate([sums, more + sums_prompt])
-    last = [low, None, swap(low, T, 2), None]
-    pieces[1] = swap(pieces[0], T, 1)
+    sums = sums + swap(sums, T, 2)
+    if direct():
+        low, sums = phase(low, sums)
+    last = [low, swap(low, T, 1), swap(low, T, 2), None]
+    if direct():
+        z_first = z_sum(z_kept.astype(f32), z_away).reshape(2, deep, widths[1])
+        z_away, z_first = pick(z_first, 1 - x).astype(bf16), pick(z_first, x)
+        parts, x_first = z_parts(x_kept.astype(f32) + x_away.astype(f32), 0)
+        z_away, z_first, x_first, pieces[0], *parts = phase(
+            z_away, z_first, x_first, pieces[0], *parts
+        )
+        parts = z_moves(parts)
+        arrived, z_away = swap(sums, T, 1), swap(z_away, C, 1)
+        later_grad = assemble(where, pieces, 0, half, f32)
+        later_grad, sums, arrived, z_away, last[1], x_first, *parts = phase(
+            later_grad, sums, arrived, z_away, last[1], x_first, *parts
+        )
+        sums = sums + arrived
+        sums, last[1], x_first, *parts = phase(sums, last[1], x_first, *parts)
+        arrived = swap(sums, C, 1)
+        prompt_grad = assemble(where, last[:2], 0, half, f32)
+        qkv_grad = jnp.concatenate(
+            [z_sum(x_first, parts), z_first + z_away.astype(f32)], axis=1
+        )
+        sums = sum_over(sums + arrived, S)
+        prompt_grad, sums, last[2], qkv_grad = phase(prompt_grad, sums, last[2], qkv_grad)
+    else:
+        pieces[1] = swap(pieces[0], T, 1)
+        pieces[3] = swap(pieces[2], T, 1)
+        later_grad = assemble(where, pieces, 0, half, f32)
+        prompt_grad = assemble(where, last[:2], 0, half, f32)
+        sums = sum_over(sum_over(sums + swap(sums, T, 1), C), S)
+    oud_grad = oud_grad.reshape(-1, WEIGHTS, 2, cols)
     if not direct():
-        pieces[3] = swap(pieces[2], T, 1)
-    later_grad = assemble(where, pieces, 0, half, f32)
-    later_output = assemble(where, outputs, 0, half, bf16)
-    prompt_output = assemble(where, outputs, 1, half, bf16)
-    if direct():
-        later_grad, later_output, prompt_output, near[0], near[1], sums, last[2], *parts = phase(
-            later_grad, later_output, prompt_output, *near, sums, last[2], *parts
-        )
-        near[1] = z_sum(near[1].astype(f32), parts)
-        split = jnp.concatenate(near, axis=1).reshape(2, deep, lanes)
-        away = swap(pick(split, 1 - x).astype(bf16), C, 1)
-        qkv_grad = pick(split, x) + away.astype(f32)
-    last[1] = swap(last[0], T, 1)
+        oud_far = swap(oud_grad[:, :, 1], T, 2)
+    oud_grad = oud_grad[:, :, 0].astype(f32) + oud_far.astype(f32)
     last[3] = swap(last[2], T, 1)
-    sums = sum_over(sum_over(sum_over(sums, C), S), T)
     squares = lax.dynamic_slice(sums[6], (lax.axis_index(S) * groups,), (groups,))
     counted = lax.dynamic_slice(sums[6], (every + lax.axis_index(S) * groups,), (groups,))
     magnitude = jnp.sqrt(squares / (counted * width))
-    oud_grad = oud_grad.reshape(-1, WEIGHTS, 2, cols)
-    oud_grad = oud_grad[:, :, 0].astype(f32) + swap(oud_grad[:, :, 1], T, 2).astype(f32)
-    prompt_grad = assemble(where, last, 0, half, f32)
+    prompt_grad = assemble(where, last[2:], 0, half, f32, 2, [prompt_grad])
     n = width // (lax.axis_size(S) * contexts)
     place = lax.axis_index(S) * contexts + x
 

time: 594 us -> 573 us (0.965)
  waiting for transfers between devices: 90.3 us -> 76 us
  Pallas kernels: 330 us -> 319 us
    ppermute x61 -> x62, waiting for transfers between devices: 90.3 us -> 76 us  [swap(): return lax.ppermute(value, axis, [(i, i ^ bit) for i in range(count)])]
    pallas_call x4 -> x3, Pallas kernels: 26.8 us -> 17.6 us  [assemble(): pl.pallas_call(functools.partial(assemble_kernel, count), grid_spec=pltpu...]
    squeeze x9 -> x11, local copies, waits for them, and re-layouts: 9.38 us -> 13.9 us  [pick(): return lax.dynamic_index_in_dim(array, index, axis, keepdims=False)]
    pallas_call x4 -> x3, Pallas kernels: 75 us -> 73.6 us  [project_back(): pl.pallas_call(functools.partial(project_back_kernel, len(sums), spans, l...]
    ppermute x61 -> x62, starting transfers between devices: 70.8 us -> 70.4 us  [swap(): return lax.ppermute(value, axis, [(i, i ^ bit) for i in range(count)])]
    dynamic_slice x8 -> x7, local copies, waits for them, and re-layouts: 12.1 us -> 11.9 us  [pick(): return lax.dynamic_index_in_dim(array, index, axis, keepdims=False)]
  transfers between devices with their start and end apart: 61 -> 62, of which waited for: 18 -> 17; matrix products, arithmetic and copies ran while one was open for 14% -> 15% of each run, Pallas kernels for 46% -> 46%
where the time goes in v2:
time: 573 us; the launch traced here: 567 us
  Pallas kernels  319 us (56%)
  waiting for transfers between devices  76 us (13%)
  starting transfers between devices  70.4 us (12%)
  local copies, waits for them, and re-layouts  61.8 us (11%)
  other arithmetic  38.3 us (7%)
    pallas_call x2, Pallas kernels, attend_back(): pl.pallas_call(functools.partial(attend_back_kernel, later, cont, first),...  77.7 us
    ppermute x62, waiting for transfers between devices, swap(): return lax.ppermute(value, axis, [(i, i ^ bit) for i in range(count)])  76 us
    pallas_call x3, Pallas kernels, project_back(): pl.pallas_call(functools.partial(project_back_kernel, len(sums), spans, l...  73.6 us
    ppermute x62, starting transfers between devices, swap(): return lax.ppermute(value, axis, [(i, i ^ bit) for i in range(count)])  70.4 us
    pallas_call x1, Pallas kernels, middle(): pl.pallas_call(functools.partial(middle_kernel, [w.shape[0] for w in weig...  53.1 us
    pallas_call x2, Pallas kernels, project(): pl.pallas_call(functools.partial(project_kernel, fresh, own, spans, [w.sh...  43.9 us
    pallas_call x2, Pallas kernels, attend(): pl.pallas_call(functools.partial(attend_kernel, later, cont), grid=(own /...  40.8 us
    pallas_call x3, Pallas kernels, assemble(): pl.pallas_call(functools.partial(assemble_kernel, count), grid_spec=pltpu...  17.6 us
  transfers between devices with their start and end apart: 62, of which 17 were waited for; matrix products, arithmetic and copies ran while one was open for 15% of the time, Pallas kernels for 46%

profile of v2, /device:TPU:0, one launch (start us, length us, event | category | flops | bytes accessed | tf_op | source)
XLA Modules:
  0.0 567.1 jit_solution(7253175813148870523)
XLA Ops:
  20.1 5.2 constant_dynamic-slice_fusion.15
  54.2 9.5 %collective-permute-done.7 = bf16[160,962]{1,0:T(8,128)(2,1)} collective-permute-done((bf16[160,962]{1,0:T(8,128)(2,1)S(1)}, bf16[160,962]{1,0:T(8,128)(2,1)}, u32[]{:S(2)}, u32[]{:S(2)}) %collective-permute-start.7) | collective-permute-done | bytes 307872 | tf_op jit(solution)/shard_map/ppermute | solution.py:710
  63.7 10.3 %collective-permute-done.8 = bf16[160,962]{1,0:T(8,128)(2,1)} collective-permute-done((bf16[160,962]{1,0:T(8,128)(2,1)S(1)}, bf16[160,962]{1,0:T(8,128)(2,1)}, u32[]{:S(2)}, u32[]{:S(2)}) %collective-permute-start.8) | collective-permute-done | bytes 307872 | tf_op jit(solution)/shard_map/ppermute | solution.py:710
  75.8 5.1 collective-permute-start.11
  85.5 25.8 %shard_map.356 = (bf16[2048,512]{1,0:T(8,128)(2,1)}, bf16[3072,512]{1,0:T(8,128)(2,1)}, bf16[3072,512]{1,0:T(8,128)(2,1)}, bf16[3072,1280]{1,0:T(8,128)(2,1)}, f32[8,1280]{1,0:T(8,128)}) custom-call(s32[16]{0:T(128)} %stack.162.info, bf16[2,1024,1280]{2,1,0:T(8,128)(2,1)} %bitcast.180, bf16[2,1024,1280]{2,1,0:T(8,128)(2,1)} %refs_1_.1, ...), custom_call_target="tpu_custom_call" | custom-call | flops 28185722880 | bytes 31457280 | tf_op jit(solution)/shard_map/pallas_call | solution.py:163
  117.7 20.3 %shard_map.357 = (bf16[2048,320]{1,0:T(8,128)(2,1)}, f32[2048,128]{1,0:T(8,128)}) custom-call(bf16[2048,512]{1,0:T(8,128)(2,1)} %get-tuple-element.269.q_ref, bf16[3072,512]{1,0:T(8,128)(2,1)} %get-tuple-element.270.k_ref, bf16[3072,512]{1,0:T(8,128)(2,1)} %get-tuple-element.271.v_ref), custom_call_target="tpu_custom_call" | custom-call | flops 12884901888 | bytes 8388608 | tf_op jit(solution)/shard_map/pallas_call | solution.py:229
  138.0 6.4 %collective-permute-done.14.refs_6_ = bf16[4,160,964]{2,1,0:T(8,128)(2,1)} collective-permute-done((bf16[4,160,964]{2,1,0:T(8,128)(2,1)S(1)}, bf16[4,160,964]{2,1,0:T(8,128)(2,1)}, u32[]{:S(2)}, u32[]{:S(2)}) %collective-permute-start.14) | collective-permute-done | bytes 1233952 | tf_op jit(solution)/shard_map/ppermute | solution.py:710
  147.9 18.1 %shard_map.358 = (bf16[2048,512]{1,0:T(8,128)(2,1)}, bf16[3072,512]{1,0:T(8,128)(2,1)}, bf16[3072,512]{1,0:T(8,128)(2,1)}) custom-call(s32[16]{0:T(128)} %stack.162.info, bf16[3072,1280]{1,0:T(8,128)(2,1)} %get-tuple-element.264.refs_0_, bf16[4,160,962]{2,1,0:T(8,128)(2,1)} %copy-done.5, bf16[4,160,962]{2,1,0:T(8,128)(2,1)} %copy-done.11, ...), custom_call_target="tpu_custom_call" | custom-call | flops 28185722880 | bytes 31457280 | tf_op jit(solution)/shard_map/pallas_call | solution.py:163
  166.0 20.5 %shard_map.359 = (bf16[2048,320]{1,0:T(8,128)(2,1)}, f32[2048,128]{1,0:T(8,128)}) custom-call(bf16[2048,512]{1,0:T(8,128)(2,1)} %get-tuple-element.285.q_ref, bf16[3072,512]{1,0:T(8,128)(2,1)} %get-tuple-element.286.k_ref, bf16[3072,512]{1,0:T(8,128)(2,1)} %get-tuple-element.287.v_ref), custom_call_target="tpu_custom_call" | custom-call | flops 12884901888 | bytes 8388608 | tf_op jit(solution)/shard_map/pallas_call | solution.py:229
  192.7 53.1 %shard_map.360 = (bf16[1024,1280]{1,0:T(8,128)(2,1)}, f32[1024,1280]{1,0:T(8,128)}, bf16[1024,640]{1,0:T(8,128)(2,1)}, bf16[1024,640]{1,0:T(8,128)(2,1)}, f32[8,...) custom-call(s32[9]{0:T(128)} %stack.173.info, bf16[1024,1280]{1,0:T(8,128)(2,1)} %bitcast.154, ...), custom_call_target="tpu_custom_call" | custom-call | flops 62075699200 | bytes 39321600 | tf_op jit(solution)/shard_map/pallas_call | solution.py:408
  254.5 39.0 %shard_map.361 = (bf16[2048,320]{1,0:T(8,128)(2,1)}, bf16[3072,320]{1,0:T(8,128)(2,1)}, bf16[3072,320]{1,0:T(8,128)(2,1)}) custom-call(bf16[2048,512]{1,0:T(8,128)(2,1)} %get-tuple-element.285.q_ref, bf16[3072,512]{1,0:T(8,128)(2,1)} %get-tuple-element.286.k_ref, bf16[3072,512]{1,0:T(8,128)(2,1)} %get-tuple-element.287.v_ref, ...), custom_call_target="tpu_custom_call" | custom-call | flops 1000 | bytes 1000 | tf_op jit(solution)/shard_map/pallas_call | solution.py:301
  302.8 33.1 %shard_map.362 = (bf16[512,1280]{1,0:T(8,128)(2,1)}, bf16[512,1280]{1,0:T(8,128)(2,1)}, bf16[1024,1280]{1,0:T(8,128)(2,1)}, bf16[1024,1280]{1,0:T(8,128)(2,1)}, ...) custom-call(s32[11]{0:T(128)} %stack.78.info, ...), custom_call_target="tpu_custom_call" | custom-call | flops 1000 | bytes 1000 | tf_op jit(solution)/shard_map/pallas_call | solution.py:613
  344.8 38.7 %shard_map.363 = (bf16[2048,320]{1,0:T(8,128)(2,1)}, bf16[3072,320]{1,0:T(8,128)(2,1)}, bf16[3072,320]{1,0:T(8,128)(2,1)}) custom-call(bf16[2048,512]{1,0:T(8,128)(2,1)} %get-tuple-element.269.q_ref, bf16[3072,512]{1,0:T(8,128)(2,1)} %get-tuple-element.270.k_ref, bf16[3072,512]{1,0:T(8,128)(2,1)} %get-tuple-element.271.v_ref, ...), custom_call_target="tpu_custom_call" | custom-call | flops 1000 | bytes 1000 | tf_op jit(solution)/shard_map/pallas_call | solution.py:301
  391.8 19.5 %shard_map.364 = (bf16[512,1280]{1,0:T(8,128)(2,1)}, bf16[512,1280]{1,0:T(8,128)(2,1)}, bf16[1024,1280]{1,0:T(8,128)(2,1)}, bf16[1024,1280]{1,0:T(8,128)(2,1)}) custom-call(s32[11]{0:T(128)} %stack.78.info, bf16[3072,1280]{1,0:T(8,128)(2,1)} %get-tuple-element.264.refs_0_, bf16[2048,320]{1,0:T(8,128)(2,1)} %get-tuple-element.388.refs_1_, ...), custom_call_target="tpu_custom_call" | custom-call | flops 1000 | bytes 1000 | tf_op jit(solution)/shard_map/pallas_call | solution.py:613
  424.9 5.7 %shard_map.365 = (bf16[512,1280]{1,0:T(8,128)(2,1)}, f32[8,1280]{1,0:T(8,128)}) custom-call(f32[8,1280]{1,0:T(8,128)} %get-tuple-element.265.gain_ref, bf16[1024,1280]{1,0:T(8,128)(2,1)} %bitcast.155, f32[1024,1280]{1,0:T(8,128)} %get-tuple-element.296.mix_ref, bf16[1024,1280]{1,0:T(8,128)(2,1)} %get-tuple-element.397.refs_0_, bf16[1024,1280]{1,0:T(8,128)(2,1)} %copy-done.4), custom_call_target="tpu_custom_call" | custom-call | flops 1000 | bytes 1000 | tf_op jit(solution)/shard_map/pallas_call | solution.py:663
  435.9 21.0 %shard_map.366 = (bf16[1280,640]{1,0:T(8,128)(2,1)}, bf16[1280,384]{1,0:T(8,128)(2,1)}, f32[8,1024]{1,0:T(8,128)}, bf16[2,1024,1280]{2,1,0:T(8,128)(2,1)}, bf16[2,1024,1280]{2,1,0:T(8,128)(2,1)}) custom-call(s32[11]{0:T(128)} %stack.78.info, bf16[3072,1280]{1,0:T(8,128)(2,1)} %get-tuple-element.264.refs_0_, bf16[2048,320]{1,0:T(8,128)(2,1)} %get-tuple-element.388.refs_1_, ...), custom_call_target="tpu_custom_call" | custom-call | flops 1000 | bytes 1000 | tf_op jit(solution)/shard_map/pallas_call | solution.py:613
  464.2 5.0 collective-permute-start.47
  471.6 6.3 %shard_map.367 = (bf16[512,1280]{1,0:T(8,128)(2,1)}, f32[8,1280]{1,0:T(8,128)}) custom-call(f32[8,1280]{1,0:T(8,128)} %get-tuple-element.265.gain_ref, bf16[1024,1280]{1,0:T(8,128)(2,1)} %bitcast.156, f32[1024,1280]{1,0:T(8,128)} %get-tuple-element.296.mix_ref, bf16[1024,1280]{1,0:T(8,128)(2,1)} %get-tuple-element.397.refs_0_, bf16[1024,1280]{1,0:T(8,128)(2,1)} %copy-done.4, ...), custom_call_target="tpu_custom_call" | custom-call | flops 1000 | bytes 1000 | tf_op jit(solution)/shard_map/pallas_call | solution.py:663
  480.2 9.7 %collective-permute-done.48 = bf16[320,384]{1,0:T(8,128)(2,1)} collective-permute-done((bf16[320,384]{1,0:T(8,128)(2,1)}, bf16[320,384]{1,0:T(8,128)(2,1)}, u32[]{:S(2)}, u32[]{:S(2)}) %collective-permute-start.48) | collective-permute-done | bytes 245792 | tf_op jit(solution)/shard_map/ppermute | solution.py:710
  507.3 7.6 %shard_map.368 = f32[2,1024,1280]{2,1,0:T(8,128)} custom-call(s32[2]{0:T(128)} %pad_add_fusion.info, bf16[512,1280]{1,0:T(8,128)(2,1)} %get-tuple-element.434.refs_0_, bf16[512,1280]{1,0:T(8,128)(2,1)} %collective-permute-done.44.refs_1_, bf16[512,1280]{1,0:T(8,128)(2,1)} %copy-done.10, bf16[512,1280]{1,0:T(8,128)(2,1)} %collective-permute-done.46.refs_3_), custom_call_target="tpu_custom_call" | custom-call | flops 1000 | bytes 1000 | tf_op jit(solution)/shard_map/pallas_call | solution.py:689
  518.3 13.6 %collective-permute-done.55 = bf16[160,640]{1,0:T(8,128)(2,1)S(1)} collective-permute-done((bf16[160,640]{1,0:T(8,128)(2,1)S(1)}, bf16[160,640]{1,0:T(8,128)(2,1)S(1)}, u32[]{:S(2)}, u32[]{:S(2)}) %collective-permute-start.55) | collective-permute-done | bytes 204832 | tf_op jit(solution)/shard_map/ppermute | solution.py:710
  536.4 5.0 collective-permute-start.58
  548.1 5.0 collective-permute-done.59
  561.8 5.1 shard_map.370
  (314 shorter events, 176.5 us)
Async XLA Ops:
  5.1 33.9 %collective-permute-start.2 = (bf16[160,962]{1,0:T(8,128)(2,1)S(1)}, bf16[160,962]{1,0:T(8,128)(2,1)}, u32[]{:S(2)}, u32[]{:S(2)}) collective-permute-start(bf16[160,962]{1,0:T(8,128)(2,1)S(1)} %concatenate.47), channel_id=1, source_target_pairs={{0,8},{8,0},{16,24},{24,16},{1,9},{9,1},{17,25},{25,17},{2,10},{10... | collective-permute-start | bytes 923528 | tf_op jit(solution)/shard_map/ppermute | solution.py:710
  8.2 30.8 %collective-permute-start.3 = (bf16[160,962]{1,0:T(8,128)(2,1)S(1)}, bf16[160,962]{1,0:T(8,128)(2,1)}, u32[]{:S(2)}, u32[]{:S(2)}) collective-permute-start(bf16[160,962]{1,0:T(8,128)(2,1)S(1)} %concatenate.47), channel_id=1, source_target_pairs={{0,16},{8,24},{16,0},{24,8},{1,17},{9,25},{17,1},{25,9},{2,18},{10... | collective-permute-start | bytes 923528 | tf_op jit(solution)/shard_map/ppermute | solution.py:710
  13.4 29.8 %collective-permute-start.1 = (bf16[512,1280]{1,0:T(8,128)(2,1)}, bf16[512,1280]{1,0:T(8,128)(2,1)}, u32[]{:S(2)}, u32[]{:S(2)}) collective-permute-start(bf16[512,1280]{1,0:T(8,128)(2,1)} %dynamic-slice_bitcast_fusion.2), channel_id=1, source_target_pairs={{0,4},{4,0},{1,5},{5,1},{2,6},{6,2},{3,7},{7,3},{8,12},{12,8},{9,1... | collective-permute-start | bytes 3932168 | tf_op jit(solution)/shard_map/ppermute | solution.py:710
  43.2 32.6 %collective-permute-start.6 = (bf16[512,1280]{1,0:T(8,128)(2,1)}, bf16[512,1280]{1,0:T(8,128)(2,1)}, u32[]{:S(2)}, u32[]{:S(2)}) collective-permute-start(bf16[512,1280]{1,0:T(8,128)(2,1)} %collective-permute-done.1.refs_2_), channel_id=1, source_target_pairs={{0,1},{1,0},{2,3},{3,2},{4,5},{5,4},{6,7},{7,6},{8,9},{9,8},{10,11... | collective-permute-start | bytes 3932168 | tf_op jit(solution)/shard_map/ppermute | solution.py:710
  44.5 31.3 %collective-permute-start.5 = (bf16[4,160,962]{2,1,0:T(8,128)(2,1)S(1)}, bf16[4,160,962]{2,1,0:T(8,128)(2,1)S(1)}, u32[]{:S(2)}, u32[]{:S(2)}) collective-permute-start(bf16[4,160,962]{2,1,0:T(8,128)(2,1)S(1)} %pad_maximum_fusion.3.refs_4_), channel_id=1, source_target_pairs={{0,4},{4,0},{1,5},{5,1},{2,6},{6,2},{3,7},{7,3},{8,12},{12,8},{9,1... | collective-permute-start | bytes 3694088 | tf_op jit(solution)/shard_map/ppermute | solution.py:710
  63.7 53.3 %collective-permute-start.20 = (f32[2,320]{1,0:T(2,128)S(1)}, f32[2,320]{1,0:T(2,128)S(1)}, u32[]{:S(2)}, u32[]{:S(2)}) collective-permute-start(f32[2,320]{1,0:T(2,128)S(1)} %fusion.13), channel_id=1, source_target_pairs={{0,1},{1,0},{2,3},{3,2},{4,5},{5,4},{6,7},{7,6},{8,9},{9,8},{10,11... | collective-permute-start | bytes 7688 | tf_op jit(solution)/shard_map/ppermute | solution.py:710
  75.8 35.5 %collective-permute-start.11 = (bf16[160,964]{1,0:T(8,128)(2,1)S(1)}, bf16[160,964]{1,0:T(8,128)(2,1)S(1)}, u32[]{:S(2)}, u32[]{:S(2)}) collective-permute-start(bf16[160,964]{1,0:T(8,128)(2,1)S(1)} %concatenate.50), channel_id=1, source_target_pairs={{0,8},{8,0},{16,24},{24,16},{1,9},{9,1},{17,25},{25,17},{2,10},{10... | collective-permute-start | bytes 925448 | tf_op jit(solution)/shard_map/ppermute | solution.py:710
  80.9 30.4 %collective-permute-start.12 = (bf16[160,964]{1,0:T(8,128)(2,1)S(1)}, bf16[160,964]{1,0:T(8,128)(2,1)S(1)}, u32[]{:S(2)}, u32[]{:S(2)}) collective-permute-start(bf16[160,964]{1,0:T(8,128)(2,1)S(1)} %concatenate.50), channel_id=1, source_target_pairs={{0,16},{8,24},{16,0},{24,8},{1,17},{9,25},{17,1},{25,9},{2,18},{10... | collective-permute-start | bytes 925448 | tf_op jit(solution)/shard_map/ppermute | solution.py:710
  84.7 29.6 %collective-permute-start.10 = (bf16[4,160,962]{2,1,0:T(8,128)(2,1)S(1)}, bf16[4,160,962]{2,1,0:T(8,128)(2,1)S(1)}, u32[]{:S(2)}, u32[]{:S(2)}) collective-permute-start(bf16[4,160,962]{2,1,0:T(8,128)(2,1)S(1)} %pad_maximum_fusion.4.refs_1_.refs_4_), channel_id=1, source_target_pairs={{0,4},{4,0},{1,5},{5,1},{2,6},{6,2},{3,7},{7,3},{8,12},{12,8},{9,1... | collective-permute-start | bytes 3694088 | tf_op jit(solution)/shard_map/ppermute | solution.py:710
  144.6 41.9 %collective-permute-start.21 = (bf16[4,160,964]{2,1,0:T(8,128)(2,1)}, bf16[4,160,964]{2,1,0:T(8,128)(2,1)}, u32[]{:S(2)}, u32[]{:S(2)}) collective-permute-start(bf16[4,160,964]{2,1,0:T(8,128)(2,1)} %collective-permute-done.14.refs_6_), channel_id=1, source_target_pairs={{0,4},{4,0},{1,5},{5,1},{2,6},{6,2},{3,7},{7,3},{8,12},{12,8},{9,1... | collective-permute-start | bytes 3701768 | tf_op jit(solution)/shard_map/ppermute | solution.py:710
  252.5 41.0 %collective-permute-start.25 = (bf16[1280,1920]{1,0:T(8,128)(2,1)}, bf16[1280,1920]{1,0:T(8,128)(2,1)}, u32[]{:S(2)}, u32[]{:S(2)}) collective-permute-start(bf16[1280,1920]{1,0:T(8,128)(2,1)} %get-tuple-element.308), channel_id=1, source_target_pairs={{0,1},{1,0},{2,3},{3,2},{4,5},{5,4},{6,7},{7,6},{8,9},{9,8},{10,11... | collective-permute-start | bytes 14745608 | tf_op jit(solution)/shard_map/ppermute | solution.py:710
  252.8 83.1 %collective-permute-start.27 = (bf16[1024,1280]{1,0:T(8,128)(2,1)}, bf16[1024,1280]{1,0:T(8,128)(2,1)}, u32[]{:S(2)}, u32[]{:S(2)}) collective-permute-start(bf16[1024,1280]{1,0:T(8,128)(2,1)} %get-tuple-element.391.refs_8_), channel_id=1, source_target_pairs={{0,1},{1,0},{2,3},{3,2},{4,5},{5,4},{6,7},{7,6},{8,9},{9,8},{10,11... | collective-permute-start | bytes 7864328 | tf_op jit(solution)/shard_map/ppermute | solution.py:710
  253.0 82.9 %collective-permute-start.28 = (bf16[1024,1280]{1,0:T(8,128)(2,1)}, bf16[1024,1280]{1,0:T(8,128)(2,1)}, u32[]{:S(2)}, u32[]{:S(2)}) collective-permute-start(bf16[1024,1280]{1,0:T(8,128)(2,1)} %get-tuple-element.391.refs_8_), channel_id=1, source_target_pairs={{0,2},{1,3},{2,0},{3,1},{4,6},{5,7},{6,4},{7,5},{8,10},{9,11},{10,... | collective-permute-start | bytes 7864328 | tf_op jit(solution)/shard_map/ppermute | solution.py:710
  301.1 34.8 %collective-permute-start.26 = (bf16[4,160,1024]{2,1,0:T(8,128)(2,1)}, bf16[4,160,1024]{2,1,0:T(8,128)(2,1)}, u32[]{:S(2)}, u32[]{:S(2)}) collective-permute-start(bf16[4,160,1024]{2,1,0:T(8,128)(2,1)} %get-tuple-element.319), channel_id=1, source_target_pairs={{0,4},{4,0},{1,5},{5,1},{2,6},{6,2},{3,7},{7,3},{8,12},{12,8},{9,1... | collective-permute-start | bytes 3932168 | tf_op jit(solution)/shard_map/ppermute | solution.py:710
  338.9 44.7 %collective-permute-start.29 = (bf16[1280,768]{1,0:T(8,128)(2,1)}, bf16[1280,768]{1,0:T(8,128)(2,1)S(1)}, u32[]{:S(2)}, u32[]{:S(2)}) collective-permute-start(bf16[1280,768]{1,0:T(8,128)(2,1)} %get-tuple-element.331), channel_id=1, source_target_pairs={{0,2},{1,3},{2,0},{3,1},{4,6},{5,7},{6,4},{7,5},{8,10},{9,11},{10,... | collective-permute-start | bytes 5898248 | tf_op jit(solution)/shard_map/ppermute | solution.py:710
  339.4 44.1 %collective-permute-start.30 = (bf16[4,160,896]{2,1,0:T(8,128)(2,1)S(1)}, bf16[4,160,896]{2,1,0:T(8,128)(2,1)S(1)}, u32[]{:S(2)}, u32[]{:S(2)}) collective-permute-start(bf16[4,160,896]{2,1,0:T(8,128)(2,1)S(1)} %copy-done.16), channel_id=1, source_target_pairs={{0,4},{4,0},{1,5},{5,1},{2,6},{6,2},{3,7},{7,3},{8,12},{12,8},{9,1... | collective-permute-start | bytes 3440648 | tf_op jit(solution)/shard_map/ppermute | solution.py:710
  340.4 43.1 %collective-permute-start.31 = (bf16[160,1024]{1,0:T(8,128)(2,1)}, bf16[160,1024]{1,0:T(8,128)(2,1)}, u32[]{:S(2)}, u32[]{:S(2)}) collective-permute-start(bf16[160,1024]{1,0:T(8,128)(2,1)} %get-tuple-element.336), channel_id=1, source_target_pairs={{0,8},{8,0},{16,24},{24,16},{1,9},{9,1},{17,25},{25,17},{2,10},{10... | collective-permute-start | bytes 983048 | tf_op jit(solution)/shard_map/ppermute | solution.py:710
  340.9 42.6 %collective-permute-start.32 = (bf16[160,1024]{1,0:T(8,128)(2,1)}, bf16[160,1024]{1,0:T(8,128)(2,1)}, u32[]{:S(2)}, u32[]{:S(2)}) collective-permute-start(bf16[160,1024]{1,0:T(8,128)(2,1)} %get-tuple-element.337), channel_id=1, source_target_pairs={{0,16},{8,24},{16,0},{24,8},{1,17},{9,25},{17,1},{25,9},{2,18},{10... | collective-permute-start | bytes 983048 | tf_op jit(solution)/shard_map/ppermute | solution.py:710
  343.4 40.1 %collective-permute-start.33 = (bf16[160,1024]{1,0:T(8,128)(2,1)}, bf16[160,1024]{1,0:T(8,128)(2,1)}, u32[]{:S(2)}, u32[]{:S(2)}) collective-permute-start(bf16[160,1024]{1,0:T(8,128)(2,1)} %get-tuple-element.338), channel_id=1, source_target_pairs={{0,24},{8,16},{16,8},{24,0},{1,25},{9,17},{17,9},{25,1},{2,26},{10... | collective-permute-start | bytes 983048 | tf_op jit(solution)/shard_map/ppermute | solution.py:710
  423.8 35.6 %collective-permute-start.42 = (bf16[512,1280]{1,0:T(8,128)(2,1)}, bf16[512,1280]{1,0:T(8,128)(2,1)}, u32[]{:S(2)}, u32[]{:S(2)}) collective-permute-start(bf16[512,1280]{1,0:T(8,128)(2,1)} %add_convert_fusion), channel_id=1, source_target_pairs={{0,4},{4,0},{1,5},{5,1},{2,6},{6,2},{3,7},{7,3},{8,12},{12,8},{9,1... | collective-permute-start | bytes 3932168 | tf_op jit(solution)/shard_map/ppermute | solution.py:710
  431.6 30.6 %collective-permute-start.43 = (bf16[512,1280]{1,0:T(8,128)(2,1)}, bf16[512,1280]{1,0:T(8,128)(2,1)S(1)}, u32[]{:S(2)}, u32[]{:S(2)}) collective-permute-start(bf16[512,1280]{1,0:T(8,128)(2,1)} %get-tuple-element.434.refs_0_), channel_id=1, source_target_pairs={{0,2},{1,3},{2,0},{3,1},{4,6},{5,7},{6,4},{7,5},{8,10},{9,11},{10,... | collective-permute-start | bytes 3932168 | tf_op jit(solution)/shard_map/ppermute | solution.py:710
  432.5 30.7 %collective-permute-start.44 = (bf16[512,1280]{1,0:T(8,128)(2,1)}, bf16[512,1280]{1,0:T(8,128)(2,1)}, u32[]{:S(2)}, u32[]{:S(2)}) collective-permute-start(bf16[512,1280]{1,0:T(8,128)(2,1)} %get-tuple-element.434.refs_0_), channel_id=1, source_target_pairs={{0,1},{1,0},{2,3},{3,2},{4,5},{5,4},{6,7},{7,6},{8,9},{9,8},{10,11... | collective-permute-start | bytes 3932168 | tf_op jit(solution)/shard_map/ppermute | solution.py:710
  495.2 36.7 %collective-permute-start.53 = (bf16[512,1280]{1,0:T(8,128)(2,1)}, bf16[512,1280]{1,0:T(8,128)(2,1)}, u32[]{:S(2)}, u32[]{:S(2)}) collective-permute-start(bf16[512,1280]{1,0:T(8,128)(2,1)} %get-tuple-element.426.refs_0_), channel_id=1, source_target_pairs={{0,1},{1,0},{2,3},{3,2},{4,5},{5,4},{6,7},{7,6},{8,9},{9,8},{10,11... | collective-permute-start | bytes 3932168 | tf_op jit(solution)/shard_map/ppermute | solution.py:710
  497.5 55.6 %collective-permute-start.60 = (bf16[512,1280]{1,0:T(8,128)(2,1)}, bf16[512,1280]{1,0:T(8,128)(2,1)S(1)}, u32[]{:S(2)}, u32[]{:S(2)}) collective-permute-start(bf16[512,1280]{1,0:T(8,128)(2,1)} %get-tuple-element.426.refs_0_), channel_id=1, source_target_pairs={{0,2},{1,3},{2,0},{3,1},{4,6},{5,7},{6,4},{7,5},{8,10},{9,11},{10,... | collective-permute-start | bytes 3932168 | tf_op jit(solution)/shard_map/ppermute | solution.py:710
  (78 other events, 1057.6 us)

commit v3 on v2

--- a/solution.py
+++ b/solution.py
@@ -705,6 +705,20 @@
     )(info, *pieces, *into)
 
 
+def rows_kernel(n, one_ref, two_ref, *outs):
+    for i, out in enumerate(outs):
+        out[...] = one_ref[i, :] if i < n else two_ref[i - n, :]
+
+
+def rows_of(one, two):
+    shapes = [(one.shape[1],)] * one.shape[0] + [(two.shape[1],)] * two.shape[0]
+    return pl.pallas_call(
+        functools.partial(rows_kernel, one.shape[0]),
+        out_shape=[jax.ShapeDtypeStruct(s, f32) for s in shapes],
+        cost_estimate=cost(1000, 1000),
+    )(one, two)
+
+
 def swap(value, axis, bit):
     count = lax.axis_size(axis)
     return lax.ppermute(value, axis, [(i, i ^ bit) for i in range(count)])
@@ -1122,12 +1136,12 @@
             z_away, z_first, x_first, pieces[0], *parts
         )
         parts = z_moves(parts)
-        arrived, z_away = swap(sums, T, 1), swap(z_away, C, 1)
         later_grad = assemble(where, pieces, 0, half, f32)
-        later_grad, sums, arrived, z_away, last[1], x_first, *parts = phase(
-            later_grad, sums, arrived, z_away, last[1], x_first, *parts
-        )
-        sums = sums + arrived
+        later_grad, sums, last[1], z_away, x_first, *parts = phase(
+            later_grad, sums, last[1], z_away, x_first, *parts
+        )
+        z_away = swap(z_away, C, 1)
+        sums = sums + swap(sums, T, 1)
         sums, last[1], x_first, *parts = phase(sums, last[1], x_first, *parts)
         arrived = swap(sums, C, 1)
         prompt_grad = assemble(where, last[:2], 0, half, f32)
@@ -1154,12 +1168,9 @@
     n = width // (lax.axis_size(S) * contexts)
     place = lax.axis_index(S) * contexts + x
 
-    def own_vector(row):
-        return lax.dynamic_slice(row, (place * n,), (n,))
-
-    def own_heads(row):
-        return lax.dynamic_slice(row, (t * cols,), (cols,))
-
+    vectors = lax.dynamic_slice(sums, (0, place * n), (10, n))
+    heads = lax.dynamic_slice(sums, (7, t * cols), (5, cols))
+    rows = rows_of(vectors, heads)
     shaped = (groups, count, cont, width)
     return (
         prompt_output,
@@ -1172,15 +1183,15 @@
         oud_grad[:, 0].T,
         oud_grad[:, 1],
         oud_grad[:, 2].T,
-        own_vector(sums[8]),
-        own_vector(sums[9]),
-        own_vector(sums[2]),
-        own_vector(sums[3]),
-        own_heads(sums[10]),
-        own_heads(sums[11]),
-        own_vector(sums[4]),
-        own_heads(sums[7]),
-        own_vector(sums[1]),
+        rows[8],
+        rows[9],
+        rows[2],
+        rows[3],
+        rows[13],
+        rows[14],
+        rows[4],
+        rows[10],
+        rows[1],
         magnitude,
     )
 

time: 573 us -> 558 us (0.974)
  waiting for transfers between devices: 76 us -> 68.1 us
  local copies, waits for them, and re-layouts: 61.8 us -> 54 us
    ppermute x62, waiting for transfers between devices: 76 us -> 68.1 us  [swap(): return lax.ppermute(value, axis, [(i, i ^ bit) for i in range(count)])]
  transfers between devices with their start and end apart: 62 -> 62, of which waited for: 17 -> 18; matrix products, arithmetic and copies ran while one was open for 15% -> 13% of each run, Pallas kernels for 46% -> 47%
where the time goes in v3:
time: 558 us; the launch traced here: 552 us
  Pallas kernels  320 us (57%)
  starting transfers between devices  71.7 us (13%)
  waiting for transfers between devices  68.1 us (12%)
  local copies, waits for them, and re-layouts  54 us (10%)
  other arithmetic  36.6 us (7%)
    pallas_call x2, Pallas kernels, attend_back(): pl.pallas_call(functools.partial(attend_back_kernel, later, cont, first),...  77.7 us
    pallas_call x3, Pallas kernels, project_back(): pl.pallas_call(functools.partial(project_back_kernel, len(sums), spans, l...  73.6 us
    ppermute x62, starting transfers between devices, swap(): return lax.ppermute(value, axis, [(i, i ^ bit) for i in range(count)])  71.7 us
    ppermute x62, waiting for transfers between devices, swap(): return lax.ppermute(value, axis, [(i, i ^ bit) for i in range(count)])  68.1 us
    pallas_call x1, Pallas kernels, middle(): pl.pallas_call(functools.partial(middle_kernel, [w.shape[0] for w in weig...  53.2 us
    pallas_call x2, Pallas kernels, project(): pl.pallas_call(functools.partial(project_kernel, fresh, own, spans, [w.sh...  43.9 us
    pallas_call x2, Pallas kernels, attend(): pl.pallas_call(functools.partial(attend_kernel, later, cont), grid=(own /...  40.8 us
    pallas_call x3, Pallas kernels, assemble(): pl.pallas_call(functools.partial(assemble_kernel, count), grid_spec=pltpu...  17.5 us
  transfers between devices with their start and end apart: 62, of which 18 were waited for; matrix products, arithmetic and copies ran while one was open for 13% of the time, Pallas kernels for 47%

profile of v3, /device:TPU:0, one launch (start us, length us, event | category | flops | bytes accessed | tf_op | source)
XLA Modules:
  0.0 552.2 jit_solution(9904471092638210950)
XLA Ops:
  20.1 5.2 constant_dynamic-slice_fusion.7
  54.2 9.5 %collective-permute-done.7 = bf16[160,962]{1,0:T(8,128)(2,1)} collective-permute-done((bf16[160,962]{1,0:T(8,128)(2,1)S(1)}, bf16[160,962]{1,0:T(8,128)(2,1)}, u32[]{:S(2)}, u32[]{:S(2)}) %collective-permute-start.7) | collective-permute-done | bytes 307872 | tf_op jit(solution)/shard_map/ppermute | solution.py:724
  63.7 10.3 %collective-permute-done.8 = bf16[160,962]{1,0:T(8,128)(2,1)} collective-permute-done((bf16[160,962]{1,0:T(8,128)(2,1)S(1)}, bf16[160,962]{1,0:T(8,128)(2,1)}, u32[]{:S(2)}, u32[]{:S(2)}) %collective-permute-start.8) | collective-permute-done | bytes 307872 | tf_op jit(solution)/shard_map/ppermute | solution.py:724
  75.8 5.1 collective-permute-start.11
  85.5 25.9 %shard_map.356 = (bf16[2048,512]{1,0:T(8,128)(2,1)}, bf16[3072,512]{1,0:T(8,128)(2,1)}, bf16[3072,512]{1,0:T(8,128)(2,1)}, bf16[3072,1280]{1,0:T(8,128)(2,1)}, f32[8,1280]{1,0:T(8,128)}) custom-call(s32[16]{0:T(128)} %stack.162.info, bf16[2,1024,1280]{2,1,0:T(8,128)(2,1)} %bitcast.174, bf16[2,1024,1280]{2,1,0:T(8,128)(2,1)} %refs_1_.1, ...), custom_call_target="tpu_custom_call" | custom-call | flops 28185722880 | bytes 31457280 | tf_op jit(solution)/shard_map/pallas_call | solution.py:163
  117.7 20.2 %shard_map.357 = (bf16[2048,320]{1,0:T(8,128)(2,1)}, f32[2048,128]{1,0:T(8,128)}) custom-call(bf16[2048,512]{1,0:T(8,128)(2,1)} %get-tuple-element.277.q_ref, bf16[3072,512]{1,0:T(8,128)(2,1)} %get-tuple-element.278.k_ref, bf16[3072,512]{1,0:T(8,128)(2,1)} %get-tuple-element.279.v_ref), custom_call_target="tpu_custom_call" | custom-call | flops 12884901888 | bytes 8388608 | tf_op jit(solution)/shard_map/pallas_call | solution.py:229
  137.9 6.5 %collective-permute-done.14.refs_6_ = bf16[4,160,964]{2,1,0:T(8,128)(2,1)} collective-permute-done((bf16[4,160,964]{2,1,0:T(8,128)(2,1)S(1)}, bf16[4,160,964]{2,1,0:T(8,128)(2,1)}, u32[]{:S(2)}, u32[]{:S(2)}) %collective-permute-start.14) | collective-permute-done | bytes 1233952 | tf_op jit(solution)/shard_map/ppermute | solution.py:724
  147.9 18.1 %shard_map.358 = (bf16[2048,512]{1,0:T(8,128)(2,1)}, bf16[3072,512]{1,0:T(8,128)(2,1)}, bf16[3072,512]{1,0:T(8,128)(2,1)}) custom-call(s32[16]{0:T(128)} %stack.162.info, bf16[3072,1280]{1,0:T(8,128)(2,1)} %get-tuple-element.272.refs_0_, bf16[4,160,962]{2,1,0:T(8,128)(2,1)} %copy-done.5, bf16[4,160,962]{2,1,0:T(8,128)(2,1)} %copy-done.9, ...), custom_call_target="tpu_custom_call" | custom-call | flops 28185722880 | bytes 31457280 | tf_op jit(solution)/shard_map/pallas_call | solution.py:163
  166.0 20.5 %shard_map.359 = (bf16[2048,320]{1,0:T(8,128)(2,1)}, f32[2048,128]{1,0:T(8,128)}) custom-call(bf16[2048,512]{1,0:T(8,128)(2,1)} %get-tuple-element.293.q_ref, bf16[3072,512]{1,0:T(8,128)(2,1)} %get-tuple-element.294.k_ref, bf16[3072,512]{1,0:T(8,128)(2,1)} %get-tuple-element.295.v_ref), custom_call_target="tpu_custom_call" | custom-call | flops 12884901888 | bytes 8388608 | tf_op jit(solution)/shard_map/pallas_call | solution.py:229
  192.6 53.2 %shard_map.360 = (bf16[1024,1280]{1,0:T(8,128)(2,1)}, f32[1024,1280]{1,0:T(8,128)}, bf16[1024,640]{1,0:T(8,128)(2,1)}, bf16[1024,640]{1,0:T(8,128)(2,1)}, f32[8,...) custom-call(s32[9]{0:T(128)} %stack.173.info, bf16[1024,1280]{1,0:T(8,128)(2,1)} %bitcast.148, ...), custom_call_target="tpu_custom_call" | custom-call | flops 62075699200 | bytes 39321600 | tf_op jit(solution)/shard_map/pallas_call | solution.py:408
  254.5 39.0 %shard_map.361 = (bf16[2048,320]{1,0:T(8,128)(2,1)}, bf16[3072,320]{1,0:T(8,128)(2,1)}, bf16[3072,320]{1,0:T(8,128)(2,1)}) custom-call(bf16[2048,512]{1,0:T(8,128)(2,1)} %get-tuple-element.293.q_ref, bf16[3072,512]{1,0:T(8,128)(2,1)} %get-tuple-element.294.k_ref, bf16[3072,512]{1,0:T(8,128)(2,1)} %get-tuple-element.295.v_ref, ...), custom_call_target="tpu_custom_call" | custom-call | flops 1000 | bytes 1000 | tf_op jit(solution)/shard_map/pallas_call | solution.py:301
  302.7 33.1 %shard_map.362 = (bf16[512,1280]{1,0:T(8,128)(2,1)}, bf16[512,1280]{1,0:T(8,128)(2,1)}, bf16[1024,1280]{1,0:T(8,128)(2,1)}, bf16[1024,1280]{1,0:T(8,128)(2,1)}, ...) custom-call(s32[11]{0:T(128)} %stack.78.info, ...), custom_call_target="tpu_custom_call" | custom-call | flops 1000 | bytes 1000 | tf_op jit(solution)/shard_map/pallas_call | solution.py:613
  344.7 38.7 %shard_map.363 = (bf16[2048,320]{1,0:T(8,128)(2,1)}, bf16[3072,320]{1,0:T(8,128)(2,1)}, bf16[3072,320]{1,0:T(8,128)(2,1)}) custom-call(bf16[2048,512]{1,0:T(8,128)(2,1)} %get-tuple-element.277.q_ref, bf16[3072,512]{1,0:T(8,128)(2,1)} %get-tuple-element.278.k_ref, bf16[3072,512]{1,0:T(8,128)(2,1)} %get-tuple-element.279.v_ref, ...), custom_call_target="tpu_custom_call" | custom-call | flops 1000 | bytes 1000 | tf_op jit(solution)/shard_map/pallas_call | solution.py:301
  391.8 19.5 %shard_map.364 = (bf16[512,1280]{1,0:T(8,128)(2,1)}, bf16[512,1280]{1,0:T(8,128)(2,1)}, bf16[1024,1280]{1,0:T(8,128)(2,1)}, bf16[1024,1280]{1,0:T(8,128)(2,1)}) custom-call(s32[11]{0:T(128)} %stack.78.info, bf16[3072,1280]{1,0:T(8,128)(2,1)} %get-tuple-element.272.refs_0_, bf16[2048,320]{1,0:T(8,128)(2,1)} %get-tuple-element.396.refs_1_, ...), custom_call_target="tpu_custom_call" | custom-call | flops 1000 | bytes 1000 | tf_op jit(solution)/shard_map/pallas_call | solution.py:613
  424.9 5.7 %shard_map.365 = (bf16[512,1280]{1,0:T(8,128)(2,1)}, f32[8,1280]{1,0:T(8,128)}) custom-call(f32[8,1280]{1,0:T(8,128)} %get-tuple-element.273.gain_ref, bf16[1024,1280]{1,0:T(8,128)(2,1)} %bitcast.149, f32[1024,1280]{1,0:T(8,128)} %get-tuple-element.304.mix_ref, bf16[1024,1280]{1,0:T(8,128)(2,1)} %get-tuple-element.405.refs_0_, bf16[1024,1280]{1,0:T(8,128)(2,1)} %copy-done.4), custom_call_target="tpu_custom_call" | custom-call | flops 1000 | bytes 1000 | tf_op jit(solution)/shard_map/pallas_call | solution.py:663
  435.3 21.0 %shard_map.366 = (bf16[1280,640]{1,0:T(8,128)(2,1)}, bf16[1280,384]{1,0:T(8,128)(2,1)}, f32[8,1024]{1,0:T(8,128)}, bf16[2,1024,1280]{2,1,0:T(8,128)(2,1)}, bf16[2,1024,1280]{2,1,0:T(8,128)(2,1)}) custom-call(s32[11]{0:T(128)} %stack.78.info, bf16[3072,1280]{1,0:T(8,128)(2,1)} %get-tuple-element.272.refs_0_, bf16[2048,320]{1,0:T(8,128)(2,1)} %get-tuple-element.396.refs_1_, ...), custom_call_target="tpu_custom_call" | custom-call | flops 1000 | bytes 1000 | tf_op jit(solution)/shard_map/pallas_call | solution.py:613
  464.2 5.0 collective-permute-start.47
  471.6 6.3 %shard_map.367 = (bf16[512,1280]{1,0:T(8,128)(2,1)}, f32[8,1280]{1,0:T(8,128)}) custom-call(f32[8,1280]{1,0:T(8,128)} %get-tuple-element.273.gain_ref, bf16[1024,1280]{1,0:T(8,128)(2,1)} %bitcast.150, f32[1024,1280]{1,0:T(8,128)} %get-tuple-element.304.mix_ref, bf16[1024,1280]{1,0:T(8,128)(2,1)} %get-tuple-element.405.refs_0_, bf16[1024,1280]{1,0:T(8,128)(2,1)} %copy-done.4, ...), custom_call_target="tpu_custom_call" | custom-call | flops 1000 | bytes 1000 | tf_op jit(solution)/shard_map/pallas_call | solution.py:663
  480.1 9.7 %collective-permute-done.48 = bf16[320,384]{1,0:T(8,128)(2,1)} collective-permute-done((bf16[320,384]{1,0:T(8,128)(2,1)}, bf16[320,384]{1,0:T(8,128)(2,1)}, u32[]{:S(2)}, u32[]{:S(2)}) %collective-permute-start.48) | collective-permute-done | bytes 245792 | tf_op jit(solution)/shard_map/ppermute | solution.py:724
  499.0 4.7 collective-permute-start.52
  506.7 7.4 %shard_map.368 = f32[2,1024,1280]{2,1,0:T(8,128)} custom-call(s32[2]{0:T(128)} %pad_add_fusion.info, bf16[512,1280]{1,0:T(8,128)(2,1)} %get-tuple-element.442.refs_0_, bf16[512,1280]{1,0:T(8,128)(2,1)} %collective-permute-done.44.refs_1_, bf16[512,1280]{1,0:T(8,128)(2,1)} %copy-done.10, bf16[512,1280]{1,0:T(8,128)(2,1)} %collective-permute-done.46.refs_3_), custom_call_target="tpu_custom_call" | custom-call | flops 1000 | bytes 1000 | tf_op jit(solution)/shard_map/pallas_call | solution.py:689
  514.2 7.2 %collective-permute-done.53 = bf16[160,640]{1,0:T(8,128)(2,1)S(1)} collective-permute-done((bf16[160,640]{1,0:T(8,128)(2,1)S(1)}, bf16[160,640]{1,0:T(8,128)(2,1)S(1)}, u32[]{:S(2)}, u32[]{:S(2)}) %collective-permute-start.53) | collective-permute-done | bytes 204832 | tf_op jit(solution)/shard_map/ppermute | solution.py:724
  523.9 5.0 shard_map.369.refs_2_
  547.0 5.1 shard_map.370
  (304 shorter events, 168.5 us)
Async XLA Ops:
  5.1 33.9 %collective-permute-start.2 = (bf16[160,962]{1,0:T(8,128)(2,1)S(1)}, bf16[160,962]{1,0:T(8,128)(2,1)}, u32[]{:S(2)}, u32[]{:S(2)}) collective-permute-start(bf16[160,962]{1,0:T(8,128)(2,1)S(1)} %concatenate.47), channel_id=1, source_target_pairs={{0,8},{8,0},{16,24},{24,16},{1,9},{9,1},{17,25},{25,17},{2,10},{10... | collective-permute-start | bytes 923528 | tf_op jit(solution)/shard_map/ppermute | solution.py:724
  8.2 30.8 %collective-permute-start.3 = (bf16[160,962]{1,0:T(8,128)(2,1)S(1)}, bf16[160,962]{1,0:T(8,128)(2,1)}, u32[]{:S(2)}, u32[]{:S(2)}) collective-permute-start(bf16[160,962]{1,0:T(8,128)(2,1)S(1)} %concatenate.47), channel_id=1, source_target_pairs={{0,16},{8,24},{16,0},{24,8},{1,17},{9,25},{17,1},{25,9},{2,18},{10... | collective-permute-start | bytes 923528 | tf_op jit(solution)/shard_map/ppermute | solution.py:724
  13.4 29.8 %collective-permute-start.1 = (bf16[512,1280]{1,0:T(8,128)(2,1)}, bf16[512,1280]{1,0:T(8,128)(2,1)}, u32[]{:S(2)}, u32[]{:S(2)}) collective-permute-start(bf16[512,1280]{1,0:T(8,128)(2,1)} %dynamic-slice_bitcast_fusion.2), channel_id=1, source_target_pairs={{0,4},{4,0},{1,5},{5,1},{2,6},{6,2},{3,7},{7,3},{8,12},{12,8},{9,1... | collective-permute-start | bytes 3932168 | tf_op jit(solution)/shard_map/ppermute | solution.py:724
  43.2 32.6 %collective-permute-start.6 = (bf16[512,1280]{1,0:T(8,128)(2,1)}, bf16[512,1280]{1,0:T(8,128)(2,1)}, u32[]{:S(2)}, u32[]{:S(2)}) collective-permute-start(bf16[512,1280]{1,0:T(8,128)(2,1)} %collective-permute-done.1.refs_2_), channel_id=1, source_target_pairs={{0,1},{1,0},{2,3},{3,2},{4,5},{5,4},{6,7},{7,6},{8,9},{9,8},{10,11... | collective-permute-start | bytes 3932168 | tf_op jit(solution)/shard_map/ppermute | solution.py:724
  44.5 31.3 %collective-permute-start.5 = (bf16[4,160,962]{2,1,0:T(8,128)(2,1)S(1)}, bf16[4,160,962]{2,1,0:T(8,128)(2,1)S(1)}, u32[]{:S(2)}, u32[]{:S(2)}) collective-permute-start(bf16[4,160,962]{2,1,0:T(8,128)(2,1)S(1)} %pad_maximum_fusion.3.refs_4_), channel_id=1, source_target_pairs={{0,4},{4,0},{1,5},{5,1},{2,6},{6,2},{3,7},{7,3},{8,12},{12,8},{9,1... | collective-permute-start | bytes 3694088 | tf_op jit(solution)/shard_map/ppermute | solution.py:724
  63.7 53.3 %collective-permute-start.20 = (f32[2,320]{1,0:T(2,128)S(1)}, f32[2,320]{1,0:T(2,128)S(1)}, u32[]{:S(2)}, u32[]{:S(2)}) collective-permute-start(f32[2,320]{1,0:T(2,128)S(1)} %fusion.10), channel_id=1, source_target_pairs={{0,1},{1,0},{2,3},{3,2},{4,5},{5,4},{6,7},{7,6},{8,9},{9,8},{10,11... | collective-permute-start | bytes 7688 | tf_op jit(solution)/shard_map/ppermute | solution.py:724
  75.8 35.5 %collective-permute-start.11 = (bf16[160,964]{1,0:T(8,128)(2,1)S(1)}, bf16[160,964]{1,0:T(8,128)(2,1)S(1)}, u32[]{:S(2)}, u32[]{:S(2)}) collective-permute-start(bf16[160,964]{1,0:T(8,128)(2,1)S(1)} %concatenate.50), channel_id=1, source_target_pairs={{0,8},{8,0},{16,24},{24,16},{1,9},{9,1},{17,25},{25,17},{2,10},{10... | collective-permute-start | bytes 925448 | tf_op jit(solution)/shard_map/ppermute | solution.py:724
  80.9 30.4 %collective-permute-start.12 = (bf16[160,964]{1,0:T(8,128)(2,1)S(1)}, bf16[160,964]{1,0:T(8,128)(2,1)S(1)}, u32[]{:S(2)}, u32[]{:S(2)}) collective-permute-start(bf16[160,964]{1,0:T(8,128)(2,1)S(1)} %concatenate.50), channel_id=1, source_target_pairs={{0,16},{8,24},{16,0},{24,8},{1,17},{9,25},{17,1},{25,9},{2,18},{10... | collective-permute-start | bytes 925448 | tf_op jit(solution)/shard_map/ppermute | solution.py:724
  82.0 29.4 %collective-permute-start.13 = (bf16[160,964]{1,0:T(8,128)(2,1)S(1)}, bf16[160,964]{1,0:T(8,128)(2,1)S(1)}, u32[]{:S(2)}, u32[]{:S(2)}) collective-permute-start(bf16[160,964]{1,0:T(8,128)(2,1)S(1)} %concatenate.50), channel_id=1, source_target_pairs={{0,24},{8,16},{16,8},{24,0},{1,25},{9,17},{17,9},{25,1},{2,26},{10... | collective-permute-start | bytes 925448 | tf_op jit(solution)/shard_map/ppermute | solution.py:724
  84.7 29.6 %collective-permute-start.10 = (bf16[4,160,962]{2,1,0:T(8,128)(2,1)S(1)}, bf16[4,160,962]{2,1,0:T(8,128)(2,1)S(1)}, u32[]{:S(2)}, u32[]{:S(2)}) collective-permute-start(bf16[4,160,962]{2,1,0:T(8,128)(2,1)S(1)} %pad_maximum_fusion.4.refs_1_.refs_4_), channel_id=1, source_target_pairs={{0,4},{4,0},{1,5},{5,1},{2,6},{6,2},{3,7},{7,3},{8,12},{12,8},{9,1... | collective-permute-start | bytes 3694088 | tf_op jit(solution)/shard_map/ppermute | solution.py:724
  144.6 41.9 %collective-permute-start.21 = (bf16[4,160,964]{2,1,0:T(8,128)(2,1)}, bf16[4,160,964]{2,1,0:T(8,128)(2,1)}, u32[]{:S(2)}, u32[]{:S(2)}) collective-permute-start(bf16[4,160,964]{2,1,0:T(8,128)(2,1)} %collective-permute-done.14.refs_6_), channel_id=1, source_target_pairs={{0,4},{4,0},{1,5},{5,1},{2,6},{6,2},{3,7},{7,3},{8,12},{12,8},{9,1... | collective-permute-start | bytes 3701768 | tf_op jit(solution)/shard_map/ppermute | solution.py:724
  252.4 41.0 %collective-permute-start.25 = (bf16[1280,1920]{1,0:T(8,128)(2,1)}, bf16[1280,1920]{1,0:T(8,128)(2,1)}, u32[]{:S(2)}, u32[]{:S(2)}) collective-permute-start(bf16[1280,1920]{1,0:T(8,128)(2,1)} %get-tuple-element.316), channel_id=1, source_target_pairs={{0,1},{1,0},{2,3},{3,2},{4,5},{5,4},{6,7},{7,6},{8,9},{9,8},{10,11... | collective-permute-start | bytes 14745608 | tf_op jit(solution)/shard_map/ppermute | solution.py:724
  252.7 83.0 %collective-permute-start.27 = (bf16[1024,1280]{1,0:T(8,128)(2,1)}, bf16[1024,1280]{1,0:T(8,128)(2,1)}, u32[]{:S(2)}, u32[]{:S(2)}) collective-permute-start(bf16[1024,1280]{1,0:T(8,128)(2,1)} %get-tuple-element.399.refs_8_), channel_id=1, source_target_pairs={{0,1},{1,0},{2,3},{3,2},{4,5},{5,4},{6,7},{7,6},{8,9},{9,8},{10,11... | collective-permute-start | bytes 7864328 | tf_op jit(solution)/shard_map/ppermute | solution.py:724
  253.0 82.8 %collective-permute-start.28 = (bf16[1024,1280]{1,0:T(8,128)(2,1)}, bf16[1024,1280]{1,0:T(8,128)(2,1)}, u32[]{:S(2)}, u32[]{:S(2)}) collective-permute-start(bf16[1024,1280]{1,0:T(8,128)(2,1)} %get-tuple-element.399.refs_8_), channel_id=1, source_target_pairs={{0,2},{1,3},{2,0},{3,1},{4,6},{5,7},{6,4},{7,5},{8,10},{9,11},{10,... | collective-permute-start | bytes 7864328 | tf_op jit(solution)/shard_map/ppermute | solution.py:724
  301.0 34.8 %collective-permute-start.26 = (bf16[4,160,1024]{2,1,0:T(8,128)(2,1)}, bf16[4,160,1024]{2,1,0:T(8,128)(2,1)}, u32[]{:S(2)}, u32[]{:S(2)}) collective-permute-start(bf16[4,160,1024]{2,1,0:T(8,128)(2,1)} %get-tuple-element.327), channel_id=1, source_target_pairs={{0,4},{4,0},{1,5},{5,1},{2,6},{6,2},{3,7},{7,3},{8,12},{12,8},{9,1... | collective-permute-start | bytes 3932168 | tf_op jit(solution)/shard_map/ppermute | solution.py:724
  338.8 44.7 %collective-permute-start.29 = (bf16[1280,768]{1,0:T(8,128)(2,1)}, bf16[1280,768]{1,0:T(8,128)(2,1)S(1)}, u32[]{:S(2)}, u32[]{:S(2)}) collective-permute-start(bf16[1280,768]{1,0:T(8,128)(2,1)} %get-tuple-element.339), channel_id=1, source_target_pairs={{0,2},{1,3},{2,0},{3,1},{4,6},{5,7},{6,4},{7,5},{8,10},{9,11},{10,... | collective-permute-start | bytes 5898248 | tf_op jit(solution)/shard_map/ppermute | solution.py:724
  339.4 44.1 %collective-permute-start.30 = (bf16[4,160,896]{2,1,0:T(8,128)(2,1)S(1)}, bf16[4,160,896]{2,1,0:T(8,128)(2,1)S(1)}, u32[]{:S(2)}, u32[]{:S(2)}) collective-permute-start(bf16[4,160,896]{2,1,0:T(8,128)(2,1)S(1)} %copy-done.14), channel_id=1, source_target_pairs={{0,4},{4,0},{1,5},{5,1},{2,6},{6,2},{3,7},{7,3},{8,12},{12,8},{9,1... | collective-permute-start | bytes 3440648 | tf_op jit(solution)/shard_map/ppermute | solution.py:724
  340.3 43.1 %collective-permute-start.31 = (bf16[160,1024]{1,0:T(8,128)(2,1)}, bf16[160,1024]{1,0:T(8,128)(2,1)}, u32[]{:S(2)}, u32[]{:S(2)}) collective-permute-start(bf16[160,1024]{1,0:T(8,128)(2,1)} %get-tuple-element.344), channel_id=1, source_target_pairs={{0,8},{8,0},{16,24},{24,16},{1,9},{9,1},{17,25},{25,17},{2,10},{10... | collective-permute-start | bytes 983048 | tf_op jit(solution)/shard_map/ppermute | solution.py:724
  340.8 42.6 %collective-permute-start.32 = (bf16[160,1024]{1,0:T(8,128)(2,1)}, bf16[160,1024]{1,0:T(8,128)(2,1)}, u32[]{:S(2)}, u32[]{:S(2)}) collective-permute-start(bf16[160,1024]{1,0:T(8,128)(2,1)} %get-tuple-element.345), channel_id=1, source_target_pairs={{0,16},{8,24},{16,0},{24,8},{1,17},{9,25},{17,1},{25,9},{2,18},{10... | collective-permute-start | bytes 983048 | tf_op jit(solution)/shard_map/ppermute | solution.py:724
  343.3 40.1 %collective-permute-start.33 = (bf16[160,1024]{1,0:T(8,128)(2,1)}, bf16[160,1024]{1,0:T(8,128)(2,1)}, u32[]{:S(2)}, u32[]{:S(2)}) collective-permute-start(bf16[160,1024]{1,0:T(8,128)(2,1)} %get-tuple-element.346), channel_id=1, source_target_pairs={{0,24},{8,16},{16,8},{24,0},{1,25},{9,17},{17,9},{25,1},{2,26},{10... | collective-permute-start | bytes 983048 | tf_op jit(solution)/shard_map/ppermute | solution.py:724
  423.8 35.0 %collective-permute-start.42 = (bf16[512,1280]{1,0:T(8,128)(2,1)}, bf16[512,1280]{1,0:T(8,128)(2,1)}, u32[]{:S(2)}, u32[]{:S(2)}) collective-permute-start(bf16[512,1280]{1,0:T(8,128)(2,1)} %add_convert_fusion), channel_id=1, source_target_pairs={{0,4},{4,0},{1,5},{5,1},{2,6},{6,2},{3,7},{7,3},{8,12},{12,8},{9,1... | collective-permute-start | bytes 3932168 | tf_op jit(solution)/shard_map/ppermute | solution.py:724
  431.6 30.6 %collective-permute-start.43 = (bf16[512,1280]{1,0:T(8,128)(2,1)}, bf16[512,1280]{1,0:T(8,128)(2,1)S(1)}, u32[]{:S(2)}, u32[]{:S(2)}) collective-permute-start(bf16[512,1280]{1,0:T(8,128)(2,1)} %get-tuple-element.442.refs_0_), channel_id=1, source_target_pairs={{0,2},{1,3},{2,0},{3,1},{4,6},{5,7},{6,4},{7,5},{8,10},{9,11},{10,... | collective-permute-start | bytes 3932168 | tf_op jit(solution)/shard_map/ppermute | solution.py:724
  432.5 30.8 %collective-permute-start.44 = (bf16[512,1280]{1,0:T(8,128)(2,1)}, bf16[512,1280]{1,0:T(8,128)(2,1)}, u32[]{:S(2)}, u32[]{:S(2)}) collective-permute-start(bf16[512,1280]{1,0:T(8,128)(2,1)} %get-tuple-element.442.refs_0_), channel_id=1, source_target_pairs={{0,1},{1,0},{2,3},{3,2},{4,5},{5,4},{6,7},{7,6},{8,9},{9,8},{10,11... | collective-permute-start | bytes 3932168 | tf_op jit(solution)/shard_map/ppermute | solution.py:724
  498.0 42.9 %collective-permute-start.59 = (bf16[512,1280]{1,0:T(8,128)(2,1)S(1)}, bf16[512,1280]{1,0:T(8,128)(2,1)}, u32[]{:S(2)}, u32[]{:S(2)}) collective-permute-start(bf16[512,1280]{1,0:T(8,128)(2,1)S(1)} %copy-done.11), channel_id=1, source_target_pairs={{0,2},{1,3},{2,0},{3,1},{4,6},{5,7},{6,4},{7,5},{8,10},{9,11},{10,... | collective-permute-start | bytes 3932168 | tf_op jit(solution)/shard_map/ppermute | solution.py:724
  (76 other events, 1009.2 us)
